TPU v7x, 32 devices: a whole 2x2x4 slice. The times are simulated.
32 devices in a mesh: seq: 8 (over y, x, core), fsdp: 4 (over z).
Axes of the slice: x: 2, y: 2, z: 4, core: 2. Of those that a mesh axis runs over, the one named last changes fastest.
Arguments:
- tokens: bfloat16 [2, 4, 1024, 2048], P(None, 'fsdp', 'seq'), may hold values from -6 to 6
- ln_gain: bfloat16 [2048], P(('seq', 'fsdp')), may hold values from 0.5 to 1.5
- ln_bias: bfloat16 [2048], P(('seq', 'fsdp')), may hold values from -1.75 to 1.75
- w_qkv: bfloat16 [2048, 6144], P(('seq', 'fsdp')), may hold values from -0.125 to 0.125
- b_qkv: bfloat16 [6144], P(('seq', 'fsdp')), may hold values from -1.75 to 1.75
- w_out: bfloat16 [2048, 2048], P(('seq', 'fsdp')), may hold values from -2 to 2
- b_out: bfloat16 [2048], P(('seq', 'fsdp')), may hold values from -1.75 to 1.75
- w_fc1: bfloat16 [2048, 8192], P(('seq', 'fsdp')), may hold values from -0.125 to 0.125
- b_fc1: bfloat16 [8192], P(('seq', 'fsdp')), may hold values from -3 to 3
- w_fc2: bfloat16 [8192, 2048], P(('seq', 'fsdp')), may hold values from -0.0625 to 0.0625
- b_fc2: bfloat16 [2048], P(('seq', 'fsdp')), may hold values from -1.75 to 1.75
- piece_starts: int32 [2, 4, 2], P(None, 'fsdp'), may hold values from 0 to 768, as said below
- cotangent: bfloat16 [2, 4, 1024, 2048], P(None, 'fsdp', 'seq'), may hold values from -6 to 6
Outputs:
- activations: bfloat16 [2, 4, 1024, 2048], P(None, 'fsdp', 'seq')
- input_grad: float32 [2, 4, 1024, 2048], P(None, 'fsdp', 'seq')
- grad_ln_gain: float32 [2048], P(('seq', 'fsdp'))
- grad_ln_bias: float32 [2048], P(('seq', 'fsdp'))
- grad_w_qkv: float32 [2048, 6144], P(('seq', 'fsdp'))
- grad_b_qk: float32 [4096], P(('seq', 'fsdp'))
- grad_b_v: float32 [2048], P(('seq', 'fsdp'))
- grad_w_out: float32 [2048, 2048], P(('seq', 'fsdp'))
- grad_b_out: float32 [2048], P(('seq', 'fsdp'))
- grad_w_fc1: float32 [2048, 8192], P(('seq', 'fsdp'))
- grad_b_fc1: float32 [8192], P(('seq', 'fsdp'))
- grad_w_fc2: float32 [8192, 2048], P(('seq', 'fsdp'))
- grad_b_fc2: float32 [2048], P(('seq', 'fsdp'))
Inputs may be any that keep to these rules, and one draw needn't show every extreme that they name: `piece_starts`: in each sequence the 2 pieces are disjoint and in increasing order; piece p starts in [p * 512, (p + 1) * 512 - 256].
All inputs are finite; a program needn't handle non-finite values.
Results may differ from a plain program's by a relative error of at most 0.015.
Values may be sent and summed in bfloat16 or wider, within the bound.
A program may use at most 512 MiB of HBM per device.

v0:
```python
import math

import jax
import jax.numpy as jnp
from jax import lax
from jax.sharding import PartitionSpec as P

HEADS = 32
HEAD_DIM = 64
ROT = 32
IMG = 256
PIECES = 2


EPSILON = 1e-05


def layer_norm(values, ln_scale, ln_shift):
    center = values - jnp.mean(values, axis=-1, keepdims=True)
    spread = jnp.mean(center * center, axis=-1, keepdims=True)
    return center * lax.rsqrt(spread + EPSILON) * ln_scale + ln_shift


def rotate(values, positions):
    half_dims = ROT // 2
    frequency = 10000.0 ** (-2.0 * jnp.arange(half_dims, dtype=jnp.float32) / ROT)
    angles = positions.astype(jnp.float32)[:, None] * frequency[None, :]
    cosine = jnp.cos(angles)[:, None, :]
    sine_part = jnp.sin(angles)[:, None, :]
    front_part = values[..., :half_dims]
    back_part = values[..., half_dims:ROT]
    return jnp.concatenate(
        [
            front_part * cosine - back_part * sine_part,
            back_part * cosine + front_part * sine_part,
            values[..., ROT:],
        ],
        axis=-1,
    )


def piece_index(positions, starts):
    inside = (positions[:, None] >= starts[None, :]) & (positions[:, None] < starts[None, :] + IMG)
    labels = jnp.arange(1, PIECES + 1, dtype=jnp.int32)
    return jnp.sum(jnp.where(inside, labels[None, :], 0), axis=1) - 1


def visible(query_pos, query_piece, key_pos, key_piece):
    causal = key_pos[None, :] <= query_pos[:, None]
    same_piece = (query_piece[:, None] == key_piece[None, :]) & (query_piece[:, None] >= 0)
    return causal | same_piece


def gelu_tanh(values):
    return jax.nn.gelu(values, approximate=True)


def slab_term(left, right, tail):
    part = jnp.einsum("td,te->de", left, right, preferred_element_type=jnp.float32)
    if tail is None:
        return part
    return jnp.concatenate([part, tail], axis=1)


def scatter_grads(
    normed,
    projected_grad,
    mixed_heads,
    hidden,
    upstream,
    pre_grad,
    gain_grad,
    shift_grad,
    resident_rows,
):
    width = normed.shape[1]
    ratio = pre_grad.shape[1] // width
    pairs = [(normed, projected_grad[:, slab * width : (slab + 1) * width]) for slab in range(3)]
    pairs = pairs + [(mixed_heads, upstream)]
    pairs = pairs + [
        (normed, pre_grad[:, slab * width : (slab + 1) * width]) for slab in range(ratio)
    ]
    pairs = pairs + [(hidden[:, slab::ratio], upstream) for slab in range(ratio)]
    bias_qk = jnp.sum(projected_grad[:, : 2 * width].astype(jnp.float32), axis=0).reshape(width, 2)
    bias_v = jnp.sum(projected_grad[:, 2 * width :].astype(jnp.float32), axis=0).reshape(width, 1)
    bias_one = jnp.sum(pre_grad.astype(jnp.float32), axis=0).reshape(width, ratio)
    bias_two = jnp.sum(upstream.astype(jnp.float32), axis=0).reshape(width, 1)
    extra = jnp.concatenate(
        [
            bias_qk,
            bias_v,
            bias_one,
            bias_two,
            gain_grad.reshape(width, 1),
            shift_grad.reshape(width, 1),
        ],
        axis=1,
    )
    results = []
    for slab_number in range(len(pairs)):
        left, right = pairs[slab_number]
        tail = extra if slab_number == len(pairs) - 1 else None

        def rows(start, count, left=left, right=right, tail=tail):
            return slab_term(left, right, tail)

        results.append(
            lax.psum_scatter(
                rows(jnp.int32(0), lax.axis_size(("seq", "fsdp")) * resident_rows),
                ("seq", "fsdp"),
                scatter_dimension=0,
                tiled=True,
            )
        )
    last = results[-1]
    tiny_epsilon_value = last[:, width:]
    results[-1] = last[:, :width]
    qkv_part = jnp.concatenate(results[0:3], axis=1)
    out_part = results[3]
    fc1_part = jnp.concatenate(results[4 : 4 + ratio], axis=1)
    fc2_part = jnp.stack(results[4 + ratio : 4 + 2 * ratio], axis=1).reshape(
        resident_rows * ratio, width
    )
    query_key_bias_slice = tiny_epsilon_value[:, :2].reshape(resident_rows * 2)
    bv_part = tiny_epsilon_value[:, 2]
    bfc1_part = tiny_epsilon_value[:, 3 : 3 + ratio].reshape(resident_rows * ratio)
    bfc2_part = tiny_epsilon_value[:, 3 + ratio]
    gain_part = tiny_epsilon_value[:, 4 + ratio]
    shift_part = tiny_epsilon_value[:, 5 + ratio]
    return [
        gain_part,
        shift_part,
        qkv_part,
        query_key_bias_slice,
        bv_part,
        out_part,
        bfc2_part,
        fc1_part,
        bfc1_part,
        fc2_part,
        bfc2_part,
    ]


def per_device(
    tokens,
    ln_gain,
    ln_bias,
    w_qkv,
    b_qkv,
    w_out,
    b_out,
    w_fc1,
    b_fc1,
    w_fc2,
    b_fc2,
    piece_starts,
    cotangent,
):
    local_rows = tokens.shape[2]
    width = tokens.shape[3]
    seq_length = local_rows * lax.axis_size("seq")
    resident_rows = width // (lax.axis_size("seq") * lax.axis_size("fsdp"))
    positions = lax.axis_index("seq") * local_rows + jnp.arange(local_rows, dtype=jnp.int32)
    all_positions = jnp.arange(seq_length, dtype=jnp.int32)
    score_scale = 1.0 / math.sqrt(HEAD_DIM)
    block_rows = math.gcd(seq_length, 512)
    block_count = seq_length // block_rows
    gathered = (
        lax.all_gather(ln_gain, ("seq", "fsdp"), axis=0, tiled=True),
        lax.all_gather(ln_bias, ("seq", "fsdp"), axis=0, tiled=True),
        lax.all_gather(w_qkv, ("seq", "fsdp"), axis=0, tiled=True),
        lax.all_gather(b_qkv, ("seq", "fsdp"), axis=0, tiled=True),
        lax.all_gather(w_out, ("seq", "fsdp"), axis=0, tiled=True),
        lax.all_gather(b_out, ("seq", "fsdp"), axis=0, tiled=True),
        lax.all_gather(w_fc1, ("seq", "fsdp"), axis=0, tiled=True),
        lax.all_gather(b_fc1, ("seq", "fsdp"), axis=0, tiled=True),
        lax.all_gather(w_fc2, ("seq", "fsdp"), axis=0, tiled=True),
        lax.all_gather(b_fc2, ("seq", "fsdp"), axis=0, tiled=True),
    )
    (
        full_gain,
        full_shift,
        full_qkv,
        full_bqkv,
        full_out,
        full_bout,
        full_fc1,
        full_bfc1,
        full_fc2,
        full_bfc2,
    ) = gathered
    gain_f32 = full_gain.astype(jnp.float32)
    shift_f32 = full_shift.astype(jnp.float32)
    totals = None
    kept_normed = []
    kept_pre = []
    kept_hidden = []
    kept_upstream = []
    kept_projected = []
    kept_mixed = []
    gain_sum = jnp.zeros((width,), jnp.float32)
    norm_shift_total = jnp.zeros((width,), jnp.float32)
    layer_outputs = []
    layer_input_gradients = []
    for micro in range(tokens.shape[0]):
        inputs = tokens[micro, 0].astype(jnp.float32)
        starts = piece_starts[micro, 0]
        pieces = piece_index(positions, starts)
        all_pieces = piece_index(all_positions, starts)
        normed = layer_norm(inputs, gain_f32, shift_f32).astype(jnp.bfloat16)
        projected = jnp.dot(
            normed, full_qkv, preferred_element_type=jnp.float32
        ) + full_bqkv.astype(jnp.float32)
        query_rows = rotate(
            projected[:, :width].reshape(local_rows, HEADS, HEAD_DIM), positions
        ).astype(jnp.bfloat16)
        key_rows = (
            rotate(projected[:, width : 2 * width].reshape(local_rows, HEADS, HEAD_DIM), positions)
            .astype(jnp.bfloat16)
            .reshape(local_rows, width)
        )
        value_rows = projected[:, 2 * width :].astype(jnp.bfloat16)
        row_max = jnp.full((HEADS, local_rows), -1e30, jnp.float32)
        weighted = jnp.zeros((local_rows, HEADS, HEAD_DIM), jnp.float32)
        key_piece_rows = lax.all_gather(key_rows, "seq", axis=0, tiled=True)
        value_piece_rows = lax.all_gather(value_rows, "seq", axis=0, tiled=True)
        piece_rows = key_piece_rows.shape[0]
        key_pos = jnp.arange(piece_rows, dtype=jnp.int32)
        key_labels = piece_index(key_pos, starts)
        scores = (
            jnp.einsum(
                "qhd,khd->hqk",
                query_rows,
                key_piece_rows.reshape(piece_rows, HEADS, HEAD_DIM),
                preferred_element_type=jnp.float32,
            )
            * score_scale
        )
        allowed = visible(positions, pieces, key_pos, key_labels)[None]
        scores = jnp.where(allowed, scores, -1e30)
        new_max = jnp.maximum(row_max, jnp.max(scores, axis=-1))
        factor = jnp.exp(row_max - new_max)
        probs = jnp.where(allowed, jnp.exp(scores - new_max[:, :, None]), 0.0)
        new_sum = jnp.sum(probs, axis=-1)
        new_weighted = weighted * factor.T[:, :, None] + jnp.einsum(
            "hqk,khd->qhd",
            probs.astype(jnp.bfloat16),
            value_piece_rows.reshape(piece_rows, HEADS, HEAD_DIM),
            preferred_element_type=jnp.float32,
        )
        row_max = new_max
        weighted = new_weighted
        attended = weighted / new_sum.T[:, :, None]
        log_sum = row_max + jnp.log(new_sum)
        mixed_heads = attended.reshape(local_rows, width).astype(jnp.bfloat16)
        attn_branch = jnp.dot(
            mixed_heads, full_out, preferred_element_type=jnp.float32
        ) + full_bout.astype(jnp.float32)
        hidden_pre = jnp.dot(
            normed, full_fc1, preferred_element_type=jnp.float32
        ) + full_bfc1.astype(jnp.float32)
        hidden = gelu_tanh(hidden_pre).astype(jnp.bfloat16)
        mlp_branch = jnp.dot(
            hidden, full_fc2, preferred_element_type=jnp.float32
        ) + full_bfc2.astype(jnp.float32)
        layer_outputs.append((inputs + attn_branch + mlp_branch).astype(jnp.bfloat16))
        upstream = cotangent[micro, 0]
        upstream_f32 = upstream.astype(jnp.float32)
        hidden_grad = jnp.einsum(
            "td,fd->tf", upstream, full_fc2, preferred_element_type=jnp.float32
        )
        gelu_pair = jax.vjp(gelu_tanh, hidden_pre)
        pre_grad = gelu_pair[1](hidden_grad)[0].astype(jnp.bfloat16)
        normed_grad = jnp.einsum(
            "tf,df->td", pre_grad, full_fc1, preferred_element_type=jnp.float32
        )
        mixed_grad = (
            jnp.einsum("te,de->td", upstream, full_out, preferred_element_type=jnp.float32)
            .astype(jnp.bfloat16)
            .reshape(local_rows, HEADS, HEAD_DIM)
        )
        delta = jnp.sum(mixed_grad.astype(jnp.float32) * attended, axis=-1).T
        all_keys, all_values = (
            lax.all_gather(key_rows, "seq", axis=0, tiled=True),
            lax.all_gather(value_rows, "seq", axis=0, tiled=True),
        )

        def backward_block(query_grad, block_index):
            start = block_index * block_rows
            block_keys = lax.dynamic_slice_in_dim(all_keys, start, block_rows, 0).reshape(
                block_rows, HEADS, HEAD_DIM
            )
            block_values = lax.dynamic_slice_in_dim(all_values, start, block_rows, 0).reshape(
                block_rows, HEADS, HEAD_DIM
            )
            key_pos = lax.dynamic_slice_in_dim(all_positions, start, block_rows, 0)
            key_labels = lax.dynamic_slice_in_dim(all_pieces, start, block_rows, 0)
            scores = (
                jnp.einsum(
                    "qhd,khd->hqk", query_rows, block_keys, preferred_element_type=jnp.float32
                )
                * score_scale
            )
            allowed = visible(positions, pieces, key_pos, key_labels)[None]
            scores = jnp.where(allowed, scores, -1e30)
            probs = jnp.where(allowed, jnp.exp(scores - log_sum[:, :, None]), 0.0)
            value_grad = jnp.einsum(
                "hqk,qhd->khd",
                probs.astype(jnp.bfloat16),
                mixed_grad,
                preferred_element_type=jnp.float32,
            )
            prob_grad = jnp.einsum(
                "qhd,khd->hqk", mixed_grad, block_values, preferred_element_type=jnp.float32
            )
            score_grad = (probs * (prob_grad - delta[:, :, None])).astype(jnp.bfloat16)
            new_query_grad = (
                query_grad
                + jnp.einsum(
                    "hqk,khd->qhd", score_grad, block_keys, preferred_element_type=jnp.float32
                )
                * score_scale
            )
            key_gradient_rows = (
                jnp.einsum(
                    "hqk,qhd->khd", score_grad, query_rows, preferred_element_type=jnp.float32
                )
                * score_scale
            )
            return (
                new_query_grad,
                (
                    key_gradient_rows.reshape(block_rows, width),
                    value_grad.reshape(block_rows, width),
                ),
            )

        query_grad, block_terms = lax.scan(
            backward_block,
            jnp.zeros((local_rows, HEADS, HEAD_DIM), jnp.float32),
            jnp.arange(block_count, dtype=jnp.int32),
        )
        key_terms = block_terms[0].reshape(seq_length, width)
        value_terms = block_terms[1].reshape(seq_length, width)
        key_gradient_rows, value_grad = (
            lax.psum_scatter(
                key_terms.astype(jnp.bfloat16), "seq", scatter_dimension=0, tiled=True
            ).astype(jnp.float32),
            lax.psum_scatter(
                value_terms.astype(jnp.bfloat16), "seq", scatter_dimension=0, tiled=True
            ).astype(jnp.float32),
        )
        query_back = rotate(query_grad, -positions).reshape(local_rows, width)
        key_back = rotate(
            key_gradient_rows.reshape(local_rows, HEADS, HEAD_DIM), -positions
        ).reshape(local_rows, width)
        projected_grad = jnp.concatenate([query_back, key_back, value_grad], axis=1).astype(
            jnp.bfloat16
        )
        normed_grad = normed_grad + jnp.einsum(
            "te,de->td", projected_grad, full_qkv, preferred_element_type=jnp.float32
        )
        norm_pair = jax.vjp(layer_norm, inputs, gain_f32, shift_f32)
        normalized_input_gradient, grad_gain, grad_shift = norm_pair[1](normed_grad)
        layer_input_gradients.append(upstream_f32 + normalized_input_gradient)
        kept_normed.append(normed)
        kept_pre.append(pre_grad)
        kept_hidden.append(hidden)
        kept_upstream.append(upstream)
        kept_projected.append(projected_grad)
        kept_mixed.append(mixed_heads)
        gain_sum = gain_sum + grad_gain
        norm_shift_total = norm_shift_total + grad_shift
    normed_all = jnp.concatenate(kept_normed, axis=0)
    pre_all = jnp.concatenate(kept_pre, axis=0)
    hidden_gathered_rows = jnp.concatenate(kept_hidden, axis=0)
    upstream_all = jnp.concatenate(kept_upstream, axis=0)
    projected_all = jnp.concatenate(kept_projected, axis=0)
    mixed_all = jnp.concatenate(kept_mixed, axis=0)
    totals = scatter_grads(
        normed_all,
        projected_all,
        mixed_all,
        hidden_gathered_rows,
        upstream_all,
        pre_all,
        gain_sum,
        norm_shift_total,
        resident_rows,
    )
    activations = jnp.stack(layer_outputs)[:, None]
    input_grad = jnp.stack(layer_input_gradients)[:, None]
    return (
        activations,
        input_grad,
        totals[0],
        totals[1],
        totals[2],
        totals[3],
        totals[4],
        totals[5],
        totals[6],
        totals[7],
        totals[8],
        totals[9],
        totals[10],
    )


def solution(mesh):
    placed = (
        P(None, "fsdp", "seq", None),
        P(("seq", "fsdp")),
        P(("seq", "fsdp")),
        P(("seq", "fsdp"), None),
        P(("seq", "fsdp")),
        P(("seq", "fsdp"), None),
        P(("seq", "fsdp")),
        P(("seq", "fsdp"), None),
        P(("seq", "fsdp")),
        P(("seq", "fsdp"), None),
        P(("seq", "fsdp")),
        P(None, "fsdp", None),
        P(None, "fsdp", "seq", None),
    )
    return jax.shard_map(
        per_device,
        mesh=mesh,
        in_specs=placed,
        out_specs=(
            P(None, "fsdp", "seq", None),
            P(None, "fsdp", "seq", None),
            P(("seq", "fsdp")),
            P(("seq", "fsdp")),
            P(("seq", "fsdp"), None),
            P(("seq", "fsdp")),
            P(("seq", "fsdp")),
            P(("seq", "fsdp"), None),
            P(("seq", "fsdp")),
            P(("seq", "fsdp"), None),
            P(("seq", "fsdp")),
            P(("seq", "fsdp"), None),
            P(("seq", "fsdp")),
        ),
        check_vma=False,
    )
```

profile of v0, /device:TPU:15, one launch (start us, length us, event | category | flops | bytes accessed | tf_op | source)
XLA Modules:
  0.0 5529.3 jit_solution(3307831269976103634)
XLA Ops:
  12.9 41.5 all-reduce.5
  60.6 105.4 %all-gather.10.cloned.1.call-done = bf16[2048,6144]{1,0:T(8,128)(2,1)} async-done(((bf16[64,6144]{1,0:T(8,128)(2,1)}), bf16[2048,6144]{1,0:T(8,128)(2,1)}) %all-gather.10.cloned.1.call-update) | async-done | bytes 25165840 | tf_op jit(solution)/shard_map/all_gather | solution.py:172
  166.0 10.0 convolution_add_fusion.2
  180.3 10.0 convolution_add_fusion.3
  203.3 43.1 all-gather.16.cloned.1.call-done
  253.7 6.7 convolution_convert_fusion
  265.6 19.2 all-gather.12.cloned.1.call-done
  296.2 28.4 all-gather.22.cloned.1.call-done
  336.0 27.7 all-gather.14.cloned.1.call-done
  370.1 13.3 multiply_reduce_fusion.1
  388.5 80.0 %while.30 = (s32[]{:T(128)}, f32[128,32,64]{0,2,1:T(8,128)}, bf16[2,512,2048]{2,1,0:T(8,128)(2,1)}, bf16[2,512,2048]{2,1,0:T(8,128)(2,1)}, s32[2]{0:T(128)S(1)},...) while((s32[]{:T(128)}, f32[128,32,64]{0,2,1:T(8,128)}, ...), condition=%wide.region_14.15_spmd.clone, body=%wide.region_13.14_spmd.clone.sunk | while | flops 1370489088 | bytes 147061904 | solution.py:339
  408.3 7.2 fusion.278
  448.0 7.2 fusion.278
  475.0 14.4 multiply_reduce_fusion
  494.5 80.1 %while.31 = (s32[]{:T(128)}, f32[128,32,64]{0,2,1:T(8,128)}, bf16[2,512,2048]{2,1,0:T(8,128)(2,1)}, bf16[2,512,2048]{2,1,0:T(8,128)(2,1)}, s32[2]{0:T(128)S(1)},...) while((s32[]{:T(128)}, f32[128,32,64]{0,2,1:T(8,128)}, ...), condition=%wide.region_21.22_spmd.clone, body=%wide.region_20.21_spmd.clone.sunk | while | flops 1370489088 | bytes 144964720 | solution.py:339
  514.6 7.3 fusion.292
  554.2 7.2 fusion.292
  580.0 46.0 reduce-scatter.31.cloned.1.call-done
  629.1 51.6 reduce-scatter.51.cloned.1.call-done
  682.7 52.9 reduce-scatter.49.cloned.1.call-done
  740.7 12.8 maximum_maximum_fusion
  755.1 8.2 fusion.132
  763.4 9.4 fusion.130
  773.1 10.1 fusion.144
  783.8 64.5 %all-gather = bf16[32,1,256]{2,1,0:T(2,128)(2,1)S(1)} all-gather(bf16[1,1,256]{2,1,0:T(2,128)(2,1)S(1)} %reshape.702), channel_id=1, replica_groups=mesh['seq'=8,'fsdp'=4] {'seq','fsdp'}, dimensions={0}, use_global_device_ids=true | all-gather | bytes 16896 | tf_op jit(solution)/shard_map/all_gather | solution.py:177
  848.5 83.6 %all-gather.18.cloned.1.call-done = bf16[2048,8192]{1,0:T(8,128)(2,1)} async-done(((bf16[64,8192]{1,0:T(8,128)(2,1)}), bf16[2048,8192]{1,0:T(8,128)(2,1)}) %all-gather.18.cloned.1.call-update) | async-done | bytes 33554448 | tf_op jit(solution)/shard_map/all_gather | solution.py:176
  932.2 15.7 multiply_convert_fusion
  947.9 16.6 multiply_convert_fusion.1
  968.0 37.6 slice.234
  1005.6 9.4 fusion.176
  1015.3 37.3 slice.235
  1052.6 9.4 fusion.175
  1062.1 37.4 slice.236
  1099.4 9.4 fusion.174
  1109.3 18.6 all-gather.20.cloned.1.call-done
  1127.9 18.9 fusion.63
  1146.9 18.0 fusion.56
  1164.9 9.2 fusion.119
  1174.2 9.3 fusion.122
  1183.7 9.2 fusion.125
  1193.0 9.2 fusion.128
  1208.8 37.7 slice.219
  1250.1 17.5 fusion.184
  1267.6 14.3 convolution_add_fusion.4
  1281.9 17.1 fusion.183
  1299.1 15.5 fusion.115
  1317.1 8.2 fusion.177
  1325.3 38.6 concatenate.81
  1363.9 16.9 copy.213
  1382.0 8.1 fusion.134
  1400.4 13.6 fusion.71
  1414.1 13.4 fusion.70
  1430.9 59.6 %reduce-scatter.33.cloned.1.call-done = f32[64,2048]{1,0:T(8,128)} async-done(((f32[2048,2048]{1,0:T(8,128)}), f32[64,2048]{1,0:T(8,128)}) %reduce-scatter.33.cloned.1.call-update) | async-done | bytes 524304 | tf_op jit(solution)/shard_map/reduce_scatter | solution.py:108
  1490.6 364.3 %reduce-scatter.35.cloned.1.call-done = f32[64,2048]{1,0:T(8,128)} async-done(((f32[2048,2048]{1,0:T(8,128)}), f32[64,2048]{1,0:T(8,128)}) %reduce-scatter.35.cloned.1.call-update) | async-done | bytes 524304 | tf_op jit(solution)/shard_map/reduce_scatter | solution.py:108
  1854.9 364.3 %reduce-scatter.37.cloned.1.call-done = f32[64,2048]{1,0:T(8,128)} async-done(((f32[2048,2048]{1,0:T(8,128)}), f32[64,2048]{1,0:T(8,128)}) %reduce-scatter.37.cloned.1.call-update) | async-done | bytes 524304 | tf_op jit(solution)/shard_map/reduce_scatter | solution.py:108
  2221.8 361.7 %reduce-scatter.55.cloned.1.call-done = f32[64,2048]{1,0:T(8,128)} async-done(((f32[2048,2048]{1,0:T(8,128)}), f32[64,2048]{1,0:T(8,128)}) %reduce-scatter.55.cloned.1.call-update) | async-done | bytes 524304
  2584.9 362.9 %reduce-scatter.57.cloned.1.call-done = f32[64,2048]{1,0:T(8,128)} async-done(((f32[2048,2048]{1,0:T(8,128)}), f32[64,2048]{1,0:T(8,128)}) %reduce-scatter.57.cloned.1.call-update) | async-done | bytes 524304
  2949.2 363.0 %reduce-scatter.59.cloned.1.call-done = f32[64,2048]{1,0:T(8,128)} async-done(((f32[2048,2048]{1,0:T(8,128)}), f32[64,2048]{1,0:T(8,128)}) %reduce-scatter.59.cloned.1.call-update) | async-done | bytes 524304
  3313.6 363.1 %reduce-scatter.41.cloned.1.call-done = f32[64,2048]{1,0:T(8,128)} async-done(((f32[2048,2048]{1,0:T(8,128)}), f32[64,2048]{1,0:T(8,128)}) %reduce-scatter.41.cloned.1.call-update) | async-done | bytes 524304 | tf_op jit(solution)/shard_map/reduce_scatter | solution.py:108
  3676.7 364.3 %reduce-scatter.43.cloned.1.call-done = f32[64,2048]{1,0:T(8,128)} async-done(((f32[2048,2048]{1,0:T(8,128)}), f32[64,2048]{1,0:T(8,128)}) %reduce-scatter.43.cloned.1.call-update) | async-done | bytes 524304 | tf_op jit(solution)/shard_map/reduce_scatter | solution.py:108
  4041.0 364.5 %reduce-scatter.45.cloned.1.call-done = f32[64,2048]{1,0:T(8,128)} async-done(((f32[2048,2048]{1,0:T(8,128)}), f32[64,2048]{1,0:T(8,128)}) %reduce-scatter.45.cloned.1.call-update) | async-done | bytes 524304 | tf_op jit(solution)/shard_map/reduce_scatter | solution.py:108
  4405.5 364.5 %reduce-scatter.47.cloned.1.call-done = f32[64,2048]{1,0:T(8,128)} async-done(((f32[2048,2048]{1,0:T(8,128)}), f32[64,2048]{1,0:T(8,128)}) %reduce-scatter.47.cloned.1.call-update) | async-done | bytes 524304 | tf_op jit(solution)/shard_map/reduce_scatter | solution.py:108
  4772.9 383.9 %reduce-scatter.53.cloned.1.call-done = f32[64,2058]{1,0:T(8,128)} async-done(((f32[2048,2058]{1,0:T(8,128)}), f32[64,2058]{1,0:T(8,128)}) %reduce-scatter.53.cloned.1.call-update) | async-done | bytes 526864
  5173.4 348.3 %reduce-scatter.39.cloned.1.call-done = f32[64,2048]{1,0:T(8,128)} async-done(((f32[2048,2048]{1,0:T(8,128)}), f32[64,2048]{1,0:T(8,128)}) %reduce-scatter.39.cloned.1.call-update) | async-done | bytes 524304 | tf_op jit(solution)/shard_map/reduce_scatter | solution.py:108
  (420 shorter events, 292.0 us)
Async XLA Ops:
  7.2 158.8 %all-gather.10.cloned.1.call-start = ((), (), s32[]{:S(2)}) async-start(), calls=%async_computation.16 | async-start | bytes 25952256 | tf_op jit(solution)/shard_map/all_gather | solution.py:172
  7.9 238.5 %all-gather.16.cloned.1.call-start = ((), (), s32[]{:S(2)}) async-start(), calls=%async_computation.19 | async-start | bytes 8650752 | tf_op jit(solution)/shard_map/all_gather | solution.py:174
  8.7 276.2 %all-gather.12.cloned.1.call-start = ((), (), s32[]{:S(2)}) async-start(), calls=%async_computation.17 | async-start | bytes 4718592 | tf_op jit(solution)/shard_map/all_gather | solution.py:226
  54.4 111.5 %copy-start.52 = (f32[2048]{0:T(1024)}, f32[2048]{0:T(1024)S(1)}, u32[]{:S(2)}) copy-start(f32[2048]{0:T(1024)S(1)} %convert_element_type.184) | copy-start | bytes 24580
  56.4 119.6 %copy-start.62 = (f32[128]{0:T(128)}, f32[128]{0:T(128)S(1)}, u32[]{:S(2)}) copy-start(f32[128]{0:T(128)S(1)} %get-tuple-element.657) | copy-start | bytes 1540
  56.4 119.6 %copy-start.64 = (f32[128]{0:T(128)}, f32[128]{0:T(128)S(1)}, u32[]{:S(2)}) copy-start(f32[128]{0:T(128)S(1)} %get-tuple-element.658) | copy-start | bytes 1540
  58.1 107.9 %copy-start.74 = (f32[128]{0:T(128)}, f32[128]{0:T(128)S(1)}, u32[]{:S(2)}) copy-start(f32[128]{0:T(128)S(1)} %get-tuple-element.504) | copy-start | bytes 1540
  58.1 107.9 %copy-start.76 = (f32[128]{0:T(128)}, f32[128]{0:T(128)S(1)}, u32[]{:S(2)}) copy-start(f32[128]{0:T(128)S(1)} %get-tuple-element.505) | copy-start | bytes 1540
  58.1 117.9 %copy-start.66 = (f32[128]{0:T(128)}, f32[128]{0:T(128)S(1)}, u32[]{:S(2)}) copy-start(f32[128]{0:T(128)S(1)} %fusion.152) | copy-start | bytes 1540
  58.1 117.9 %copy-start.68 = (f32[128]{0:T(128)}, f32[128]{0:T(128)S(1)}, u32[]{:S(2)}) copy-start(f32[128]{0:T(128)S(1)} %fusion.153) | copy-start | bytes 1540
  60.5 115.5 %copy-start.11 = (bf16[128,2048]{1,0:T(8,128)(2,1)}, bf16[128,2048]{1,0:T(8,128)(2,1)S(1)}, u32[]{:S(2)}) copy-start(bf16[128,2048]{1,0:T(8,128)(2,1)S(1)} %get-tuple-element.600) | copy-start | bytes 1572868
  60.5 119.7 %copy-start.9 = (bf16[128,2048]{1,0:T(8,128)(2,1)}, bf16[128,2048]{1,0:T(8,128)(2,1)S(1)}, u32[]{:S(2)}) copy-start(bf16[128,2048]{1,0:T(8,128)(2,1)S(1)} %get-tuple-element.599) | copy-start | bytes 1572868
  193.8 52.6 copy-start.29
  197.0 127.7 %all-gather.22.cloned.1.call-start = ((), (), s32[]{:S(2)}) async-start(), calls=%async_computation.22 | async-start | bytes 4718592 | tf_op jit(solution)/shard_map/all_gather | solution.py:226
  199.9 163.8 %all-gather.14.cloned.1.call-start = ((), (), s32[]{:S(2)}) async-start(), calls=%async_computation.18 | async-start | bytes 4718592 | tf_op jit(solution)/shard_map/all_gather | solution.py:227
  202.1 266.5 %all-gather.24.cloned.1.call-start = ((), (), s32[]{:S(2)}) async-start(), calls=%async_computation.23 | async-start | bytes 4718592 | tf_op jit(solution)/shard_map/all_gather | solution.py:227
  202.9 49.8 copy-start.58
  202.9 49.7 copy-start.54
  253.7 11.0 copy-start.47
  264.6 312.9 %reduce-scatter.29.cloned.1.call-start = ((), (), s32[]{:S(2)}) async-start(), calls=%async_computation.24 | async-start | bytes 4718592 | tf_op jit(solution)/shard_map/reduce_scatter | solution.py:347
  336.0 34.1 copy-start.50
  468.5 157.5 %reduce-scatter.31.cloned.1.call-start = ((), (), s32[]{:S(2)}) async-start(), calls=%async_computation.25 | async-start | bytes 4718592 | tf_op jit(solution)/shard_map/reduce_scatter | solution.py:347
  574.7 106.0 %reduce-scatter.51.cloned.1.call-start = ((), (), s32[]{:S(2)}) async-start(), calls=%async_computation.35 | async-start | bytes 4718592
  575.5 160.1 %reduce-scatter.49.cloned.1.call-start = ((), (), s32[]{:S(2)}) async-start(), calls=%async_computation.34 | async-start | bytes 4718592
  576.0 356.1 %all-gather.18.cloned.1.call-start = ((), (), s32[]{:S(2)}) async-start(), calls=%async_computation.20 | async-start | bytes 34603008 | tf_op jit(solution)/shard_map/all_gather | solution.py:176
  576.8 551.2 %all-gather.20.cloned.1.call-start = ((), (), s32[]{:S(2)}) async-start(), calls=%async_computation.21 | async-start | bytes 34603008 | tf_op jit(solution)/shard_map/all_gather | solution.py:178
  577.4 913.2 %reduce-scatter.33.cloned.1.call-start = ((), (), s32[]{:S(2)}) async-start(), calls=%async_computation.26 | async-start | bytes 17301504 | tf_op jit(solution)/shard_map/reduce_scatter | solution.py:108
  577.5 160.1 %copy-start.56 = (f32[128,16]{0,1:T(8,128)S(1)}, f32[128,16]{0,1:T(8,128)}, u32[]{:S(2)}) copy-start(f32[128,16]{0,1:T(8,128)} %get-tuple-element.631) | copy-start | bytes 24580
  577.5 160.1 %copy-start.57 = (f32[128,16]{0,1:T(8,128)S(1)}, f32[128,16]{0,1:T(8,128)}, u32[]{:S(2)}) copy-start(f32[128,16]{0,1:T(8,128)} %get-tuple-element.632) | copy-start | bytes 24580
  739.4 15.7 copy-start.10
  739.4 15.7 copy-start.12
  763.3 1091.6 %reduce-scatter.35.cloned.1.call-start = ((), (), s32[]{:S(2)}) async-start(), calls=%async_computation.27 | async-start | bytes 17301504 | tf_op jit(solution)/shard_map/reduce_scatter | solution.py:108
  772.8 1446.4 %reduce-scatter.37.cloned.1.call-start = ((), (), s32[]{:S(2)}) async-start(), calls=%async_computation.28 | async-start | bytes 17301504 | tf_op jit(solution)/shard_map/reduce_scatter | solution.py:108
  783.2 65.2 %copy-start.30 = (bf16[2,1,128,2048]{3,2,1,0:T(8,128)(2,1)S(1)}, bf16[2,1,128,2048]{3,2,1,0:T(8,128)(2,1)}, u32[]{:S(2)}) copy-start(bf16[2,1,128,2048]{3,2,1,0:T(8,128)(2,1)} %param.29) | copy-start | bytes 3145732
  783.2 1800.4 %reduce-scatter.55.cloned.1.call-start = ((), (), s32[]{:S(2)}) async-start(), calls=%async_computation.37 | async-start | bytes 17301504
  848.5 250.9 %copy-start.17 = (bf16[128,2048]{1,0:T(8,128)(2,1)}, bf16[128,2048]{1,0:T(8,128)(2,1)S(1)}, u32[]{:S(2)}) copy-start(bf16[128,2048]{1,0:T(8,128)(2,1)S(1)} %get-tuple-element.605) | copy-start | bytes 1572868
  848.5 250.9 %copy-start.20 = (bf16[128,2048]{1,0:T(8,128)(2,1)}, bf16[128,2048]{1,0:T(8,128)(2,1)S(1)}, u32[]{:S(2)}) copy-start(bf16[128,2048]{1,0:T(8,128)(2,1)S(1)} %get-tuple-element.606) | copy-start | bytes 1572868
  947.9 16.6 copy-start.25
  1015.0 1932.9 %reduce-scatter.57.cloned.1.call-start = ((), (), s32[]{:S(2)}) async-start(), calls=%async_computation.38 | async-start | bytes 17301504
  1062.0 2250.2 %reduce-scatter.59.cloned.1.call-start = ((), (), s32[]{:S(2)}) async-start(), calls=%async_computation.39 | async-start | bytes 17301504
  1108.9 2567.8 %reduce-scatter.41.cloned.1.call-start = ((), (), s32[]{:S(2)}) async-start(), calls=%async_computation.30 | async-start | bytes 17301504 | tf_op jit(solution)/shard_map/reduce_scatter | solution.py:108
  1174.2 2866.8 %reduce-scatter.43.cloned.1.call-start = ((), (), s32[]{:S(2)}) async-start(), calls=%async_computation.31 | async-start | bytes 17301504 | tf_op jit(solution)/shard_map/reduce_scatter | solution.py:108
  1183.5 3222.0 %reduce-scatter.45.cloned.1.call-start = ((), (), s32[]{:S(2)}) async-start(), calls=%async_computation.32 | async-start | bytes 17301504 | tf_op jit(solution)/shard_map/reduce_scatter | solution.py:108
  1193.0 3577.0 %reduce-scatter.47.cloned.1.call-start = ((), (), s32[]{:S(2)}) async-start(), calls=%async_computation.33 | async-start | bytes 17301504 | tf_op jit(solution)/shard_map/reduce_scatter | solution.py:108
  1202.3 3954.5 %reduce-scatter.53.cloned.1.call-start = ((), (), s32[]{:S(2)}) async-start(), calls=%async_computation.36 | async-start | bytes 18382848
  1250.1 17.5 copy-start.40
  1250.1 17.5 copy-start.44
  1281.9 17.1 copy-start.13
  1281.9 17.1 copy-start.53
  1281.9 17.1 copy-start.63
  1281.9 17.1 copy-start.65
  1299.0 15.6 copy-start.77
  1299.0 15.6 copy-start.75
  1299.0 15.6 copy-start.67
  1299.0 15.6 copy-start.69
  1299.1 18.1 copy-start.19
  1299.1 18.1 copy-start.22
  1299.1 18.1 copy-start.32
  1380.8 4140.9 %reduce-scatter.39.cloned.1.call-start = ((), (), s32[]{:S(2)}) async-start(), calls=%async_computation.29 | async-start | bytes 17301504 | tf_op jit(solution)/shard_map/reduce_scatter | solution.py:108
  1400.4 13.6 copy-start.26
  1414.0 14.5 copy-start.31
  1414.1 14.5 copy-start.33
  1414.1 14.5 copy-start.34
  5170.2 352.0 %copy-start.78 = (f32[64,1]{0,1:T(1,128)}, f32[64,1]{0,1:T(1,128)S(1)}, u32[]{:S(2)}) copy-start(f32[64,1]{0,1:T(1,128)S(1)} %copy.233) | copy-start | bytes 772
  (48 other events, 160.7 us)
Sparse Core Ops, SparseCore 0:
  10.9 155.0 all-gather.9
  168.9 77.4 all-gather.15
  248.8 35.9 all-gather.11
  287.2 37.4 all-gather.21
  326.9 36.7 all-gather.13
  366.0 36.7 all-gather.23
  468.6 50.8 reduce-scatter.28
  574.8 51.0 reduce-scatter.30
  629.3 51.3 reduce-scatter.50
  684.2 51.2 reduce-scatter.48
  738.5 193.6 all-gather.17
  935.0 192.9 all-gather.19
  1130.2 360.2 reduce-scatter.32
  1492.7 362.1 reduce-scatter.34
  1857.0 362.1 reduce-scatter.36
  2221.4 362.1 reduce-scatter.54
  2585.7 362.1 reduce-scatter.56
  2950.0 362.1 reduce-scatter.58
  3314.5 362.1 reduce-scatter.40
  3678.8 362.1 reduce-scatter.42
  4043.3 362.1 reduce-scatter.44
  4407.8 362.1 reduce-scatter.46
  4772.3 384.4 reduce-scatter.52
  5159.5 362.1 reduce-scatter.38
where the time goes:
time: 5550 us; the launch traced here: 5530 us
  waiting for transfers between devices  4550 us (82%)
  matrix products  432 us (8%)
  local copies, waits for them, and re-layouts  359 us (6%)
  blocking collectives  106 us (2%)
  other arithmetic  65.2 us (1%)
    reduce_scatter x8, waiting for transfers between devices, scatter_grads(): lax.psum_scatter(rows(jnp.int32(0), lax.axis_size(('seq', 'fsdp')) * resi...  2590 us
    unnamed x30, waiting for transfers between devices  1580 us
    slice x4, local copies, waits for them, and re-layouts, scatter_grads(): hidden[:, slab::ratio]  150 us
  transfers between devices with their start and end apart: 24, of which 22 were waited for; matrix products, arithmetic and copies ran while one was open for 15% of the time, Pallas kernels for 0%

commit v1 on v0

v1 whole, which is shorter than its diff:
```python
import functools
import math

import jax
import jax.numpy as jnp
from jax import lax
from jax.experimental import pallas as pl
from jax.experimental.pallas import tpu as pltpu
from jax.sharding import PartitionSpec as P

HEADS = 32
HEAD_DIM = 64
ROT = 32
IMG = 256
PIECES = 2
EPSILON = 1e-05
BF = jnp.bfloat16
F32 = jnp.float32
SCALE = 1.0 / math.sqrt(HEAD_DIM)
LANES = 2 * HEAD_DIM


def swap(value, bit):
    size = lax.axis_size("seq")
    return lax.ppermute(value, "seq", [(i, i ^ bit) for i in range(size)])


def gather_seq(rows):
    size = lax.axis_size("seq")
    count = size.bit_length() - 1
    micro, length, width = rows.shape
    half = width // 2
    wide = []
    bits = list(range(1, count))
    for part, order in ((rows[..., :half], bits), (rows[..., half:], bits[::-1])):
        held = part.reshape((micro,) + (1,) * (count - 1) + (length, half))
        for bit in order:
            other = swap(held, 1 << bit)
            held = jnp.concatenate([held, other], axis=count - bit)
        wide.append(held.reshape(micro, size // 2, length, half))
    both = [jnp.stack([part, swap(part, 1)], axis=2) for part in wide]
    return jnp.concatenate(both, axis=-1).reshape(micro, size, length, width)


def scatter_seq(terms):
    size = lax.axis_size("seq")
    count = size.bit_length() - 1
    micro, _, length, width = terms.shape
    half = width // 2
    pairs = terms.reshape(micro, size // 2, 2, length, width)
    bits = list(range(1, count))
    sums = []
    for cols, order in ((slice(0, half), bits), (slice(half, width), bits[::-1])):
        held = pairs[:, :, 0, :, cols].astype(F32) + swap(pairs[:, :, 1, :, cols], 1).astype(F32)
        held = held.reshape((micro,) + (2,) * (count - 1) + (length, half))
        for bit in order:
            axis = count - bit
            held = held.astype(BF)
            away = lax.slice_in_dim(held, 1, 2, axis=axis)
            kept = lax.slice_in_dim(held, 0, 1, axis=axis)
            held = kept.astype(F32) + swap(away, 1 << bit).astype(F32)
        sums.append(held.reshape(micro, length, half))
    return jnp.concatenate(sums, axis=-1)


def gather_fsdp(mine, place):
    size = lax.axis_size("fsdp")
    at = lax.axis_index("fsdp")
    right = [mine]
    left = [mine]
    for step in range(1, size):
        right.append(
            lax.ppermute(right[-1], "fsdp", [(i, i + 1) for i in range(step - 1, size - 1)])
        )
        left.append(lax.ppermute(left[-1], "fsdp", [(i + 1, i) for i in range(0, size - step)]))
    out = place(None, mine, at)
    for step in range(1, size):
        piece = jnp.where(at >= step, right[step], left[size - step])
        out = place(out, piece, lax.rem(at - step + size, size))
    return out


def scatter_fsdp(chunk):
    size = lax.axis_size("fsdp")
    at = lax.axis_index("fsdp")
    right = left = None
    for step in range(1, size):
        going = chunk(jnp.minimum(size - step + at, size - 1))
        coming = chunk(jnp.maximum(step - size + at, 0))
        if step > 1:
            going = (going.astype(F32) + right.astype(F32)).astype(BF)
            coming = (coming.astype(F32) + left.astype(F32)).astype(BF)
        right = lax.ppermute(going, "fsdp", [(i, i + 1) for i in range(min(step, size - 1))])
        left = lax.ppermute(
            coming, "fsdp", [(size - 1 - i, size - 2 - i) for i in range(min(step, size - 1))]
        )
    return chunk(at).astype(F32) + right.astype(F32) + left.astype(F32)


def by_index(blocks):
    me = lax.axis_index("seq")
    shape = blocks.shape
    for bit in range(shape[0].bit_length() - 1):
        split = blocks.reshape((-1, 2, 1 << bit) + shape[1:])
        blocks = jnp.where((me >> bit) & 1 == 1, split[:, ::-1], split).reshape(shape)
    return blocks


def gather_small(vector):
    size, depth = lax.axis_size("seq"), lax.axis_size("fsdp")
    held = vector[None]
    for bit in range(size.bit_length() - 1):
        held = jnp.concatenate([held, swap(held, 1 << bit)], axis=0)
    deep = [held] + [
        lax.ppermute(held, "fsdp", [(i, (i + step) % depth) for i in range(depth)])
        for step in range(1, depth)
    ]
    deep = jnp.stack(deep[::-1] * 2, axis=1)
    start = depth - 1 - lax.axis_index("fsdp")
    return by_index(lax.dynamic_slice_in_dim(deep, start, depth, 1))


def scatter_small(terms):
    size, depth = lax.axis_size("seq"), lax.axis_size("fsdp")
    held = by_index(terms)
    for bit in reversed(range(size.bit_length() - 1)):
        n = held.shape[0] // 2
        held = held[:n] + swap(held[n:], 1 << bit)
    at = lax.axis_index("fsdp")
    held = held[0]
    total = lax.dynamic_index_in_dim(held, at, 0, keepdims=False)
    for step in range(1, depth):
        away = lax.dynamic_index_in_dim(held, (at + step) % depth, 0, keepdims=False)
        total = total + lax.ppermute(
            away, "fsdp", [(i, (i + step) % depth) for i in range(depth)]
        )
    return total


def attention_kernel(
    blocks,
    length,
    me_ref,
    starts_ref,
    cos_ref,
    sin_ref,
    q_ref,
    k_ref,
    v_ref,
    do_ref,
    mixed_ref,
    dq_ref,
    dk_ref,
    dv_ref,
    q_s,
    k_s,
    v_s,
    do_s,
    dk_s,
    dv_s,
    bias_s,
):
    micro = pl.program_id(0)
    me = me_ref[0]
    total = blocks * length
    tile = 256
    lane = lax.broadcasted_iota(jnp.int32, (1, LANES), 1)
    low_lane = (lane % HEAD_DIM) < (ROT // 2)

    def turn(value, cosine, sine):
        other = jnp.where(
            low_lane,
            pltpu.roll(value, LANES - ROT // 2, 1),
            pltpu.roll(value, ROT // 2, 1),
        )
        return value * cosine + other * sine

    for block in range(blocks):
        source = me ^ block
        at = slice(block * length, (block + 1) * length)
        cosine, sine = cos_ref[at, :], sin_ref[at, :]
        q_s[at, :] = (turn(q_ref[0, source], cosine, sine)).astype(BF) * jnp.asarray(SCALE, BF)
        k_s[at, :] = turn(k_ref[0, source], cosine, sine).astype(BF)
        v_s[at, :] = v_ref[0, source].astype(BF)
        do_s[at, :] = do_ref[0, source]
    dk_s[...] = jnp.zeros_like(dk_s)
    dv_s[...] = jnp.zeros_like(dv_s)

    def label(positions):
        found = jnp.full(positions.shape, -1, jnp.int32)
        for piece in range(PIECES):
            start = starts_ref[micro, piece]
            found = jnp.where((positions >= start) & (positions < start + IMG), piece, found)
        return found

    for first in range(0, total, tile):
        last = min(total, first + tile + IMG)
        qpos = first + lax.broadcasted_iota(jnp.int32, (tile, 1), 0)
        kpos = first + lax.broadcasted_iota(jnp.int32, (1, last - first), 1)
        qlab, klab = label(qpos), label(kpos)
        allowed = (kpos <= qpos) | ((qlab == klab) & (qlab >= 0))
        bias_s[:, : last - first] = jnp.where(allowed, 0.0, -1e30)
        rows = slice(first, first + tile)
        keys = k_s[:last, :]
        values = v_s[:last, :]
        mixed = jnp.zeros((tile, LANES), F32)
        dq = jnp.zeros((tile, LANES), F32)
        for head in range(LANES // HEAD_DIM):
            mine = (lane // HEAD_DIM) == head
            q = jnp.where(mine, q_s[rows, :], 0)
            do = jnp.where(mine, do_s[rows, :], 0)
            dims = (((1,), (1,)), ((), ()))
            s = lax.dot_general(q, keys, dims, preferred_element_type=F32)
            if first:
                s = jnp.concatenate(
                    [s[:, :first], s[:, first:] + bias_s[:, : last - first]], axis=1
                )
            else:
                s = s + bias_s[:, : last - first]
            p = jnp.exp(s - jnp.max(s, axis=1, keepdims=True))
            p = p * (1.0 / jnp.sum(p, axis=1, keepdims=True))
            probs = p.astype(BF)
            att = jnp.dot(probs, values, preferred_element_type=F32)
            mixed = jnp.where(mine, att, mixed)
            dp = lax.dot_general(do, values, dims, preferred_element_type=F32)
            delta = jnp.sum(p * dp, axis=1, keepdims=True)
            ds = (p * (dp - delta)).astype(BF)
            dq = jnp.where(mine, jnp.dot(ds, keys, preferred_element_type=F32), dq)
            over = (((0,), (0,)), ((), ()))
            dk_s[:last, :] += lax.dot_general(ds, q, over, preferred_element_type=F32)
            dv_s[:last, :] += lax.dot_general(probs, do, over, preferred_element_type=F32)
        dq = dq * SCALE
        for part in range(tile // length):
            block = first // length + part
            here = slice(part * length, (part + 1) * length)
            at = slice(block * length, (block + 1) * length)
            mixed_ref[0, me ^ block] = mixed[here].astype(BF)
            dq_ref[0, me ^ block] = turn(dq[here], cos_ref[at, :], -sin_ref[at, :]).astype(BF)
    for block in range(blocks):
        at = slice(block * length, (block + 1) * length)
        dk_ref[0, me ^ block] = turn(dk_s[at, :], cos_ref[at, :], -sin_ref[at, :]).astype(BF)
        dv_ref[0, me ^ block] = dv_s[at, :].astype(BF)


def attention(starts, projected, mixed_grad):
    micro, blocks, length, cols = mixed_grad.shape
    total = blocks * length
    groups = cols // LANES
    half = ROT // 2
    frequency = 10000.0 ** (-2.0 * jnp.arange(half, dtype=F32) / ROT)
    angles = jnp.arange(total, dtype=jnp.int32).astype(F32)[:, None] * frequency[None, :]
    cosine, sine = jnp.cos(angles), jnp.sin(angles)
    ones = jnp.ones((total, HEAD_DIM - ROT), F32)
    cosine = jnp.concatenate([cosine, cosine, ones] * 2, axis=1)
    sine = jnp.concatenate([-sine, sine, 0 * ones] * 2, axis=1)

    def spec(offset):
        return pl.BlockSpec(
            (1, blocks, length, LANES), lambda m, g, offset=offset: (m, 0, 0, offset * groups + g)
        )

    table = pl.BlockSpec((total, LANES), lambda m, g: (0, 0))
    shape = jax.ShapeDtypeStruct(mixed_grad.shape, BF)
    return pl.pallas_call(
        functools.partial(attention_kernel, blocks, length),
        grid=(micro, groups),
        in_specs=[
            pl.BlockSpec(memory_space=pltpu.SMEM),
            pl.BlockSpec(memory_space=pltpu.SMEM),
            table,
            table,
            spec(0),
            spec(1),
            spec(2),
            spec(0),
        ],
        out_specs=[spec(0)] * 4,
        out_shape=[shape] * 4,
        scratch_shapes=[pltpu.VMEM((total, LANES), BF)] * 4
        + [pltpu.VMEM((total, LANES), F32)] * 2
        + [pltpu.VMEM((256, 512), F32)],
        compiler_params=pltpu.CompilerParams(vmem_limit_bytes=48 * 1024 * 1024),
        cost_estimate=pl.CostEstimate(
            flops=micro * groups * 40 * total * total * HEAD_DIM,
            bytes_accessed=micro * groups * total * LANES * 22,
            transcendentals=micro * groups * 2 * total * total,
        ),
    )(lax.axis_index("seq")[None], starts, cosine, sine, projected, projected, projected, mixed_grad)


def gelu_tanh(values):
    return jax.nn.gelu(values, approximate=True)


def layer_norm(values, gain, shift):
    center = values - jnp.mean(values, axis=-1, keepdims=True)
    spread = jnp.mean(center * center, axis=-1, keepdims=True)
    return center * lax.rsqrt(spread + EPSILON) * gain + shift


def per_device(
    tokens,
    ln_gain,
    ln_bias,
    w_qkv,
    b_qkv,
    w_out,
    b_out,
    w_fc1,
    b_fc1,
    w_fc2,
    b_fc2,
    piece_starts,
    cotangent,
):
    size, depth = lax.axis_size("seq"), lax.axis_size("fsdp")
    me = lax.axis_index("seq")
    micro, _, length, width = tokens.shape
    rows = width // (size * depth)
    hidden_rows = w_fc2.shape[0]
    cols = width // size
    units = hidden_rows * depth
    tokens = tokens[:, 0]
    upstream = cotangent[:, 0]

    smalls = [ln_gain, ln_bias, b_qkv, b_out, b_fc1, b_fc2]
    sizes = [v.shape[0] for v in smalls]
    small = gather_small(jnp.concatenate(smalls)).astype(F32)
    full = []
    start = 0
    for count in sizes:
        full.append(small[:, :, start : start + count].reshape(-1))
        start += count
    gain, shift, bias_qkv, bias_out, bias_one, bias_two = full

    def to_columns(weight, parts):
        split = weight.reshape(rows, parts, size, -1).transpose(2, 0, 1, 3)
        split = split.reshape(size, rows, -1)
        return lax.all_to_all(split, "seq", 0, 0, tiled=True)

    def place_columns(buffer, piece, origin):
        if buffer is None:
            buffer = jnp.zeros((size, depth) + piece.shape[1:], piece.dtype)
        return lax.dynamic_update_slice_in_dim(buffer, piece[:, None], origin, 1)

    def place_rows(buffer, piece, origin):
        if buffer is None:
            buffer = jnp.zeros((depth,) + piece.shape, piece.dtype)
        return lax.dynamic_update_slice_in_dim(buffer, piece[None], origin, 0)

    all_tokens = gather_seq(tokens)
    my_out = gather_fsdp(w_out, place_rows).reshape(cols, width)
    my_qkv = gather_fsdp(to_columns(w_qkv, 3), place_columns).reshape(width, 3 * cols)
    all_up = gather_seq(upstream)
    my_one = gather_fsdp(to_columns(w_fc1, 1), place_columns).reshape(width, units)
    my_two = gather_fsdp(w_fc2, place_rows).reshape(units, width)

    count = micro * size * length
    bias_qkv = lax.dynamic_slice_in_dim(bias_qkv.reshape(3, width), me * cols, cols, 1).reshape(-1)
    bias_one = lax.dynamic_slice_in_dim(bias_one, me * units, units, 0)

    normed = layer_norm(all_tokens.astype(F32), gain, shift).astype(BF).reshape(count, width)
    up = all_up.reshape(count, width)

    def contract_last(left, right):
        return lax.dot_general(left, right, (((1,), (1,)), ((), ())), preferred_element_type=F32)

    def contract_first(left, right):
        return lax.dot_general(left, right, (((0,), (0,)), ((), ())), preferred_element_type=F32)

    projected = jnp.dot(normed, my_qkv, preferred_element_type=F32) + bias_qkv
    mixed_grad = contract_last(up, my_out).astype(BF)
    mixed, dq, dk, dv = attention(
        piece_starts[:, 0],
        projected.reshape(micro, size, length, 3 * cols),
        mixed_grad.reshape(micro, size, length, cols),
    )
    mixed = mixed.reshape(count, cols)
    projected_grad = jnp.concatenate([dq, dk, dv], axis=-1).reshape(count, 3 * cols)

    pre = jnp.dot(normed, my_one, preferred_element_type=F32) + bias_one
    hidden, back = jax.vjp(gelu_tanh, pre)
    hidden = hidden.astype(BF)
    pre_grad = back(contract_last(up, my_two))[0].astype(BF)

    terms = jnp.dot(mixed, my_out, preferred_element_type=F32)
    terms = terms + jnp.dot(hidden, my_two, preferred_element_type=F32)
    sums = scatter_seq(terms.astype(BF).reshape(micro, size, length, width))
    activations = (tokens.astype(F32) + sums + (bias_out + bias_two)).astype(BF)

    grad_terms = contract_last(projected_grad, my_qkv) + contract_last(pre_grad, my_one)
    normed_grad = scatter_seq(grad_terms.astype(BF).reshape(micro, size, length, width))
    _, norm_back = jax.vjp(layer_norm, tokens.astype(F32), gain, shift)
    input_grad, gain_grad, shift_grad = norm_back(normed_grad)
    input_grad = input_grad + upstream.astype(F32)

    def scatter_rows(grad):
        grad = grad.astype(BF).reshape(depth, -1, width)
        return scatter_fsdp(lambda o: lax.dynamic_index_in_dim(grad, o, 0, keepdims=False))

    def scatter_columns(grad, parts):
        grad = grad.astype(BF).reshape(size, depth, rows, -1)
        mine = scatter_fsdp(lambda o: lax.dynamic_index_in_dim(grad, o, 1, keepdims=False))
        mine = lax.all_to_all(mine.astype(BF), "seq", 0, 0, tiled=True).astype(F32)
        mine = mine.reshape(size, rows, parts, -1).transpose(1, 2, 0, 3)
        return mine.reshape(rows, -1)

    grad_two = scatter_rows(contract_first(hidden, up))
    grad_out = scatter_rows(contract_first(mixed, up))
    grad_one = scatter_columns(contract_first(normed, pre_grad), 1)
    grad_qkv = scatter_columns(contract_first(normed, projected_grad), 3)

    def put(values, extent, at):
        return lax.dynamic_update_slice_in_dim(jnp.zeros(extent, F32), values, at, -1)

    bqkv = jnp.sum(projected_grad.astype(F32), axis=0).reshape(3, cols)
    bqkv = put(bqkv, (3, width), me * cols)
    bone = put(jnp.sum(pre_grad.astype(F32), axis=0), (size * units,), me * units)
    btwo = jnp.sum(upstream.astype(F32), axis=(0, 1))
    packed = [gain_grad, shift_grad, bqkv[:2], bqkv[2], bone, btwo]
    packed = [v.reshape(size, depth, -1) for v in packed]
    summed = scatter_small(jnp.concatenate(packed, axis=-1))
    parts = []
    start = 0
    for v in packed:
        parts.append(summed[start : start + v.shape[-1]])
        start += v.shape[-1]
    return (
        activations[:, None],
        input_grad[:, None],
        parts[0],
        parts[1],
        grad_qkv,
        parts[2],
        parts[3],
        grad_out,
        parts[5],
        grad_one,
        parts[4],
        grad_two,
        parts[5],
    )


def solution(mesh):
    both = ("seq", "fsdp")
    row = P(both)
    matrix = P(both, None)
    tokens = P(None, "fsdp", "seq", None)
    weights = (row, row, matrix, row, matrix, row, matrix, row, matrix, row)
    grads = (row, row, matrix, row, row, matrix, row, matrix, row, matrix, row)
    return jax.shard_map(
        per_device,
        mesh=mesh,
        in_specs=(tokens,) + weights + (P(None, "fsdp", None), tokens),
        out_specs=(tokens, tokens) + grads,
        check_vma=False,
    )
```

time: 5550 us -> 842 us (0.15)
  waiting for transfers between devices: 4550 us -> 201 us
  matrix products: 432 us -> 145 us
  local copies, waits for them, and re-layouts: 359 us -> 80.1 us
  starting transfers between devices: 2.4 us -> 239 us
  blocking collectives: 106 us -> 0 us
    reduce_scatter x10 -> x0, waiting for transfers between devices: 2640 us -> none  [the longest x8 2590 us: scatter_grads(): lax.psum_scatter(rows(jnp.int32(0), lax.axis_size(('seq', 'fsdp')) * resi...]
    unnamed x30 -> x0, waiting for transfers between devices: 1580 us -> none
    all_gather x8 -> x0, waiting for transfers between devices: 326 us -> none  [the longest x1 105 us: per_device(): lax.all_gather(w_qkv, ('seq', 'fsdp'), axis=0, tiled=True)]
    dot_general x49 -> x12, matrix products: 404 us -> 145 us  [the longest x4 50.7 us: contract_last(): lax.dot_general(left, right, (((1,), (1,)), ((), ())), preferred_element_...]
    ppermute x0 -> x84, starting transfers between devices: none -> 209 us  [the longest x12 57.1 us: scatter_fsdp(): lax.ppermute(going, 'fsdp', [(i, i + 1) for i in range(min(step, size - 1...]
    ppermute x0 -> x84, waiting for transfers between devices: none -> 194 us  [the longest x12 51.2 us: scatter_fsdp(): lax.ppermute(going, 'fsdp', [(i, i + 1) for i in range(min(step, size - 1...]
    slice x25 -> x17, local copies, waits for them, and re-layouts: 164 us -> 7.86 us  [the longest x8 6.07 us: scatter_seq(): away = lax.slice_in_dim(held, 1, 2, axis=axis)]
    all_gather x1 -> x0, blocking collectives: 64.5 us -> none  [per_device(): lax.all_gather(b_fc1, ('seq', 'fsdp'), axis=0, tiled=True)]
  transfers between devices with their start and end apart: 24 -> 88, of which waited for: 22 -> 28; matrix products, arithmetic and copies ran while one was open for 15% -> 40% of each run, Pallas kernels for 0% -> 5%
where the time goes in v1:
time: 842 us; the launch traced here: 825 us
  starting transfers between devices  239 us (28%)
  waiting for transfers between devices  201 us (24%)
  matrix products  145 us (17%)
  other arithmetic  114 us (14%)
  local copies, waits for them, and re-layouts  80.1 us (10%)
  Pallas kernels  43.8 us (5%)
    ppermute x12, starting transfers between devices, scatter_fsdp(): lax.ppermute(going, 'fsdp', [(i, i + 1) for i in range(min(step, size - 1...  57.1 us
    ppermute x12, waiting for transfers between devices, scatter_fsdp(): lax.ppermute(going, 'fsdp', [(i, i + 1) for i in range(min(step, size - 1...  51.2 us
    dot_general x4, matrix products, contract_last(): lax.dot_general(left, right, (((1,), (1,)), ((), ())), preferred_element_...  50.7 us
    ppermute x30, starting transfers between devices, swap(): return lax.ppermute(value, 'seq', [(i, i ^ bit) for i in range(size)])  49.9 us
    ppermute x30, waiting for transfers between devices, swap(): return lax.ppermute(value, 'seq', [(i, i ^ bit) for i in range(size)])  49.8 us
    pallas_call x1, Pallas kernels, attention(): pl.pallas_call(functools.partial(attention_kernel, blocks, length), grid=...  43.8 us
    ppermute x12, waiting for transfers between devices, scatter_fsdp(): lax.ppermute(coming, 'fsdp', [(size - 1 - i, size - 2 - i) for i in range...  42.9 us
    ppermute x12, waiting for transfers between devices, gather_fsdp(): lax.ppermute(left[-1], 'fsdp', [(i + 1, i) for i in range(0, size - step)])  41.9 us
  transfers between devices with their start and end apart: 88, of which 28 were waited for; matrix products, arithmetic and copies ran while one was open for 40% of the time, Pallas kernels for 5%

profile of v1, /device:TPU:15, one launch (start us, length us, event | category | flops | bytes accessed | tf_op | source)
XLA Modules:
  0.0 825.3 jit_solution(16608419718295168566)
XLA Ops:
  2.9 3.2 collective-permute-start.24
  6.1 4.1 concatenate.110
  14.9 4.3 all-to-all-start
  30.0 10.2 %collective-permute-done.7 = bf16[2,704]{1,0:T(2,128)(2,1)S(1)} collective-permute-done((bf16[2,704]{1,0:T(2,128)(2,1)S(1)}, bf16[2,704]{1,0:T(2,128)(2,1)S(1)}, u32[]{:S(2)}, u32[]{:S(2)}) %collective-permute-start.7) | collective-permute-done | bytes 2848 | tf_op jit(solution)/shard_map/ppermute | solution.py:25
  57.3 4.5 collective-permute-start.26
  66.7 4.0 collective-permute-start.36
  72.8 12.1 %all-to-all-start.1 = ((bf16[8,64,1024]{2,1,0:T(8,128)(2,1)}), bf16[8,64,1024]{2,1,0:T(8,128)(2,1)}, u32[]{:S(2)}, u32[]{:S(2)}) async-start(bf16[8,64,1024]{2,1,0:T(8,128)(2,1)} %copy.257), calls=%async_computation.1 | async-start | bytes 2097152 | tf_op jit(solution)/shard_map/all_to_all | solution.py:339
  93.8 15.9 %collective-permute-done.27 = bf16[64,2048]{1,0:T(8,128)(2,1)S(1)} collective-permute-done((bf16[64,2048]{1,0:T(8,128)(2,1)S(1)}, bf16[64,2048]{1,0:T(8,128)(2,1)S(1)}, u32[]{:S(2)}, u32[]{:S(2)}) %collective-permute-start.27) | collective-permute-done | bytes 262176 | tf_op jit(solution)/shard_map/ppermute | solution.py:75
  118.7 4.4 collective-permute-start.14
  124.9 5.2 collective-permute-done.12
  130.0 2.9 collective-permute-start.16
  133.6 2.8 collective-permute-done.19
  137.4 4.2 collective-permute-start.38
  145.6 13.3 %collective-permute-done.1 = bf16[2,1,2,128,1024]{4,3,0,2,1:T(8,128)(2,1)} collective-permute-done((bf16[2,1,2,128,1024]{4,3,0,2,1:T(8,128)(2,1)}, bf16[2,1,2,128,1024]{4,3,0,2,1:T(8,128)(2,1)}, u32[]{:S(2)}, u32[]{:S(2)}) %collective-permute-start.1) | collective-permute-done | bytes 1048608 | tf_op jit(solution)/shard_map/ppermute | solution.py:25
  158.9 4.2 collective-permute-start.31
  172.3 4.9 collective-permute-done.15
  177.2 4.2 collective-permute-start.39
  187.9 11.8 %collective-permute-done.31 = bf16[8,64,1024]{2,1,0:T(8,128)(2,1)S(1)} collective-permute-done((bf16[8,64,1024]{2,1,0:T(8,128)(2,1)}, bf16[8,64,1024]{2,1,0:T(8,128)(2,1)S(1)}, u32[]{:S(2)}, u32[]{:S(2)}) %collective-permute-start.31) | collective-permute-done | bytes 1048608 | tf_op jit(solution)/shard_map/ppermute | solution.py:75
  199.7 9.5 %collective-permute-start.5 = (bf16[2,4,128,1024]{3,2,1,0:T(8,128)(2,1)S(1)}, bf16[2,4,128,1024]{3,2,1,0:T(8,128)(2,1)S(1)}, u32[]{:S(2)}, u32[]{:S(2)}) collective-permute-start(bf16[2,4,128,1024]{3,2,1,0:T(8,128)(2,1)S(1)} %bitcast.354), channel_id=1, source_target_pairs={{0,4},{4,0},{8,12},{12,8},{16,20},{20,16},{24,28},{28,24},{1,5},{5... | collective-permute-start | bytes 6291464 | tf_op jit(solution)/shard_map/ppermute | solution.py:25
  212.6 4.0 collective-permute-start.32
  216.6 11.9 %collective-permute-start.34 = (bf16[8,64,1024]{2,1,0:T(8,128)(2,1)S(1)}, bf16[8,64,1024]{2,1,0:T(8,128)(2,1)}, u32[]{:S(2)}, u32[]{:S(2)}) collective-permute-start(bf16[8,64,1024]{2,1,0:T(8,128)(2,1)S(1)} %collective-permute-done.30), channel_id=1, source_target_pairs={{1,2},{2,3},{5,6},{6,7},{9,10},{10,11},{13,14},{14,15},{17,18},{18... | collective-permute-start | bytes 3145736 | tf_op jit(solution)/shard_map/ppermute | solution.py:73
  232.4 3.4 collective-permute-start.23
  237.4 7.1 collective-permute-done.32
  244.5 5.0 collective-permute-start.20
  249.5 5.2 collective-permute-start.33
  263.4 6.4 maximum_convert_fusion
  270.6 5.5 convolution_convert_fusion.3
  276.2 11.5 %broadcast_add_fusion = f32[2048,768]{1,0:T(8,128)} fusion(f32[768]{0:T(1024)S(1)} %add.390, bf16[2048,768]{1,0:T(8,128)(2,1)} %bitcast.33, bf16[2048,1024]{1,0:T(8,128)(2,1)S(1)} %bitcast.416, bf16[2048,1024]{1,0:T(8,128)(2,1)S(1)} %bitcast.414, f32[2048]{0:T(1024)S(1)} %add.379, f32[2048]{0:T(1024)S(1)} %mul.236, f32[2048]{0:T(1024)S(1)} %bitcast.440, ...), kind=kOutput, calls=%fused_computation.44 | convolution fusion | flops 6481772544 | bytes 17861632 | tf_op jit(solution)/shard_map/dot_general | solution.py:371
  287.7 43.8 %shard_map.228 = (bf16[2,8,128,256]{3,2,1,0:T(8,128)(2,1)S(1)}, bf16[2,8,128,256]{3,2,1,0:T(8,128)(2,1)S(1)}, bf16[2,8,128,256]{3,2,1,0:T(8,128)(2,1)S(1)}, bf16[2,8,128,256]{3,2,1,0:T(8,128)(2,1)S(1)}) custom-call(s32[1]{0:T(128)} %bitcast.me_ref, s32[2,2]{1,0:T(2,128)S(1)} %bitcast.341, f32[1024,128]{1,0:T(8,128)S(1)} %concatenate.100.cos_ref, ...), custom_call_target="tpu_custom_call" | custom-call | flops 10737418240 | bytes 11534336 | tf_op jit(solution)/shard_map/pallas_call | solution.py:264
  338.5 10.2 %fusion.3 = bf16[2048,2048]{1,0:T(8,128)(2,1)} fusion(f32[2,4,2,128,2048]{4,3,2,1,0:T(8,128)} %maximum_convert_fusion, f32[2048]{0:T(1024)S(1)} %add.379, f32[2048]{0:T(1024)S(1)} %mul.236, f32[2048]{0:T(1024)S(1)} %bitcast.441, f32[2048]{0:T(1024)S(1)} %bitcast.436), kind=kLoop, calls=%fused_computation.4 | loop fusion | flops 20971520 | bytes 25198592 | tf_op jit(solution)/shard_map/convert_element_type | solution.py:362
  348.7 17.2 %copy.269 = f32[2,8,128,2048]{2,3,1,0:T(8,128)} copy(f32[2,8,128,2048]{3,2,1,0:T(8,128)} %bitcast.342) | data formatting | bytes 33554432 | tf_op jit(solution)/shard_map/convert_element_type | solution.py:362
  368.2 12.8 %bitcast_convert_fusion = bf16[2048,768]{1,0:T(8,128)(2,1)S(1)} fusion(bf16[2,8,128,768]{3,2,1,0:T(8,128)(2,1)} %constant_dynamic-update-slice_fusion.8, f32[2,8,128,2048]{2,3,1,0:T(8,128)} %copy.269, f32[2048]{0:T(1024)S(1)} %add.379, f32[2048]{0:T(1024)S(1)} %mul.236, f32[2,8,128]{2,1,0:T(8,128)S(1)} %bitcast.442, f32[2,8,128]{2,1,0:T(8,128)S(1)} %bitcast.437), kind=kOutput, calls=%fused_computation.28 | convolution fusion | flops 6464995328 | bytes 23101440 | tf_op jit(solution)/shard_map/dot_general | solution.py:369
  389.5 28.9 %collective-permute-start.67 = (bf16[64,2048]{1,0:T(8,128)(2,1)}, bf16[64,2048]{1,0:T(8,128)(2,1)}, u32[]{:S(2)}, u32[]{:S(2)}) collective-permute-start(bf16[64,2048]{1,0:T(8,128)(2,1)} %fusion.59), channel_id=1, source_target_pairs={{0,1},{1,2},{4,5},{5,6},{8,9},{9,10},{12,13},{13,14},{16,17},{17,1... | collective-permute-start | bytes 786440 | tf_op jit(solution)/shard_map/ppermute | solution.py:93
  423.9 13.7 %fusion.71 = f32[2048,1024]{1,0:T(8,128)} fusion(bf16[2048,1024]{1,0:T(8,128)(2,1)} %bitcast.418, bf16[2048,1024]{1,0:T(8,128)(2,1)S(1)} %bitcast.417, bf16[2048,1024]{1,0:T(8,128)(2,1)S(1)} %bitcast.415, f32[2048]{0:T(1024)S(1)} %add.379, f32[2048]{0:T(1024)S(1)} %mul.236, f32[2048]{0:T(1024)S(1)} %bitcast.443, f32[2048]{0:T(1024)S(1)} %bitcast.438), kind=kOutput, calls=%fused_computation.225 | convolution fusion | flops 8627683328 | bytes 21004288 | tf_op jit(solution)/shard_map/dot_general | solution.py:381
  437.6 13.3 %convolution_convert_fusion = bf16[1024,2048]{1,0:T(8,128)(2,1)S(1)} fusion(bf16[2048,2048]{1,0:T(8,128)(2,1)S(1)} %bitcast.347, f32[2048,1024]{1,0:T(8,128)} %fusion.71, f32[1024]{0:T(1024)S(1)} %dynamic_slice.112), kind=kOutput, calls=%fused_computation.40 | convolution fusion | flops 8613003264 | bytes 20975616 | tf_op jit(solution)/shard_map/dot_general | solution.py:369
  450.9 19.5 %convert_reduce_fusion = (f32[1024]{0:T(1024)S(1)}, bf16[2048,1024]{1,0:T(8,128)(2,1)}) fusion(f32[2048,1024]{1,0:T(8,128)} %fusion.71, f32[1024]{0:T(1024)S(1)} %dynamic_slice.112, bf16[2048,2048]{1,0:T(8,128)(2,1)S(1)} %bitcast.348, bf16[1024,2048]{1,0:T(8,128)(2,1)S(1)} %bitcast.421), kind=kOutput, calls=%fused_computation.26 | convolution fusion | flops 8638168064 | bytes 25174016 | tf_op jit(solution)/shard_map/dot_general | solution.py:366
  470.4 17.3 %fusion.69 = f32[2048,2048]{1,0:T(8,128)} fusion(bf16[1024,2048]{1,0:T(8,128)(2,1)} %bitcast.420, f32[2048,1024]{1,0:T(8,128)} %fusion.71, f32[1024]{0:T(1024)S(1)} %dynamic_slice.112), kind=kOutput, calls=%fused_computation.223 | convolution fusion | flops 8610906112 | bytes 29364224 | tf_op jit(solution)/shard_map/dot_general | solution.py:387
  490.7 11.7 %fusion.75 = f32[2048,2048]{1,0:T(8,128)} fusion(bf16[2048,1024]{1,0:T(8,128)(2,1)S(1)} %copy-done.65, bf16[2048,1024]{1,0:T(8,128)(2,1)S(1)} %bitcast.419), kind=kOutput, calls=%fused_computation.228 | convolution fusion | flops 8589934592 | bytes 25165824 | tf_op jit(solution)/shard_map/dot_general | solution.py:366
  502.3 10.8 %convolution_convert_fusion.1 = bf16[2048,1024]{1,0:T(8,128)(2,1)} fusion(bf16[2048,2048]{1,0:T(8,128)(2,1)S(1)} %bitcast.401, bf16[2048,1024]{1,0:T(8,128)(2,1)S(1)} %copy-done.65), kind=kOutput, calls=%fused_computation.41 | convolution fusion | flops 8592031744 | bytes 16777216 | tf_op jit(solution)/shard_map/dot_general | solution.py:369
  513.1 14.0 %add_convert_fusion.1 = bf16[2048,2048]{1,0:T(8,128)(2,1)} fusion(f32[2048,2048]{1,0:T(8,128)} %fusion.75, bf16[2048,768]{1,0:T(8,128)(2,1)} %bitcast.412, bf16[2048,768]{1,0:T(8,128)(2,1)} %bitcast.33), kind=kOutput, calls=%fused_computation.6 | convolution fusion | flops 6450839552 | bytes 31457280 | tf_op jit(solution)/shard_map/dot_general | solution.py:366
  527.1 12.0 %add_convert_fusion.2 = bf16[2048,2048]{1,0:T(8,128)(2,1)} fusion(f32[2048,2048]{1,0:T(8,128)} %fusion.69, bf16[2048,256]{1,0:T(8,128)(2,1)S(1)} %bitcast.340, bf16[256,2048]{1,0:T(8,128)(2,1)} %bitcast.49), kind=kOutput, calls=%fused_computation.7 | convolution fusion | flops 2155872256 | bytes 27262976 | tf_op jit(solution)/shard_map/dot_general | solution.py:386
  547.1 7.5 collective-permute-start.61
  559.7 2.9 slice_bitcast_fusion.6
  562.6 35.7 %collective-permute-done.71 = bf16[64,2048]{1,0:T(8,128)(2,1)S(1)} collective-permute-done((bf16[64,2048]{1,0:T(8,128)(2,1)S(1)}, bf16[64,2048]{1,0:T(8,128)(2,1)S(1)}, u32[]{:S(2)}, u32[]{:S(2)}) %collective-permute-start.71) | collective-permute-done | bytes 262176 | tf_op jit(solution)/shard_map/ppermute | solution.py:94
  612.0 15.5 %collective-permute-done.72 = bf16[8,64,1024]{2,1,0:T(8,128)(2,1)S(1)} collective-permute-done((bf16[8,64,1024]{2,1,0:T(8,128)(2,1)S(1)}, bf16[8,64,1024]{2,1,0:T(8,128)(2,1)S(1)}, u32[]{:S(2)}, u32[]{:S(2)}) %collective-permute-start.72) | collective-permute-done | bytes 1048608 | tf_op jit(solution)/shard_map/ppermute | solution.py:93
  629.8 14.5 %collective-permute-done.62 = bf16[8,64,768]{2,1,0:T(8,128)(2,1)S(1)} collective-permute-done((bf16[8,64,768]{2,1,0:T(8,128)(2,1)S(1)}, bf16[8,64,768]{2,1,0:T(8,128)(2,1)S(1)}, u32[]{:S(2)}, u32[]{:S(2)}) %collective-permute-start.62) | collective-permute-done | bytes 786464 | tf_op jit(solution)/shard_map/ppermute | solution.py:93
  645.7 2.9 fusion.37
  656.7 4.2 all-to-all-start.2
  660.8 5.7 fusion.19
  667.9 7.7 collective-permute-done.79
  675.9 3.4 fusion.38
  684.5 13.5 %collective-permute-done.73 = bf16[8,64,1024]{2,1,0:T(8,128)(2,1)} collective-permute-done((bf16[8,64,1024]{2,1,0:T(8,128)(2,1)}, bf16[8,64,1024]{2,1,0:T(8,128)(2,1)}, u32[]{:S(2)}, u32[]{:S(2)}) %collective-permute-start.73) | collective-permute-done | bytes 1048608 | tf_op jit(solution)/shard_map/ppermute | solution.py:93
  698.3 4.0 fusion.43
  703.6 4.0 collective-permute-start.74
  707.7 4.3 fusion.17
  730.4 3.0 fusion.36
  733.3 11.8 %collective-permute-done.49 = bf16[2,2,1,128,1024]{4,3,0,2,1:T(8,128)(2,1)S(1)} collective-permute-done((bf16[2,2,1,128,1024]{4,3,0,2,1:T(8,128)(2,1)S(1)}, bf16[2,2,1,128,1024]{4,3,0,2,1:T(8,128)(2,1)S(1)}, u32[]{:S(2)}, u32[]{:S(2)}) %collective-permute-start.49) | collective-permute-done | bytes 1048608 | tf_op jit(solution)/shard_map/ppermute | solution.py:25
  749.9 3.1 collective-permute-done.76
  768.5 3.4 collective-permute-start.77
  780.8 9.6 %collective-permute-start.56 = (f32[1,4,640]{2,1,0:T(4,128)S(1)}, f32[1,4,640]{2,1,0:T(4,128)S(1)}, u32[]{:S(2)}, u32[]{:S(2)}) collective-permute-start(f32[1,4,640]{2,1,0:T(4,128)S(1)} %slice.241), channel_id=1, source_target_pairs={{0,4},{4,0},{8,12},{12,8},{16,20},{20,16},{24,28},{28,24},{1,5},{5... | collective-permute-start | bytes 30728 | tf_op jit(solution)/shard_map/ppermute | solution.py:25
  798.1 3.1 fusion.45
  801.3 8.7 %all-to-all-start.3 = ((bf16[8,64,1024]{2,1,0:T(8,128)(2,1)}), bf16[8,64,1024]{2,1,0:T(8,128)(2,1)S(1)}, u32[]{:S(2)}, u32[]{:S(2)}) async-start(bf16[8,64,1024]{2,1,0:T(8,128)(2,1)} %fusion.45), calls=%async_computation.3 | async-start | bytes 2097152 | tf_op jit(solution)/shard_map/all_to_all | solution.py:404
  811.7 3.7 fusion.39
  815.5 7.2 all-to-all-done.3
  (452 shorter events, 232.0 us)
Async XLA Ops:
  0.7 56.6 %collective-permute-start.25 = (bf16[64,2048]{1,0:T(8,128)(2,1)}, bf16[64,2048]{1,0:T(8,128)(2,1)}, u32[]{:S(2)}, u32[]{:S(2)}) collective-permute-start(bf16[64,2048]{1,0:T(8,128)(2,1)} %param.18), channel_id=1, source_target_pairs={{1,0},{2,1},{3,2},{5,4},{6,5},{7,6},{9,8},{10,9},{11,10},{13,12},{... | collective-permute-start | bytes 786440 | tf_op jit(solution)/shard_map/ppermute | solution.py:75
  2.9 58.9 %collective-permute-start.24 = (bf16[64,2048]{1,0:T(8,128)(2,1)}, bf16[64,2048]{1,0:T(8,128)(2,1)}, u32[]{:S(2)}, u32[]{:S(2)}) collective-permute-start(bf16[64,2048]{1,0:T(8,128)(2,1)} %param.18), channel_id=1, source_target_pairs={{0,1},{1,2},{2,3},{4,5},{5,6},{6,7},{8,9},{9,10},{10,11},{12,13},{... | collective-permute-start | bytes 786440 | tf_op jit(solution)/shard_map/ppermute | solution.py:73
  14.9 58.0 %all-to-all-start = ((bf16[8,64,768]{2,1,0:T(8,128)(2,1)}), bf16[8,64,768]{2,1,0:T(8,128)(2,1)}, u32[]{:S(2)}, u32[]{:S(2)}) async-start(bf16[8,64,768]{2,1,0:T(8,128)(2,1)} %reshape.422), calls=%async_computation | async-start | bytes 1572864 | tf_op jit(solution)/shard_map/all_to_all | solution.py:339
  20.0 50.8 %collective-permute-start = (bf16[2,1,1,128,1024]{4,3,0,2,1:T(8,128)(2,1)}, bf16[2,1,1,128,1024]{4,3,0,2,1:T(8,128)(2,1)}, u32[]{:S(2)}, u32[]{:S(2)}) collective-permute-start(bf16[2,1,1,128,1024]{4,3,0,2,1:T(8,128)(2,1)} %get-tuple-element.66), channel_id=1, source_target_pairs={{0,8},{4,12},{8,0},{12,4},{16,24},{20,28},{24,16},{28,20},{1,9},{5... | collective-permute-start | bytes 1572872 | tf_op jit(solution)/shard_map/ppermute | solution.py:25
  20.2 92.9 %collective-permute-start.37 = (bf16[256,2048]{1,0:T(8,128)(2,1)}, bf16[256,2048]{1,0:T(8,128)(2,1)}, u32[]{:S(2)}, u32[]{:S(2)}) collective-permute-start(bf16[256,2048]{1,0:T(8,128)(2,1)} %param.22), channel_id=1, source_target_pairs={{1,0},{2,1},{3,2},{5,4},{6,5},{7,6},{9,8},{10,9},{11,10},{13,12},{... | collective-permute-start | bytes 3145736 | tf_op jit(solution)/shard_map/ppermute | solution.py:75
  56.9 28.1 %collective-permute-start.3 = (bf16[2,1,1,128,1024]{4,3,0,2,1:T(8,128)(2,1)S(1)}, bf16[2,1,1,128,1024]{4,3,0,2,1:T(8,128)(2,1)S(1)}, u32[]{:S(2)}, u32[]{:S(2)}) collective-permute-start(bf16[2,1,1,128,1024]{4,3,0,2,1:T(8,128)(2,1)S(1)} %get-tuple-element.67), channel_id=1, source_target_pairs={{0,16},{4,20},{8,24},{12,28},{16,0},{20,4},{24,8},{28,12},{1,17},{... | collective-permute-start | bytes 1572872 | tf_op jit(solution)/shard_map/ppermute | solution.py:25
  65.4 23.0 %collective-permute-start.18 = (bf16[2,1,1,128,1024]{4,3,0,2,1:T(8,128)(2,1)}, bf16[2,1,1,128,1024]{4,3,0,2,1:T(8,128)(2,1)}, u32[]{:S(2)}, u32[]{:S(2)}) collective-permute-start(bf16[2,1,1,128,1024]{4,3,0,2,1:T(8,128)(2,1)} %get-tuple-element.64), channel_id=1, source_target_pairs={{0,8},{4,12},{8,0},{12,4},{16,24},{20,28},{24,16},{28,20},{1,9},{5... | collective-permute-start | bytes 1572872 | tf_op jit(solution)/shard_map/ppermute | solution.py:25
  66.7 50.8 %collective-permute-start.36 = (bf16[256,2048]{1,0:T(8,128)(2,1)}, bf16[256,2048]{1,0:T(8,128)(2,1)}, u32[]{:S(2)}, u32[]{:S(2)}) collective-permute-start(bf16[256,2048]{1,0:T(8,128)(2,1)} %param.22), channel_id=1, source_target_pairs={{0,1},{1,2},{2,3},{4,5},{5,6},{6,7},{8,9},{9,10},{10,11},{12,13},{... | collective-permute-start | bytes 3145736 | tf_op jit(solution)/shard_map/ppermute | solution.py:73
  72.8 72.8 %all-to-all-start.1 = ((bf16[8,64,1024]{2,1,0:T(8,128)(2,1)}), bf16[8,64,1024]{2,1,0:T(8,128)(2,1)}, u32[]{:S(2)}, u32[]{:S(2)}) async-start(bf16[8,64,1024]{2,1,0:T(8,128)(2,1)} %copy.257), calls=%async_computation.1 | async-start | bytes 2097152 | tf_op jit(solution)/shard_map/all_to_all | solution.py:339
  85.0 33.7 %collective-permute-start.13 = (bf16[8,64,768]{2,1,0:T(8,128)(2,1)}, bf16[8,64,768]{2,1,0:T(8,128)(2,1)S(1)}, u32[]{:S(2)}, u32[]{:S(2)}) collective-permute-start(bf16[8,64,768]{2,1,0:T(8,128)(2,1)} %all-to-all-done), channel_id=1, source_target_pairs={{1,0},{2,1},{3,2},{5,4},{6,5},{7,6},{9,8},{10,9},{11,10},{13,12},{... | collective-permute-start | bytes 2359304 | tf_op jit(solution)/shard_map/ppermute | solution.py:75
  88.4 21.3 %collective-permute-start.27 = (bf16[64,2048]{1,0:T(8,128)(2,1)S(1)}, bf16[64,2048]{1,0:T(8,128)(2,1)S(1)}, u32[]{:S(2)}, u32[]{:S(2)}) collective-permute-start(bf16[64,2048]{1,0:T(8,128)(2,1)S(1)} %collective-permute-done.26), channel_id=1, source_target_pairs={{1,0},{5,4},{9,8},{13,12},{17,16},{21,20},{25,24},{29,28}} | collective-permute-start | bytes 786440 | tf_op jit(solution)/shard_map/ppermute | solution.py:75
  112.8 23.6 %collective-permute-start.19 = (bf16[2,1,2,128,1024]{4,3,0,2,1:T(8,128)(2,1)S(1)}, bf16[2,1,2,128,1024]{4,3,0,2,1:T(8,128)(2,1)S(1)}, u32[]{:S(2)}, u32[]{:S(2)}) collective-permute-start(bf16[2,1,2,128,1024]{4,3,0,2,1:T(8,128)(2,1)S(1)} %pad_maximum_fusion.9), channel_id=1, source_target_pairs={{0,16},{4,20},{8,24},{12,28},{16,0},{20,4},{24,8},{28,12},{1,17},{... | collective-permute-start | bytes 3145736 | tf_op jit(solution)/shard_map/ppermute | solution.py:25
  113.1 23.6 %collective-permute-start.22 = (bf16[2,2,1,128,1024]{4,3,0,2,1:T(8,128)(2,1)S(1)}, bf16[2,2,1,128,1024]{4,3,0,2,1:T(8,128)(2,1)S(1)}, u32[]{:S(2)}, u32[]{:S(2)}) collective-permute-start(bf16[2,2,1,128,1024]{4,3,0,2,1:T(8,128)(2,1)S(1)} %pad_maximum_fusion.10), channel_id=1, source_target_pairs={{0,8},{4,12},{8,0},{12,4},{16,24},{20,28},{24,16},{28,20},{1,9},{5... | collective-permute-start | bytes 3145736 | tf_op jit(solution)/shard_map/ppermute | solution.py:25
  117.5 41.4 %collective-permute-start.1 = (bf16[2,1,2,128,1024]{4,3,0,2,1:T(8,128)(2,1)}, bf16[2,1,2,128,1024]{4,3,0,2,1:T(8,128)(2,1)}, u32[]{:S(2)}, u32[]{:S(2)}) collective-permute-start(bf16[2,1,2,128,1024]{4,3,0,2,1:T(8,128)(2,1)} %pad_maximum_fusion.7), channel_id=1, source_target_pairs={{0,16},{4,20},{8,24},{12,28},{16,0},{20,4},{24,8},{28,12},{1,17},{... | collective-permute-start | bytes 3145736 | tf_op jit(solution)/shard_map/ppermute | solution.py:25
  118.7 23.0 %collective-permute-start.14 = (bf16[8,64,768]{2,1,0:T(8,128)(2,1)S(1)}, bf16[8,64,768]{2,1,0:T(8,128)(2,1)}, u32[]{:S(2)}, u32[]{:S(2)}) collective-permute-start(bf16[8,64,768]{2,1,0:T(8,128)(2,1)S(1)} %collective-permute-done.13), channel_id=1, source_target_pairs={{1,0},{2,1},{5,4},{6,5},{9,8},{10,9},{13,12},{14,13},{17,16},{18,1... | collective-permute-start | bytes 2359304 | tf_op jit(solution)/shard_map/ppermute | solution.py:75
  130.0 35.1 %collective-permute-start.16 = (bf16[8,64,768]{2,1,0:T(8,128)(2,1)}, bf16[8,64,768]{2,1,0:T(8,128)(2,1)}, u32[]{:S(2)}, u32[]{:S(2)}) collective-permute-start(bf16[8,64,768]{2,1,0:T(8,128)(2,1)} %collective-permute-done.12), channel_id=1, source_target_pairs={{1,2},{2,3},{5,6},{6,7},{9,10},{10,11},{13,14},{14,15},{17,18},{18... | collective-permute-start | bytes 2359304 | tf_op jit(solution)/shard_map/ppermute | solution.py:73
  136.5 32.6 %collective-permute-start.4 = (bf16[2,2,1,128,1024]{4,3,0,2,1:T(8,128)(2,1)}, bf16[2,2,1,128,1024]{4,3,0,2,1:T(8,128)(2,1)}, u32[]{:S(2)}, u32[]{:S(2)}) collective-permute-start(bf16[2,2,1,128,1024]{4,3,0,2,1:T(8,128)(2,1)} %pad_maximum_fusion.8), channel_id=1, source_target_pairs={{0,8},{4,12},{8,0},{12,4},{16,24},{20,28},{24,16},{28,20},{1,9},{5... | collective-permute-start | bytes 3145736 | tf_op jit(solution)/shard_map/ppermute | solution.py:25
  137.4 33.6 %collective-permute-start.38 = (bf16[256,2048]{1,0:T(8,128)(2,1)}, bf16[256,2048]{1,0:T(8,128)(2,1)}, u32[]{:S(2)}, u32[]{:S(2)}) collective-permute-start(bf16[256,2048]{1,0:T(8,128)(2,1)} %collective-permute-done.37), channel_id=1, source_target_pairs={{1,0},{2,1},{5,4},{6,5},{9,8},{10,9},{13,12},{14,13},{17,16},{18,1... | collective-permute-start | bytes 3145736 | tf_op jit(solution)/shard_map/ppermute | solution.py:75
  141.7 35.5 %collective-permute-start.15 = (bf16[8,64,768]{2,1,0:T(8,128)(2,1)}, bf16[8,64,768]{2,1,0:T(8,128)(2,1)}, u32[]{:S(2)}, u32[]{:S(2)}) collective-permute-start(bf16[8,64,768]{2,1,0:T(8,128)(2,1)} %collective-permute-done.14), channel_id=1, source_target_pairs={{1,0},{5,4},{9,8},{13,12},{17,16},{21,20},{25,24},{29,28}} | collective-permute-start | bytes 2359304 | tf_op jit(solution)/shard_map/ppermute | solution.py:75
  158.9 40.8 %collective-permute-start.31 = (bf16[8,64,1024]{2,1,0:T(8,128)(2,1)}, bf16[8,64,1024]{2,1,0:T(8,128)(2,1)S(1)}, u32[]{:S(2)}, u32[]{:S(2)}) collective-permute-start(bf16[8,64,1024]{2,1,0:T(8,128)(2,1)} %all-to-all-done.1), channel_id=1, source_target_pairs={{1,0},{2,1},{3,2},{5,4},{6,5},{7,6},{9,8},{10,9},{11,10},{13,12},{... | collective-permute-start | bytes 3145736 | tf_op jit(solution)/shard_map/ppermute | solution.py:75
  165.2 44.1 %collective-permute-start.17 = (bf16[8,64,768]{2,1,0:T(8,128)(2,1)}, bf16[8,64,768]{2,1,0:T(8,128)(2,1)S(1)}, u32[]{:S(2)}, u32[]{:S(2)}) collective-permute-start(bf16[8,64,768]{2,1,0:T(8,128)(2,1)} %collective-permute-done.16), channel_id=1, source_target_pairs={{2,3},{6,7},{10,11},{14,15},{18,19},{22,23},{26,27},{30,31}} | collective-permute-start | bytes 2359304 | tf_op jit(solution)/shard_map/ppermute | solution.py:73
  169.0 43.6 %collective-permute-start.30 = (bf16[8,64,1024]{2,1,0:T(8,128)(2,1)}, bf16[8,64,1024]{2,1,0:T(8,128)(2,1)S(1)}, u32[]{:S(2)}, u32[]{:S(2)}) collective-permute-start(bf16[8,64,1024]{2,1,0:T(8,128)(2,1)} %all-to-all-done.1), channel_id=1, source_target_pairs={{0,1},{1,2},{2,3},{4,5},{5,6},{6,7},{8,9},{9,10},{10,11},{12,13},{... | collective-permute-start | bytes 3145736 | tf_op jit(solution)/shard_map/ppermute | solution.py:73
  171.0 45.6 %collective-permute-start.40 = (bf16[256,2048]{1,0:T(8,128)(2,1)}, bf16[256,2048]{1,0:T(8,128)(2,1)S(1)}, u32[]{:S(2)}, u32[]{:S(2)}) collective-permute-start(bf16[256,2048]{1,0:T(8,128)(2,1)} %collective-permute-done.36), channel_id=1, source_target_pairs={{1,2},{2,3},{5,6},{6,7},{9,10},{10,11},{13,14},{14,15},{17,18},{18... | collective-permute-start | bytes 3145736 | tf_op jit(solution)/shard_map/ppermute | solution.py:73
  177.2 51.2 %collective-permute-start.39 = (bf16[256,2048]{1,0:T(8,128)(2,1)}, bf16[256,2048]{1,0:T(8,128)(2,1)S(1)}, u32[]{:S(2)}, u32[]{:S(2)}) collective-permute-start(bf16[256,2048]{1,0:T(8,128)(2,1)} %collective-permute-done.38), channel_id=1, source_target_pairs={{1,0},{5,4},{9,8},{13,12},{17,16},{21,20},{25,24},{29,28}} | collective-permute-start | bytes 3145736 | tf_op jit(solution)/shard_map/ppermute | solution.py:75
  199.7 57.0 %collective-permute-start.5 = (bf16[2,4,128,1024]{3,2,1,0:T(8,128)(2,1)S(1)}, bf16[2,4,128,1024]{3,2,1,0:T(8,128)(2,1)S(1)}, u32[]{:S(2)}, u32[]{:S(2)}) collective-permute-start(bf16[2,4,128,1024]{3,2,1,0:T(8,128)(2,1)S(1)} %bitcast.354), channel_id=1, source_target_pairs={{0,4},{4,0},{8,12},{12,8},{16,20},{20,16},{24,28},{28,24},{1,5},{5... | collective-permute-start | bytes 6291464 | tf_op jit(solution)/shard_map/ppermute | solution.py:25
  209.2 45.5 %collective-permute-start.2 = (bf16[2,4,128,1024]{3,2,1,0:T(8,128)(2,1)S(1)}, bf16[2,4,128,1024]{3,2,1,0:T(8,128)(2,1)S(1)}, u32[]{:S(2)}, u32[]{:S(2)}) collective-permute-start(bf16[2,4,128,1024]{3,2,1,0:T(8,128)(2,1)S(1)} %bitcast.349), channel_id=1, source_target_pairs={{0,4},{4,0},{8,12},{12,8},{16,20},{20,16},{24,28},{28,24},{1,5},{5... | collective-permute-start | bytes 6291464 | tf_op jit(solution)/shard_map/ppermute | solution.py:25
  212.6 31.9 %collective-permute-start.32 = (bf16[8,64,1024]{2,1,0:T(8,128)(2,1)S(1)}, bf16[8,64,1024]{2,1,0:T(8,128)(2,1)}, u32[]{:S(2)}, u32[]{:S(2)}) collective-permute-start(bf16[8,64,1024]{2,1,0:T(8,128)(2,1)S(1)} %collective-permute-done.31), channel_id=1, source_target_pairs={{1,0},{2,1},{5,4},{6,5},{9,8},{10,9},{13,12},{14,13},{17,16},{18,1... | collective-permute-start | bytes 3145736 | tf_op jit(solution)/shard_map/ppermute | solution.py:75
  216.6 32.9 %collective-permute-start.34 = (bf16[8,64,1024]{2,1,0:T(8,128)(2,1)S(1)}, bf16[8,64,1024]{2,1,0:T(8,128)(2,1)}, u32[]{:S(2)}, u32[]{:S(2)}) collective-permute-start(bf16[8,64,1024]{2,1,0:T(8,128)(2,1)S(1)} %collective-permute-done.30), channel_id=1, source_target_pairs={{1,2},{2,3},{5,6},{6,7},{9,10},{10,11},{13,14},{14,15},{17,18},{18... | collective-permute-start | bytes 3145736 | tf_op jit(solution)/shard_map/ppermute | solution.py:73
  232.4 37.4 %collective-permute-start.23 = (bf16[2,4,128,1024]{3,2,1,0:T(8,128)(2,1)S(1)}, bf16[2,4,128,1024]{3,2,1,0:T(8,128)(2,1)S(1)}, u32[]{:S(2)}, u32[]{:S(2)}) collective-permute-start(bf16[2,4,128,1024]{3,2,1,0:T(8,128)(2,1)S(1)} %bitcast.404), channel_id=1, source_target_pairs={{0,4},{4,0},{8,12},{12,8},{16,20},{20,16},{24,28},{28,24},{1,5},{5... | collective-permute-start | bytes 6291464 | tf_op jit(solution)/shard_map/ppermute | solution.py:25
  244.5 25.3 %collective-permute-start.20 = (bf16[2,4,128,1024]{3,2,1,0:T(8,128)(2,1)S(1)}, bf16[2,4,128,1024]{3,2,1,0:T(8,128)(2,1)S(1)}, u32[]{:S(2)}, u32[]{:S(2)}) collective-permute-start(bf16[2,4,128,1024]{3,2,1,0:T(8,128)(2,1)S(1)} %bitcast.402), channel_id=1, source_target_pairs={{0,4},{4,0},{8,12},{12,8},{16,20},{20,16},{24,28},{28,24},{1,5},{5... | collective-permute-start | bytes 6291464 | tf_op jit(solution)/shard_map/ppermute | solution.py:25
  249.5 140.0 %collective-permute-start.33 = (bf16[8,64,1024]{2,1,0:T(8,128)(2,1)}, bf16[8,64,1024]{2,1,0:T(8,128)(2,1)}, u32[]{:S(2)}, u32[]{:S(2)}) collective-permute-start(bf16[8,64,1024]{2,1,0:T(8,128)(2,1)} %collective-permute-done.32), channel_id=1, source_target_pairs={{1,0},{5,4},{9,8},{13,12},{17,16},{21,20},{25,24},{29,28}} | collective-permute-start | bytes 3145736 | tf_op jit(solution)/shard_map/ppermute | solution.py:75
  254.7 167.7 %collective-permute-start.35 = (bf16[8,64,1024]{2,1,0:T(8,128)(2,1)}, bf16[8,64,1024]{2,1,0:T(8,128)(2,1)}, u32[]{:S(2)}, u32[]{:S(2)}) collective-permute-start(bf16[8,64,1024]{2,1,0:T(8,128)(2,1)} %collective-permute-done.34), channel_id=1, source_target_pairs={{2,3},{6,7},{10,11},{14,15},{18,19},{22,23},{26,27},{30,31}} | collective-permute-start | bytes 3145736 | tf_op jit(solution)/shard_map/ppermute | solution.py:73
  334.7 51.4 %collective-permute-start.66 = (bf16[64,2048]{1,0:T(8,128)(2,1)S(1)}, bf16[64,2048]{1,0:T(8,128)(2,1)}, u32[]{:S(2)}, u32[]{:S(2)}) collective-permute-start(bf16[64,2048]{1,0:T(8,128)(2,1)S(1)} %get-tuple-element.60), channel_id=1, source_target_pairs={{0,1},{4,5},{8,9},{12,13},{16,17},{20,21},{24,25},{28,29}} | collective-permute-start | bytes 786440 | tf_op jit(solution)/shard_map/ppermute | solution.py:93
  336.0 203.4 %collective-permute-start.69 = (bf16[64,2048]{1,0:T(8,128)(2,1)}, bf16[64,2048]{1,0:T(8,128)(2,1)}, u32[]{:S(2)}, u32[]{:S(2)}) collective-permute-start(bf16[64,2048]{1,0:T(8,128)(2,1)} %get-tuple-element.61), channel_id=1, source_target_pairs={{3,2},{7,6},{11,10},{15,14},{19,18},{23,22},{27,26},{31,30}} | collective-permute-start | bytes 786440 | tf_op jit(solution)/shard_map/ppermute | solution.py:94
  384.7 159.1 %collective-permute-start.60 = (bf16[8,64,768]{2,1,0:T(8,128)(2,1)}, bf16[8,64,768]{2,1,0:T(8,128)(2,1)}, u32[]{:S(2)}, u32[]{:S(2)}) collective-permute-start(bf16[8,64,768]{2,1,0:T(8,128)(2,1)} %get-tuple-element.52), channel_id=1, source_target_pairs={{0,1},{4,5},{8,9},{12,13},{16,17},{20,21},{24,25},{28,29}} | collective-permute-start | bytes 2359304 | tf_op jit(solution)/shard_map/ppermute | solution.py:93
  386.1 159.0 %collective-permute-start.63 = (bf16[8,64,768]{2,1,0:T(8,128)(2,1)}, bf16[8,64,768]{2,1,0:T(8,128)(2,1)}, u32[]{:S(2)}, u32[]{:S(2)}) collective-permute-start(bf16[8,64,768]{2,1,0:T(8,128)(2,1)} %get-tuple-element.53), channel_id=1, source_target_pairs={{3,2},{7,6},{11,10},{15,14},{19,18},{23,22},{27,26},{31,30}} | collective-permute-start | bytes 2359304 | tf_op jit(solution)/shard_map/ppermute | solution.py:94
  389.5 150.8 %collective-permute-start.67 = (bf16[64,2048]{1,0:T(8,128)(2,1)}, bf16[64,2048]{1,0:T(8,128)(2,1)}, u32[]{:S(2)}, u32[]{:S(2)}) collective-permute-start(bf16[64,2048]{1,0:T(8,128)(2,1)} %fusion.59), channel_id=1, source_target_pairs={{0,1},{1,2},{4,5},{5,6},{8,9},{9,10},{12,13},{13,14},{16,17},{17,1... | collective-permute-start | bytes 786440 | tf_op jit(solution)/shard_map/ppermute | solution.py:93
  489.2 114.0 %collective-permute-start.78 = (bf16[256,2048]{1,0:T(8,128)(2,1)}, bf16[256,2048]{1,0:T(8,128)(2,1)}, u32[]{:S(2)}, u32[]{:S(2)}) collective-permute-start(bf16[256,2048]{1,0:T(8,128)(2,1)} %get-tuple-element.42), channel_id=1, source_target_pairs={{0,1},{4,5},{8,9},{12,13},{16,17},{20,21},{24,25},{28,29}} | collective-permute-start | bytes 3145736 | tf_op jit(solution)/shard_map/ppermute | solution.py:93
  539.4 69.1 %collective-permute-start.81 = (bf16[256,2048]{1,0:T(8,128)(2,1)}, bf16[256,2048]{1,0:T(8,128)(2,1)S(1)}, u32[]{:S(2)}, u32[]{:S(2)}) collective-permute-start(bf16[256,2048]{1,0:T(8,128)(2,1)} %get-tuple-element.43), channel_id=1, source_target_pairs={{3,2},{7,6},{11,10},{15,14},{19,18},{23,22},{27,26},{31,30}} | collective-permute-start | bytes 3145736 | tf_op jit(solution)/shard_map/ppermute | solution.py:94
  547.1 53.0 %collective-permute-start.61 = (bf16[8,64,768]{2,1,0:T(8,128)(2,1)S(1)}, bf16[8,64,768]{2,1,0:T(8,128)(2,1)S(1)}, u32[]{:S(2)}, u32[]{:S(2)}) collective-permute-start(bf16[8,64,768]{2,1,0:T(8,128)(2,1)S(1)} %get-tuple-element.50), channel_id=1, source_target_pairs={{0,1},{1,2},{4,5},{5,6},{8,9},{9,10},{12,13},{13,14},{16,17},{17,1... | collective-permute-start | bytes 2359304 | tf_op jit(solution)/shard_map/ppermute | solution.py:93
  556.4 44.9 %collective-permute-start.64 = (bf16[8,64,768]{2,1,0:T(8,128)(2,1)S(1)}, bf16[8,64,768]{2,1,0:T(8,128)(2,1)S(1)}, u32[]{:S(2)}, u32[]{:S(2)}) collective-permute-start(bf16[8,64,768]{2,1,0:T(8,128)(2,1)S(1)} %get-tuple-element.51), channel_id=1, source_target_pairs={{3,2},{2,1},{7,6},{6,5},{11,10},{10,9},{15,14},{14,13},{19,18},{18... | collective-permute-start | bytes 2359304 | tf_op jit(solution)/shard_map/ppermute | solution.py:94
  557.8 40.5 %collective-permute-start.71 = (bf16[64,2048]{1,0:T(8,128)(2,1)S(1)}, bf16[64,2048]{1,0:T(8,128)(2,1)S(1)}, u32[]{:S(2)}, u32[]{:S(2)}) collective-permute-start(bf16[64,2048]{1,0:T(8,128)(2,1)S(1)} %fusion.58), channel_id=1, source_target_pairs={{3,2},{2,1},{1,0},{7,6},{6,5},{5,4},{11,10},{10,9},{9,8},{15,14},{... | collective-permute-start | bytes 786440 | tf_op jit(solution)/shard_map/ppermute | solution.py:94
  598.3 53.6 %collective-permute-start.42 = (bf16[2,4,128,1024]{3,2,1,0:T(8,128)(2,1)S(1)}, bf16[2,4,128,1024]{3,2,1,0:T(8,128)(2,1)}, u32[]{:S(2)}, u32[]{:S(2)}) collective-permute-start(bf16[2,4,128,1024]{3,2,1,0:T(8,128)(2,1)S(1)} %get-tuple-element.38), channel_id=1, source_target_pairs={{0,4},{4,0},{8,12},{12,8},{16,20},{20,16},{24,28},{28,24},{1,5},{5... | collective-permute-start | bytes 6291464 | tf_op jit(solution)/shard_map/ppermute | solution.py:25
  600.2 53.4 %collective-permute-start.45 = (bf16[2,4,128,1024]{3,2,1,0:T(8,128)(2,1)S(1)}, bf16[2,4,128,1024]{3,2,1,0:T(8,128)(2,1)}, u32[]{:S(2)}, u32[]{:S(2)}) collective-permute-start(bf16[2,4,128,1024]{3,2,1,0:T(8,128)(2,1)S(1)} %get-tuple-element.39), channel_id=1, source_target_pairs={{0,4},{4,0},{8,12},{12,8},{16,20},{20,16},{24,28},{28,24},{1,5},{5... | collective-permute-start | bytes 6291464 | tf_op jit(solution)/shard_map/ppermute | solution.py:25
  601.3 26.1 %collective-permute-start.72 = (bf16[8,64,1024]{2,1,0:T(8,128)(2,1)S(1)}, bf16[8,64,1024]{2,1,0:T(8,128)(2,1)S(1)}, u32[]{:S(2)}, u32[]{:S(2)}) collective-permute-start(bf16[8,64,1024]{2,1,0:T(8,128)(2,1)S(1)} %get-tuple-element.46), channel_id=1, source_target_pairs={{0,1},{4,5},{8,9},{12,13},{16,17},{20,21},{24,25},{28,29}} | collective-permute-start | bytes 3145736 | tf_op jit(solution)/shard_map/ppermute | solution.py:93
  603.1 41.2 %collective-permute-start.62 = (bf16[8,64,768]{2,1,0:T(8,128)(2,1)S(1)}, bf16[8,64,768]{2,1,0:T(8,128)(2,1)S(1)}, u32[]{:S(2)}, u32[]{:S(2)}) collective-permute-start(bf16[8,64,768]{2,1,0:T(8,128)(2,1)S(1)} %get-tuple-element.48), channel_id=1, source_target_pairs={{0,1},{1,2},{2,3},{4,5},{5,6},{6,7},{8,9},{9,10},{10,11},{12,13},{... | collective-permute-start | bytes 2359304 | tf_op jit(solution)/shard_map/ppermute | solution.py:93
  608.5 40.1 %collective-permute-start.65 = (bf16[8,64,768]{2,1,0:T(8,128)(2,1)S(1)}, bf16[8,64,768]{2,1,0:T(8,128)(2,1)S(1)}, u32[]{:S(2)}, u32[]{:S(2)}) collective-permute-start(bf16[8,64,768]{2,1,0:T(8,128)(2,1)S(1)} %get-tuple-element.49), channel_id=1, source_target_pairs={{3,2},{2,1},{1,0},{7,6},{6,5},{5,4},{11,10},{10,9},{9,8},{15,14},{... | collective-permute-start | bytes 2359304 | tf_op jit(solution)/shard_map/ppermute | solution.py:94
  627.5 74.9 %collective-permute-start.48 = (bf16[2,4,128,1024]{3,2,1,0:T(8,128)(2,1)}, bf16[2,4,128,1024]{3,2,1,0:T(8,128)(2,1)}, u32[]{:S(2)}, u32[]{:S(2)}) collective-permute-start(bf16[2,4,128,1024]{3,2,1,0:T(8,128)(2,1)} %get-tuple-element.34), channel_id=1, source_target_pairs={{0,4},{4,0},{8,12},{12,8},{16,20},{20,16},{24,28},{28,24},{1,5},{5... | collective-permute-start | bytes 6291464 | tf_op jit(solution)/shard_map/ppermute | solution.py:25
  644.3 59.3 %collective-permute-start.51 = (bf16[2,4,128,1024]{3,2,1,0:T(8,128)(2,1)}, bf16[2,4,128,1024]{3,2,1,0:T(8,128)(2,1)}, u32[]{:S(2)}, u32[]{:S(2)}) collective-permute-start(bf16[2,4,128,1024]{3,2,1,0:T(8,128)(2,1)} %get-tuple-element.35), channel_id=1, source_target_pairs={{0,4},{4,0},{8,12},{12,8},{16,20},{20,16},{24,28},{28,24},{1,5},{5... | collective-permute-start | bytes 6291464 | tf_op jit(solution)/shard_map/ppermute | solution.py:25
  648.6 27.0 %collective-permute-start.79 = (bf16[256,2048]{1,0:T(8,128)(2,1)}, bf16[256,2048]{1,0:T(8,128)(2,1)}, u32[]{:S(2)}, u32[]{:S(2)}) collective-permute-start(bf16[256,2048]{1,0:T(8,128)(2,1)} %fusion.37), channel_id=1, source_target_pairs={{0,1},{1,2},{4,5},{5,6},{8,9},{9,10},{12,13},{13,14},{16,17},{17,1... | collective-permute-start | bytes 3145736 | tf_op jit(solution)/shard_map/ppermute | solution.py:93
  651.9 30.0 %collective-permute-start.75 = (bf16[8,64,1024]{2,1,0:T(8,128)(2,1)}, bf16[8,64,1024]{2,1,0:T(8,128)(2,1)}, u32[]{:S(2)}, u32[]{:S(2)}) collective-permute-start(bf16[8,64,1024]{2,1,0:T(8,128)(2,1)} %get-tuple-element.47), channel_id=1, source_target_pairs={{3,2},{7,6},{11,10},{15,14},{19,18},{23,22},{27,26},{31,30}} | collective-permute-start | bytes 3145736 | tf_op jit(solution)/shard_map/ppermute | solution.py:94
  653.5 44.5 %collective-permute-start.73 = (bf16[8,64,1024]{2,1,0:T(8,128)(2,1)}, bf16[8,64,1024]{2,1,0:T(8,128)(2,1)}, u32[]{:S(2)}, u32[]{:S(2)}) collective-permute-start(bf16[8,64,1024]{2,1,0:T(8,128)(2,1)} %fusion.42), channel_id=1, source_target_pairs={{0,1},{1,2},{4,5},{5,6},{8,9},{9,10},{12,13},{13,14},{16,17},{17,1... | collective-permute-start | bytes 3145736 | tf_op jit(solution)/shard_map/ppermute | solution.py:93
  656.7 59.7 %all-to-all-start.2 = ((bf16[8,64,768]{2,1,0:T(8,128)(2,1)}), bf16[8,64,768]{2,1,0:T(8,128)(2,1)S(1)}, u32[]{:S(2)}, u32[]{:S(2)}) async-start(bf16[8,64,768]{2,1,0:T(8,128)(2,1)} %fusion.51), calls=%async_computation.2 | async-start | bytes 1572864 | tf_op jit(solution)/shard_map/all_to_all | solution.py:404
  675.6 46.9 %collective-permute-start.43 = (bf16[2,2,1,128,1024]{4,3,0,2,1:T(8,128)(2,1)}, bf16[2,2,1,128,1024]{4,3,0,2,1:T(8,128)(2,1)}, u32[]{:S(2)}, u32[]{:S(2)}) collective-permute-start(bf16[2,2,1,128,1024]{4,3,0,2,1:T(8,128)(2,1)} %slice.211), channel_id=1, source_target_pairs={{0,8},{4,12},{8,0},{12,4},{16,24},{20,28},{24,16},{28,20},{1,9},{5... | collective-permute-start | bytes 3145736 | tf_op jit(solution)/shard_map/ppermute | solution.py:25
  681.9 129.8 %collective-permute-start.80 = (bf16[256,2048]{1,0:T(8,128)(2,1)}, bf16[256,2048]{1,0:T(8,128)(2,1)}, u32[]{:S(2)}, u32[]{:S(2)}) collective-permute-start(bf16[256,2048]{1,0:T(8,128)(2,1)} %get-tuple-element.40), channel_id=1, source_target_pairs={{0,1},{1,2},{2,3},{4,5},{5,6},{6,7},{8,9},{9,10},{10,11},{12,13},{... | collective-permute-start | bytes 3145736 | tf_op jit(solution)/shard_map/ppermute | solution.py:93
  698.0 27.7 %collective-permute-start.46 = (bf16[2,1,2,128,1024]{4,3,0,2,1:T(8,128)(2,1)}, bf16[2,1,2,128,1024]{4,3,0,2,1:T(8,128)(2,1)}, u32[]{:S(2)}, u32[]{:S(2)}) collective-permute-start(bf16[2,1,2,128,1024]{4,3,0,2,1:T(8,128)(2,1)} %slice.217), channel_id=1, source_target_pairs={{0,16},{4,20},{8,24},{12,28},{16,0},{20,4},{24,8},{28,12},{1,17},{... | collective-permute-start | bytes 3145736 | tf_op jit(solution)/shard_map/ppermute | solution.py:25
  702.3 26.6 %collective-permute-start.82 = (bf16[256,2048]{1,0:T(8,128)(2,1)}, bf16[256,2048]{1,0:T(8,128)(2,1)}, u32[]{:S(2)}, u32[]{:S(2)}) collective-permute-start(bf16[256,2048]{1,0:T(8,128)(2,1)} %get-tuple-element.41), channel_id=1, source_target_pairs={{3,2},{2,1},{7,6},{6,5},{11,10},{10,9},{15,14},{14,13},{19,18},{18... | collective-permute-start | bytes 3145736 | tf_op jit(solution)/shard_map/ppermute | solution.py:94
  703.6 89.8 %collective-permute-start.74 = (bf16[8,64,1024]{2,1,0:T(8,128)(2,1)}, bf16[8,64,1024]{2,1,0:T(8,128)(2,1)}, u32[]{:S(2)}, u32[]{:S(2)}) collective-permute-start(bf16[8,64,1024]{2,1,0:T(8,128)(2,1)} %get-tuple-element.44), channel_id=1, source_target_pairs={{0,1},{1,2},{2,3},{4,5},{5,6},{6,7},{8,9},{9,10},{10,11},{12,13},{... | collective-permute-start | bytes 3145736 | tf_op jit(solution)/shard_map/ppermute | solution.py:93
  722.4 22.7 %collective-permute-start.49 = (bf16[2,2,1,128,1024]{4,3,0,2,1:T(8,128)(2,1)S(1)}, bf16[2,2,1,128,1024]{4,3,0,2,1:T(8,128)(2,1)S(1)}, u32[]{:S(2)}, u32[]{:S(2)}) collective-permute-start(bf16[2,2,1,128,1024]{4,3,0,2,1:T(8,128)(2,1)S(1)} %copy-done.44), channel_id=1, source_target_pairs={{0,8},{4,12},{8,0},{12,4},{16,24},{20,28},{24,16},{28,20},{1,9},{5... | collective-permute-start | bytes 3145736 | tf_op jit(solution)/shard_map/ppermute | solution.py:25
  725.7 22.4 %collective-permute-start.52 = (bf16[2,1,2,128,1024]{4,3,0,2,1:T(8,128)(2,1)S(1)}, bf16[2,1,2,128,1024]{4,3,0,2,1:T(8,128)(2,1)S(1)}, u32[]{:S(2)}, u32[]{:S(2)}) collective-permute-start(bf16[2,1,2,128,1024]{4,3,0,2,1:T(8,128)(2,1)S(1)} %copy-done.43), channel_id=1, source_target_pairs={{0,16},{4,20},{8,24},{12,28},{16,0},{20,4},{24,8},{28,12},{1,17},{... | collective-permute-start | bytes 3145736 | tf_op jit(solution)/shard_map/ppermute | solution.py:25
  728.9 24.1 %collective-permute-start.76 = (bf16[8,64,1024]{2,1,0:T(8,128)(2,1)S(1)}, bf16[8,64,1024]{2,1,0:T(8,128)(2,1)S(1)}, u32[]{:S(2)}, u32[]{:S(2)}) collective-permute-start(bf16[8,64,1024]{2,1,0:T(8,128)(2,1)S(1)} %copy-done.47), channel_id=1, source_target_pairs={{3,2},{2,1},{7,6},{6,5},{11,10},{10,9},{15,14},{14,13},{19,18},{18... | collective-permute-start | bytes 3145736 | tf_op jit(solution)/shard_map/ppermute | solution.py:94
  745.1 66.6 %collective-permute-start.83 = (bf16[256,2048]{1,0:T(8,128)(2,1)}, bf16[256,2048]{1,0:T(8,128)(2,1)}, u32[]{:S(2)}, u32[]{:S(2)}) collective-permute-start(bf16[256,2048]{1,0:T(8,128)(2,1)} %fusion.36), channel_id=1, source_target_pairs={{3,2},{2,1},{1,0},{7,6},{6,5},{5,4},{11,10},{10,9},{9,8},{15,14},{... | collective-permute-start | bytes 3145736 | tf_op jit(solution)/shard_map/ppermute | solution.py:94
  768.5 28.1 %collective-permute-start.77 = (bf16[8,64,1024]{2,1,0:T(8,128)(2,1)}, bf16[8,64,1024]{2,1,0:T(8,128)(2,1)S(1)}, u32[]{:S(2)}, u32[]{:S(2)}) collective-permute-start(bf16[8,64,1024]{2,1,0:T(8,128)(2,1)} %fusion.41), channel_id=1, source_target_pairs={{3,2},{2,1},{1,0},{7,6},{6,5},{5,4},{11,10},{10,9},{9,8},{15,14},{... | collective-permute-start | bytes 3145736 | tf_op jit(solution)/shard_map/ppermute | solution.py:94
  801.3 21.4 %all-to-all-start.3 = ((bf16[8,64,1024]{2,1,0:T(8,128)(2,1)}), bf16[8,64,1024]{2,1,0:T(8,128)(2,1)S(1)}, u32[]{:S(2)}, u32[]{:S(2)}) async-start(bf16[8,64,1024]{2,1,0:T(8,128)(2,1)} %fusion.45), calls=%async_computation.3 | async-start | bytes 2097152 | tf_op jit(solution)/shard_map/all_to_all | solution.py:404
  (98 other events, 2042.4 us)

commit v2 on v1

v2 whole, which is shorter than its diff:
```python
import functools
import math

import jax
import jax.numpy as jnp
from jax import lax
from jax.experimental import pallas as pl
from jax.experimental.pallas import tpu as pltpu
from jax.sharding import PartitionSpec as P

HEADS = 32
HEAD_DIM = 64
ROT = 32
IMG = 256
PIECES = 2
EPSILON = 1e-05
BF = jnp.bfloat16
F32 = jnp.float32
SCALE = 1.0 / math.sqrt(HEAD_DIM)
LANES = 2 * HEAD_DIM


def swap(value, bit):
    size = lax.axis_size("seq")
    return lax.ppermute(value, "seq", [(i, i ^ bit) for i in range(size)])


def scatter_seq(terms):
    size = lax.axis_size("seq")
    me = lax.axis_index("seq")
    count = size.bit_length() - 1
    micro, _, length, width = terms.shape
    half = width // 2
    bits = list(range(1, count))

    def exchange(held, bit, axis):
        held = held.astype(BF)
        mine = (me >> bit) & 1
        away = lax.dynamic_index_in_dim(held, 1 - mine, axis, keepdims=False)
        kept = lax.dynamic_index_in_dim(held, mine, axis, keepdims=False)
        return kept.astype(F32) + swap(away, 1 << bit).astype(F32)

    sums = []
    for cols, order in ((slice(0, half), bits), (slice(half, width), bits[::-1])):
        held = terms[..., cols].reshape((micro,) + (2,) * count + (length, half))
        left = list(range(count))[::-1]
        for bit in [0] + order:
            held = exchange(held, bit, 1 + left.index(bit))
            left.remove(bit)
        sums.append(held)
    return jnp.concatenate(sums, axis=-1)


def by_index(blocks):
    me = lax.axis_index("seq")
    shape = blocks.shape
    for bit in range(shape[0].bit_length() - 1):
        split = blocks.reshape((-1, 2, 1 << bit) + shape[1:])
        blocks = jnp.where((me >> bit) & 1 == 1, split[:, ::-1], split).reshape(shape)
    return blocks


def scatter_small(terms):
    size, depth = lax.axis_size("seq"), lax.axis_size("fsdp")
    held = by_index(terms)
    for bit in reversed(range(size.bit_length() - 1)):
        n = held.shape[0] // 2
        held = held[:n] + swap(held[n:], 1 << bit)
    at = lax.axis_index("fsdp")
    held = held[0]
    total = lax.dynamic_index_in_dim(held, at, 0, keepdims=False)
    for step in range(1, depth):
        away = lax.dynamic_index_in_dim(held, (at + step) % depth, 0, keepdims=False)
        total = total + lax.ppermute(
            away, "fsdp", [(i, (i + step) % depth) for i in range(depth)]
        )
    return total


def attention_kernel(
    blocks,
    length,
    starts_ref,
    cos_ref,
    sin_ref,
    q_ref,
    k_ref,
    v_ref,
    do_ref,
    mixed_ref,
    dq_ref,
    dk_ref,
    dv_ref,
    q_s,
    k_s,
    v_s,
    do_s,
    dk_s,
    dv_s,
    bias_s,
):
    micro = pl.program_id(0)
    total = blocks * length
    tile = 256
    lane = lax.broadcasted_iota(jnp.int32, (1, LANES), 1)
    low_lane = (lane % HEAD_DIM) < (ROT // 2)

    def turn(value, cosine, sine):
        other = jnp.where(
            low_lane,
            pltpu.roll(value, LANES - ROT // 2, 1),
            pltpu.roll(value, ROT // 2, 1),
        )
        return value * cosine + other * sine

    for block in range(blocks):
        source = block
        at = slice(block * length, (block + 1) * length)
        cosine, sine = cos_ref[at, :], sin_ref[at, :]
        q_s[at, :] = (turn(q_ref[0, source], cosine, sine)).astype(BF) * jnp.asarray(SCALE, BF)
        k_s[at, :] = turn(k_ref[0, source], cosine, sine).astype(BF)
        v_s[at, :] = v_ref[0, source].astype(BF)
        do_s[at, :] = do_ref[0, source]
    dk_s[...] = jnp.zeros_like(dk_s)
    dv_s[...] = jnp.zeros_like(dv_s)

    def label(positions):
        found = jnp.full(positions.shape, -1, jnp.int32)
        for piece in range(PIECES):
            start = starts_ref[micro, piece]
            found = jnp.where((positions >= start) & (positions < start + IMG), piece, found)
        return found

    for first in range(0, total, tile):
        last = min(total, first + tile + IMG)
        qpos = first + lax.broadcasted_iota(jnp.int32, (tile, 1), 0)
        kpos = first + lax.broadcasted_iota(jnp.int32, (1, last - first), 1)
        qlab, klab = label(qpos), label(kpos)
        allowed = (kpos <= qpos) | ((qlab == klab) & (qlab >= 0))
        bias_s[:, : last - first] = jnp.where(allowed, 0.0, -1e30)
        rows = slice(first, first + tile)
        keys = k_s[:last, :]
        values = v_s[:last, :]
        mixed = jnp.zeros((tile, LANES), F32)
        dq = jnp.zeros((tile, LANES), F32)
        for head in range(LANES // HEAD_DIM):
            mine = (lane // HEAD_DIM) == head
            q = jnp.where(mine, q_s[rows, :], 0)
            do = jnp.where(mine, do_s[rows, :], 0)
            dims = (((1,), (1,)), ((), ()))
            s = lax.dot_general(q, keys, dims, preferred_element_type=F32)
            if first:
                s = jnp.concatenate(
                    [s[:, :first], s[:, first:] + bias_s[:, : last - first]], axis=1
                )
            else:
                s = s + bias_s[:, : last - first]
            p = jnp.exp(s - jnp.max(s, axis=1, keepdims=True))
            p = p * (1.0 / jnp.sum(p, axis=1, keepdims=True))
            probs = p.astype(BF)
            att = jnp.dot(probs, values, preferred_element_type=F32)
            mixed = jnp.where(mine, att, mixed)
            dp = lax.dot_general(do, values, dims, preferred_element_type=F32)
            delta = jnp.sum(p * dp, axis=1, keepdims=True)
            ds = (p * (dp - delta)).astype(BF)
            dq = jnp.where(mine, jnp.dot(ds, keys, preferred_element_type=F32), dq)
            over = (((0,), (0,)), ((), ()))
            dk_s[:last, :] += lax.dot_general(ds, q, over, preferred_element_type=F32)
            dv_s[:last, :] += lax.dot_general(probs, do, over, preferred_element_type=F32)
        dq = dq * SCALE
        for part in range(tile // length):
            block = first // length + part
            here = slice(part * length, (part + 1) * length)
            at = slice(block * length, (block + 1) * length)
            mixed_ref[0, block] = mixed[here].astype(BF)
            dq_ref[0, block] = turn(dq[here], cos_ref[at, :], -sin_ref[at, :]).astype(BF)
    for block in range(blocks):
        at = slice(block * length, (block + 1) * length)
        dk_ref[0, block] = turn(dk_s[at, :], cos_ref[at, :], -sin_ref[at, :]).astype(BF)
        dv_ref[0, block] = dv_s[at, :].astype(BF)


def attention(starts, projected, mixed_grad):
    micro, blocks, length, cols = mixed_grad.shape
    total = blocks * length
    groups = cols // LANES
    half = ROT // 2
    frequency = 10000.0 ** (-2.0 * jnp.arange(half, dtype=F32) / ROT)
    angles = jnp.arange(total, dtype=jnp.int32).astype(F32)[:, None] * frequency[None, :]
    cosine, sine = jnp.cos(angles), jnp.sin(angles)
    ones = jnp.ones((total, HEAD_DIM - ROT), F32)
    cosine = jnp.concatenate([cosine, cosine, ones] * 2, axis=1)
    sine = jnp.concatenate([-sine, sine, 0 * ones] * 2, axis=1)

    def spec(offset):
        return pl.BlockSpec(
            (1, blocks, length, LANES), lambda m, g, offset=offset: (m, 0, 0, offset * groups + g)
        )

    table = pl.BlockSpec((total, LANES), lambda m, g: (0, 0))
    shape = jax.ShapeDtypeStruct(mixed_grad.shape, BF)
    return pl.pallas_call(
        functools.partial(attention_kernel, blocks, length),
        grid=(micro, groups),
        in_specs=[
            pl.BlockSpec(memory_space=pltpu.SMEM),
            table,
            table,
            spec(0),
            spec(1),
            spec(2),
            spec(0),
        ],
        out_specs=[spec(0)] * 4,
        out_shape=[shape] * 4,
        scratch_shapes=[pltpu.VMEM((total, LANES), BF)] * 4
        + [pltpu.VMEM((total, LANES), F32)] * 2
        + [pltpu.VMEM((256, 512), F32)],
        compiler_params=pltpu.CompilerParams(vmem_limit_bytes=48 * 1024 * 1024),
        cost_estimate=pl.CostEstimate(
            flops=micro * groups * 40 * total * total * HEAD_DIM,
            bytes_accessed=micro * groups * total * LANES * 22,
            transcendentals=micro * groups * 2 * total * total,
        ),
    )(starts, cosine, sine, projected, projected, projected, mixed_grad)


MESH = pl.DeviceIdType.MESH


def load_kernel(
    dims,
    tokens_ref,
    up_ref,
    one_ref,
    two_ref,
    qkv_ref,
    out_ref,
    vec_ref,
    normed_ref,
    all_up_ref,
    my_one_ref,
    two_right_ref,
    two_left_ref,
    attn_ref,
    full_ref,
    gathered,
    vec_seq,
    vec_sum,
    vec_all,
    local_sem,
    vec_send,
    vec_recv,
    a2a_send,
    a2a_recv,
    line_send,
    line_recv,
    row_send,
    row_recv,
):
    size, depth, micro, length, width, units, cols = dims
    me, at = lax.axis_index("seq"), lax.axis_index("fsdp")
    count = size.bit_length() - 1
    half = width // 2

    def seq(step):
        return {"seq": me ^ step}

    def line(step):
        return {"fsdp": lax.rem(at + step, depth)}

    barrier = pltpu.get_barrier_semaphore()
    for step in range(1, size):
        pl.semaphore_signal(barrier, inc=1, device_id=seq(step), device_id_type=MESH)
    for step in range(1, depth):
        pl.semaphore_signal(barrier, inc=1, device_id=line(step), device_id_type=MESH)
    pl.semaphore_wait(barrier, size + depth - 2)

    def remote(src, dst, send, recv, device):
        return pltpu.make_async_remote_copy(
            src_ref=src,
            dst_ref=dst,
            send_sem=send,
            recv_sem=recv,
            device_id=device,
            device_id_type=MESH,
        )

    def vec_seq_copy(step):
        return remote(
            vec_ref, vec_seq.at[step], vec_send.at[step], vec_recv.at[step], seq(step)
        )

    def vec_line_copy(step):
        number = size + step
        return remote(
            vec_sum, vec_all.at[step], vec_send.at[number], vec_recv.at[number], line(step)
        )

    def one_copy(step):
        peer = me ^ step
        return remote(
            one_ref.at[:, pl.ds(pl.multiple_of(peer * units, 128), units)],
            my_one_ref.at[me, at],
            a2a_send.at[step],
            a2a_recv.at[step],
            seq(step),
        )

    def qkv_copy(step, part):
        peer = me ^ step
        number = size * (1 + part) + step
        return remote(
            qkv_ref.at[:, pl.ds(pl.multiple_of(part * width + peer * cols, 128), cols)],
            attn_ref.at[me, :, pl.ds(part * cols, cols)],
            a2a_send.at[number],
            a2a_recv.at[number],
            seq(step),
        )

    local = [
        pltpu.make_async_copy(
            one_ref.at[:, pl.ds(pl.multiple_of(me * units, 128), units)],
            my_one_ref.at[me, at],
            local_sem.at[0],
        ),
        pltpu.make_async_copy(
            tokens_ref,
            gathered.at[:, me],
            local_sem.at[1],
        ),
        pltpu.make_async_copy(
            up_ref,
            all_up_ref.at[:, me],
            local_sem.at[2],
        ),
    ]
    for part in range(3):
        local.append(
            pltpu.make_async_copy(
                qkv_ref.at[:, pl.ds(pl.multiple_of(part * width + me * cols, 128), cols)],
                attn_ref.at[me, :, pl.ds(part * cols, cols)],
                local_sem.at[3 + part],
            )
        )
    for peer in range(size):
        local.append(
            pltpu.make_async_copy(
                out_ref.at[:, pl.ds(peer * cols, cols)],
                attn_ref.at[peer, :, pl.ds(3 * cols, cols)],
                local_sem.at[6 + peer],
            )
        )

    def one_line(step, way):
        origin = jnp.clip(at - way * (step - 1), 0, depth - 1)
        number = 2 * step + (way > 0)
        piece = my_one_ref.at[:, origin]
        ok = (at + way >= 0) & (at + way < depth)
        ok = ok & (at - way * (step - 1) >= 0) & (at - way * (step - 1) < depth)
        return ok, remote(
            piece,
            piece,
            line_send.at[number],
            line_recv.at[number],
            {"fsdp": jnp.clip(at + way, 0, depth - 1)},
        )

    def one_arrives(step, way):
        ok = (at - way * step >= 0) & (at - way * step < depth)
        return ok, one_line(step, way)[1]

    def two_line(way):
        ok = (at + way >= 0) & (at + way < depth)
        number = way > 0
        return ok, remote(
            two_ref,
            two_right_ref if way > 0 else two_left_ref,
            line_send.at[int(number)],
            line_recv.at[int(number)],
            {"fsdp": jnp.clip(at + way, 0, depth - 1)},
        )

    def two_arrives(way):
        return (at - way >= 0) & (at - way < depth), two_line(way)[1]

    def start(pair):
        ok, copy = pair

        @pl.when(ok)
        def _():
            copy.start()

    def wait_recv(pair):
        ok, copy = pair

        @pl.when(ok)
        def _():
            copy.wait_recv()

    def wait_send(pair):
        ok, copy = pair

        @pl.when(ok)
        def _():
            copy.wait_send()

    sources = (tokens_ref, up_ref)
    targets = (gathered, all_up_ref)
    orders = (list(range(1, count)), list(range(1, count))[::-1])

    def row_copy(which, part, mask, bit):
        columns = slice(part * half, (part + 1) * half)
        block = me ^ mask
        if mask == 0:
            src = sources[which].at[:, :, columns]
        else:
            src = targets[which].at[:, block, :, columns]
        number = (which * 2 + part) * size + (mask | (1 << bit))
        return remote(
            src,
            targets[which].at[:, block, :, columns],
            row_send.at[number],
            row_recv.at[number],
            seq(1 << bit),
        )

    def row_stage(which, part, stage):
        order = orders[part]
        masks = [0]
        for bit in order[:stage]:
            masks = masks + [mask | (1 << bit) for mask in masks]
        return [row_copy(which, part, mask, order[stage]) for mask in masks]

    def row_cores(which, part, stage):
        order = orders[part]
        masks = [0]
        new = [0]
        for bit in order[: stage + 1]:
            new = [mask | (1 << bit) for mask in masks]
            masks = masks + new
        return [row_copy(which, part, mask, 0) for mask in new]

    def both_parts(function, which, stage):
        return function(which, 0, stage) + function(which, 1, stage)

    def issue(copies):
        for copy in copies:
            copy.start()

    def arrive(copies):
        for copy in copies:
            copy.wait_recv()

    issue(vec_seq_copy(step) for step in range(1, size))
    issue(one_copy(step) for step in range(1, size))
    for way in (1, -1):
        start(two_line(way))
    issue(local)
    vec_seq[0] = vec_ref[...]
    arrive(vec_seq_copy(step) for step in range(1, size))
    summed = vec_seq[0].astype(F32)
    for step in range(1, size):
        summed = summed + vec_seq[step].astype(F32)
    vec_sum[...] = summed.astype(BF)
    issue(vec_line_copy(step) for step in range(1, depth))
    for which in range(2):
        issue(both_parts(row_cores, which, -1))
    arrive(one_copy(step) for step in range(1, size))
    local[0].wait()
    for way in (1, -1):
        start(one_line(1, way))
    for which in range(2):
        issue(both_parts(row_stage, which, 0))
    arrive(vec_line_copy(step) for step in range(1, depth))
    for step in range(1, depth):
        summed = summed + vec_all[step].astype(F32)
    full_ref[...] = summed

    line_step = 1
    for stage in range(count - 1):
        for which in range(2):
            arrive(both_parts(row_stage, which, stage))
            issue(both_parts(row_cores, which, stage))
            if stage + 1 < count - 1:
                issue(both_parts(row_stage, which, stage + 1))
        if line_step < depth - 1:
            for way in (1, -1):
                wait_recv(one_arrives(line_step, way))
                start(one_line(line_step + 1, way))
            line_step += 1
    for part in range(3):
        issue(qkv_copy(step, part) for step in range(1, size))
    while line_step < depth - 1:
        for way in (1, -1):
            wait_recv(one_arrives(line_step, way))
            start(one_line(line_step + 1, way))
        line_step += 1

    local[1].wait()
    for stage in range(-1, count - 1):
        arrive(both_parts(row_cores, 0, stage))
    gain = full_ref[0:1, :]
    shift = full_ref[1:2, :]

    @pl.loop(0, micro * size)
    def _(index):
        m, block = index // size, lax.rem(index, size)
        x = gathered[m, block].astype(F32)
        center = x - jnp.mean(x, axis=-1, keepdims=True)
        spread = jnp.mean(center * center, axis=-1, keepdims=True)
        y = center * lax.rsqrt(spread + EPSILON) * gain + shift
        normed_ref[m, block] = y.astype(BF)

    for copy in local[2:]:
        copy.wait()
    for stage in range(-1, count - 1):
        arrive(both_parts(row_cores, 1, stage))
    for part in range(3):
        arrive(qkv_copy(step, part) for step in range(1, size))
    for way in (1, -1):
        wait_recv(two_arrives(way))
        wait_recv(one_arrives(depth - 1, way))

    for step in range(1, size):
        vec_seq_copy(step).wait_send()
        one_copy(step).wait_send()
        for part in range(3):
            qkv_copy(step, part).wait_send()
    for step in range(1, depth):
        vec_line_copy(step).wait_send()
        for way in (1, -1):
            wait_send(one_line(step, way))
    for way in (1, -1):
        wait_send(two_line(way))
    for which in range(2):
        for stage in range(-1, count - 1):
            for copy in both_parts(row_cores, which, stage):
                copy.wait_send()
            if stage >= 0:
                for copy in both_parts(row_stage, which, stage):
                    copy.wait_send()


def load_all(tokens, upstream, w_fc1, w_fc2, w_qkv, w_out, vectors):
    size, depth = lax.axis_size("seq"), lax.axis_size("fsdp")
    micro, length, width = tokens.shape
    rows, units, cols = w_fc1.shape[0], w_fc1.shape[1] // size, width // size
    dims = (size, depth, micro, length, width, units, cols)
    hbm = pl.BlockSpec(memory_space=pl.ANY)
    vmem = pl.BlockSpec(memory_space=pltpu.VMEM)
    gathered = (micro, size, length, width)
    dma = pltpu.SemaphoreType.DMA
    return pl.pallas_call(
        functools.partial(load_kernel, dims),
        in_specs=[hbm] * 6 + [vmem],
        out_specs=[vmem] + [hbm] * 5 + [vmem],
        out_shape=[
            jax.ShapeDtypeStruct(gathered, BF),
            jax.ShapeDtypeStruct(gathered, BF),
            jax.ShapeDtypeStruct((size, depth, rows, units), BF),
            jax.ShapeDtypeStruct(w_fc2.shape, BF),
            jax.ShapeDtypeStruct(w_fc2.shape, BF),
            jax.ShapeDtypeStruct((size, rows, 4 * cols), BF),
            jax.ShapeDtypeStruct(vectors.shape, F32),
        ],
        scratch_shapes=[
            pltpu.VMEM(gathered, BF),
            pltpu.VMEM((size,) + vectors.shape, BF),
            pltpu.VMEM(vectors.shape, BF),
            pltpu.VMEM((depth,) + vectors.shape, BF),
            dma((6 + size,)),
            dma((size + depth,)),
            dma((size + depth,)),
            dma((4 * size,)),
            dma((4 * size,)),
            dma((2 * depth + 2,)),
            dma((2 * depth + 2,)),
            dma((4 * size,)),
            dma((4 * size,)),
        ],
        compiler_params=pltpu.CompilerParams(
            collective_id=1, has_side_effects=True, vmem_limit_bytes=40 * 1024 * 1024
        ),
        cost_estimate=pl.CostEstimate(
            flops=1000, bytes_accessed=300 * 1000 * 1000, transcendentals=0
        ),
    )(tokens, upstream, w_fc1, w_fc2, w_qkv, w_out, vectors)


def gelu_tanh(values):
    return jax.nn.gelu(values, approximate=True)


def layer_norm(values, gain, shift):
    center = values - jnp.mean(values, axis=-1, keepdims=True)
    spread = jnp.mean(center * center, axis=-1, keepdims=True)
    return center * lax.rsqrt(spread + EPSILON) * gain + shift


def fence(*values):
    return lax.optimization_barrier(values)


def line_right(value, senders):
    return lax.ppermute(value, "fsdp", [(i, i + 1) for i in senders])


def line_left(value, senders):
    last = lax.axis_size("fsdp") - 1
    return lax.ppermute(value, "fsdp", [(last - i, last - i - 1) for i in senders])


class Gather:
    def __init__(self, mine):
        self.right, self.left = [mine], [mine]

    def step(self):
        size = lax.axis_size("fsdp")
        number = len(self.right)
        if number < size:
            self.right.append(line_right(self.right[-1], range(number - 1, size - 1)))
            self.left.append(line_left(self.left[-1], range(number - 1, size - 1)))

    def fence(self, *others):
        (self.right[-1], self.left[-1]), *others = fence((self.right[-1], self.left[-1]), *others)
        return others

    def rest(self):
        while len(self.right) < lax.axis_size("fsdp"):
            self.step()

    def pieces(self):
        size = lax.axis_size("fsdp")
        at = lax.axis_index("fsdp")
        found = [(self.right[0], at)]
        for step in range(1, size):
            piece = jnp.where(at >= step, self.right[step], self.left[size - step])
            found.append((piece, lax.rem(at - step + size, size)))
        return found


class Scatter:
    def __init__(self, chunk):
        self.chunk = chunk
        self.number = 0
        self.right = self.left = None

    def step(self):
        size = lax.axis_size("fsdp")
        at = lax.axis_index("fsdp")
        if self.number == size - 1:
            return
        self.number += 1
        going = self.chunk(jnp.minimum(size - self.number + at, size - 1))
        coming = self.chunk(jnp.maximum(self.number - size + at, 0))
        if self.number > 1:
            going = (going.astype(F32) + self.right.astype(F32)).astype(BF)
            coming = (coming.astype(F32) + self.left.astype(F32)).astype(BF)
        self.right = line_right(going, range(self.number))
        self.left = line_left(coming, range(self.number))

    def rest(self):
        while self.number < lax.axis_size("fsdp") - 1:
            self.step()

    def fence(self, *others):
        (self.right, self.left), *others = fence((self.right, self.left), *others)
        return others

    def total(self):
        mine = self.chunk(lax.axis_index("fsdp")).astype(F32)
        return mine + self.right.astype(F32) + self.left.astype(F32)


def per_device(
    tokens,
    ln_gain,
    ln_bias,
    w_qkv,
    b_qkv,
    w_out,
    b_out,
    w_fc1,
    b_fc1,
    w_fc2,
    b_fc2,
    piece_starts,
    cotangent,
):
    size, depth = lax.axis_size("seq"), lax.axis_size("fsdp")
    me = lax.axis_index("seq")
    micro, _, length, width = tokens.shape
    rows = width // (size * depth)
    hidden_rows = w_fc2.shape[0]
    cols = width // size
    units = hidden_rows * depth
    count = micro * size * length
    tokens = tokens[:, 0]
    upstream = cotangent[:, 0]

    def contract_last(left, right):
        return lax.dot_general(left, right, (((1,), (1,)), ((), ())), preferred_element_type=F32)

    def contract_first(left, right):
        return lax.dot_general(left, right, (((0,), (0,)), ((), ())), preferred_element_type=F32)

    def place_columns(pieces):
        out = jnp.zeros((size, depth) + pieces[0][0].shape[1:], BF)
        for piece, origin in pieces:
            out = lax.dynamic_update_slice_in_dim(out, piece[:, None], origin, 1)
        return out

    def place_rows(pieces):
        out = jnp.zeros((depth,) + pieces[0][0].shape, BF)
        for piece, origin in pieces:
            out = lax.dynamic_update_slice_in_dim(out, piece[None], origin, 0)
        return out

    index = me * depth + lax.axis_index("fsdp")
    packed = []
    for vector in (ln_gain, ln_bias, b_qkv, b_out, b_fc1, b_fc2):
        extent = vector.shape[0]
        flat = jnp.zeros((extent * size * depth,), BF)
        flat = lax.dynamic_update_slice(flat, vector, (index * extent,))
        packed.append(flat.reshape(-1, width))
    packed = jnp.concatenate(packed, axis=0)
    packed = jnp.pad(packed, ((0, -packed.shape[0] % 16), (0, 0)))
    normed, up, my_one, two_right, two_left, attn_cols, full = load_all(
        tokens, upstream, w_fc1, w_fc2, w_qkv, w_out, packed
    )
    normed = normed.reshape(count, width)
    up = up.reshape(count, width)
    my_one = my_one.reshape(width, units)
    two = Gather(w_fc2)
    two.right.append(two_right)
    two.left.append(two_left)
    gain, shift, bias_out = full[0], full[1], full[5]
    bias_qkv = lax.dynamic_slice_in_dim(full[2:5], me * cols, cols, 1).reshape(-1)
    ratio = size * units // width
    bias_one = lax.dynamic_slice_in_dim(full[6 : 6 + ratio].reshape(-1), me * units, units, 0)
    bias_two = full[6 + ratio]
    two.step()
    pre = jnp.dot(normed, my_one, preferred_element_type=F32) + bias_one
    hidden, back = jax.vjp(gelu_tanh, pre)
    hidden = hidden.astype(BF)
    grad_two = contract_first(hidden, up).astype(BF).reshape(depth, hidden_rows, width)
    hidden, grad_two = two.fence(hidden, grad_two)
    two.step()
    sum_two = Scatter(lambda o: lax.dynamic_index_in_dim(grad_two, o, 0, keepdims=False))
    sum_two.step()
    (two.right, two.left), (sum_two.right, sum_two.left), attn_cols = fence(
        (two.right, two.left), (sum_two.right, sum_two.left), attn_cols
    )
    attn = Gather(attn_cols)
    attn.step()
    two.rest()
    my_two = place_rows(two.pieces()).reshape(units, width)
    pre_grad = back(contract_last(up, my_two))[0].astype(BF)
    grad_one = contract_first(normed, pre_grad).astype(BF).reshape(size, depth, rows, units)
    pre_grad, grad_one = attn.fence(pre_grad, grad_one)
    attn.step()
    sum_one = Scatter(lambda o: lax.dynamic_index_in_dim(grad_one, o, 1, keepdims=False))
    sum_one.step()
    (sum_one.right, sum_one.left), (sum_two.right, sum_two.left) = attn.fence(
        (sum_one.right, sum_one.left), (sum_two.right, sum_two.left)
    )
    attn.step()
    sum_two.step()
    (sum_two.right, sum_two.left), normed, up = attn.fence(
        (sum_two.right, sum_two.left), normed, up
    )
    sum_two.step()
    attn.rest()
    pieces = attn.pieces()
    my_qkv = place_columns([(p[..., : 3 * cols], o) for p, o in pieces]).reshape(width, 3 * cols)
    my_out = place_rows([(p[..., 3 * cols :].transpose(1, 0, 2), o) for p, o in pieces])
    my_out = my_out.reshape(cols, width)
    projected = jnp.dot(normed, my_qkv, preferred_element_type=F32) + bias_qkv
    projected = projected.reshape(micro, size, length, 3 * cols)
    mixed_grad = contract_last(up, my_out).astype(BF).reshape(micro, size, length, cols)
    starts = piece_starts[:, 0]
    parts = [attention(starts[:1], projected[:1], mixed_grad[:1])]
    (sum_one.right, sum_one.left), (projected, mixed_grad), parts = sum_two.fence(
        (sum_one.right, sum_one.left), (projected, mixed_grad), parts
    )
    sum_one.step()
    for m in range(1, micro):
        parts.append(attention(starts[m:][:1], projected[m:][:1], mixed_grad[m:][:1]))
    mixed = jnp.concatenate([part[0] for part in parts]).reshape(count, cols)
    projected_grad = jnp.concatenate(
        [jnp.concatenate(part[1:], axis=-1) for part in parts]
    ).reshape(count, 3 * cols)
    projected_grad, mixed = sum_one.fence(projected_grad, mixed)
    sum_one.step()
    grad_qkv = contract_first(normed, projected_grad).astype(BF).reshape(size, depth, rows, 3 * cols)
    grad_out = contract_first(mixed, up).astype(BF).reshape(depth, rows, size, cols)
    grad_qkv, grad_out, (sum_two.right, sum_two.left) = sum_one.fence(
        grad_qkv, grad_out, (sum_two.right, sum_two.left)
    )

    def attn_chunk(o):
        return jnp.concatenate(
            [
                lax.dynamic_index_in_dim(grad_qkv, o, 1, keepdims=False),
                lax.dynamic_index_in_dim(grad_out, o, 0, keepdims=False).transpose(1, 0, 2),
            ],
            axis=-1,
        )

    sum_attn = Scatter(attn_chunk)
    sum_attn.step()
    sum_one.rest()
    sum_two.rest()

    def to_rows(mine, parts):
        mine = lax.all_to_all(mine.astype(BF), "seq", 0, 0, tiled=True).astype(F32)
        return mine.reshape(size, rows, parts, -1).transpose(1, 2, 0, 3).reshape(rows, -1)

    out_two = sum_two.total()
    out_one = to_rows(sum_one.total(), 1)
    grad_terms = contract_last(projected_grad, my_qkv) + contract_last(pre_grad, my_one)
    grad_terms = grad_terms.astype(BF).reshape(micro, size, length, width)
    (grad_terms,) = sum_attn.fence(grad_terms)
    sum_attn.step()
    normed_grad = scatter_seq(grad_terms)
    terms = jnp.dot(mixed, my_out, preferred_element_type=F32)
    terms = terms + jnp.dot(hidden, my_two, preferred_element_type=F32)
    terms = terms.astype(BF).reshape(micro, size, length, width)
    sums = scatter_seq(terms)
    sum_attn.rest()
    attn_total = sum_attn.total()
    out_qkv = to_rows(attn_total[..., : 3 * cols], 3)
    out_out = attn_total[..., 3 * cols :].transpose(1, 0, 2).reshape(rows, width)
    activations = (tokens.astype(F32) + sums + (bias_out + bias_two)).astype(BF)
    _, norm_back = jax.vjp(layer_norm, tokens.astype(F32), gain, shift)
    input_grad, gain_grad, shift_grad = norm_back(normed_grad)
    input_grad = input_grad + upstream.astype(F32)

    def put(values, extent, at):
        return lax.dynamic_update_slice_in_dim(jnp.zeros(extent, F32), values, at, -1)

    bqkv = jnp.sum(projected_grad.astype(F32), axis=0).reshape(3, cols)
    bqkv = put(bqkv, (3, width), me * cols)
    bone = put(jnp.sum(pre_grad.astype(F32), axis=0), (size * units,), me * units)
    btwo = jnp.sum(upstream.astype(F32), axis=(0, 1))
    packed = [gain_grad, shift_grad, bqkv[:2], bqkv[2], bone, btwo]
    packed = [v.reshape(size, depth, -1) for v in packed]
    summed = scatter_small(jnp.concatenate(packed, axis=-1))
    vectors = []
    start = 0
    for v in packed:
        vectors.append(summed[start : start + v.shape[-1]])
        start += v.shape[-1]
    return (
        activations[:, None],
        input_grad[:, None],
        vectors[0],
        vectors[1],
        out_qkv,
        vectors[2],
        vectors[3],
        out_out,
        vectors[5],
        out_one,
        vectors[4],
        out_two,
        vectors[5],
    )


def solution(mesh):
    both = ("seq", "fsdp")
    row = P(both)
    matrix = P(both, None)
    tokens = P(None, "fsdp", "seq", None)
    weights = (row, row, matrix, row, matrix, row, matrix, row, matrix, row)
    grads = (row, row, matrix, row, row, matrix, row, matrix, row, matrix, row)
    return jax.shard_map(
        per_device,
        mesh=mesh,
        in_specs=(tokens,) + weights + (P(None, "fsdp", None), tokens),
        out_specs=(tokens, tokens) + grads,
        check_vma=False,
    )
```

time: 842 us -> 642 us (0.76)
  starting transfers between devices: 239 us -> 101 us
  Pallas kernels: 43.8 us -> 162 us
  waiting for transfers between devices: 201 us -> 96.5 us
  other arithmetic: 114 us -> 61.2 us
  matrix products: 145 us -> 131 us
    pallas_call x0 -> x1, Pallas kernels: none -> 117 us  [load_all(): pl.pallas_call(functools.partial(load_kernel, dims), in_specs=[hbm] * 6 +...]
    ppermute x51 -> x28, starting transfers between devices: 156 us -> 66 us  [the longest x14 39 us: line_right(): return lax.ppermute(value, 'fsdp', [(i, i + 1) for i in senders])]
    ppermute x51 -> x28, waiting for transfers between devices: 144 us -> 60.8 us  [the longest x14 36 us: line_left(): lax.ppermute(value, 'fsdp', [(last - i, last - i - 1) for i in senders])]
    ppermute x30 -> x15, starting transfers between devices: 49.9 us -> 9.47 us  [swap(): return lax.ppermute(value, 'seq', [(i, i ^ bit) for i in range(size)])]
    convert_element_type x22 -> x17, other arithmetic: 58 us -> 30.3 us  [the longest x6 16 us: step(): coming = (coming.astype(F32) + self.left.astype(F32)).astype(BF)]
    convert_element_type x5 -> x0, local copies, waits for them, and re-layouts: 18 us -> none  [the longest x1 17.2 us: per_device(): all_tokens.astype(F32)]
    dynamic_update_slice x12 -> x3, other arithmetic: 20.2 us -> 4.12 us  [place_rows(): out = lax.dynamic_update_slice_in_dim(out, piece[None], origin, 0)]
    ppermute x30 -> x15, waiting for transfers between devices: 49.8 us -> 35.7 us  [swap(): return lax.ppermute(value, 'seq', [(i, i ^ bit) for i in range(size)])]
  transfers between devices with their start and end apart: 88 -> 48, of which waited for: 28 -> 13; matrix products, arithmetic and copies ran while one was open for 40% -> 34% of each run, Pallas kernels for 5% -> 7%
where the time goes in v2:
time: 642 us; the launch traced here: 633 us
  Pallas kernels  162 us (25%)
  matrix products  131 us (20%)
  starting transfers between devices  101 us (16%)
  waiting for transfers between devices  96.5 us (15%)
  local copies, waits for them, and re-layouts  79.2 us (12%)
  other arithmetic  61.2 us (10%)
    pallas_call x1, Pallas kernels, load_all(): pl.pallas_call(functools.partial(load_kernel, dims), in_specs=[hbm] * 6 +...  117 us
    pallas_call x2, Pallas kernels, attention(): pl.pallas_call(functools.partial(attention_kernel, blocks, length), grid=...  45.1 us
    dot_general x4, matrix products, contract_last(): lax.dot_general(left, right, (((1,), (1,)), ((), ())), preferred_element_...  44.4 us
    dot_general x4, matrix products, contract_first(): lax.dot_general(left, right, (((0,), (0,)), ((), ())), preferred_element_...  41.3 us
    ppermute x14, starting transfers between devices, line_right(): return lax.ppermute(value, 'fsdp', [(i, i + 1) for i in senders])  39 us
    ppermute x14, waiting for transfers between devices, line_left(): lax.ppermute(value, 'fsdp', [(last - i, last - i - 1) for i in senders])  36 us
    ppermute x15, waiting for transfers between devices, swap(): return lax.ppermute(value, 'seq', [(i, i ^ bit) for i in range(size)])  35.7 us
    ppermute x14, starting transfers between devices, line_left(): lax.ppermute(value, 'fsdp', [(last - i, last - i - 1) for i in senders])  27 us
  transfers between devices with their start and end apart: 48, of which 13 were waited for; matrix products, arithmetic and copies ran while one was open for 34% of the time, Pallas kernels for 7%

profile of v2, /device:TPU:15, one launch (start us, length us, event | category | flops | bytes accessed | tf_op | source)
XLA Modules:
  0.0 633.4 jit_solution(14271350570207102308)
XLA Ops:
  13.2 117.2 %shard_map.228 = (bf16[2,8,128,2048]{3,2,1,0:T(8,128)(2,1)}, bf16[2,8,128,2048]{3,2,1,0:T(8,128)(2,1)}, bf16[8,4,64,1024]{3,2,1,0:T(8,128)(2,1)S(1)}, bf16[256,2...) custom-call(bf16[2,128,2048]{2,1,0:T(8,128)(2,1)S(1)} %bitcast.322, ...), custom_call_target="tpu_custom_call" | custom-call | flops 1000 | bytes 300000000 | tf_op jit(solution)/shard_map/pallas_call | solution.py:554
  130.4 2.0 copy-done.11
  132.4 3.9 collective-permute-start
  136.3 2.1 collective-permute-start.1
  139.4 3.1 multiply_sine_fusion
  143.3 2.1 concatenate.85.cos_ref
  146.2 2.8 concatenate.86.sin_ref
  149.0 16.0 %multiply_convert_fusion = (bf16[2048,1024]{1,0:T(8,128)(2,1)S(1)}, f32[2048,1024]{1,0:T(8,128)}) fusion(f32[1024]{0:T(1024)S(1)} %dynamic_slice.183, bf16[2048,2048]{1,0:T(8,128)(2,1)} %bitcast.392, bf16[2048,1024]{1,0:T(8,128)(2,1)} %bitcast.325), kind=kOutput, calls=%fused_computation.12 | convolution fusion | flops 8610906112 | bytes 25169920 | tf_op jit(solution)/shard_map/dot_general | solution.py:744
  165.0 13.2 %convolution_convert_fusion = bf16[1024,2048]{1,0:T(8,128)(2,1)S(1)} fusion(bf16[2048,1024]{1,0:T(8,128)(2,1)S(1)} %get-tuple-element.133, bf16[2048,2048]{1,0:T(8,128)(2,1)} %bitcast.328), kind=kOutput, calls=%fused_computation.22 | convolution fusion | flops 8592031744 | bytes 16777216 | tf_op jit(solution)/shard_map/dot_general | solution.py:706
  184.6 17.9 %collective-permute-done.3 = bf16[256,2048]{1,0:T(8,128)(2,1)S(1)} collective-permute-done((bf16[256,2048]{1,0:T(8,128)(2,1)}, bf16[256,2048]{1,0:T(8,128)(2,1)S(1)}, u32[]{:S(2)}, u32[]{:S(2)}) %collective-permute-start.3) | collective-permute-done | bytes 1048608 | tf_op jit(solution)/shard_map/ppermute | solution.py:611
  202.5 4.7 collective-permute-done.4
  209.1 3.4 collective-permute-start.6
  219.3 17.6 %fusion.6 = bf16[2048,1024]{1,0:T(8,128)(2,1)S(1)} fusion(f32[2048,1024]{1,0:T(8,128)} %get-tuple-element.277, f32[1024]{0:T(1024)S(1)} %dynamic_slice.183, bf16[2048,2048]{1,0:T(8,128)(2,1)S(1)} %bitcast.332, bf16[1024,2048]{1,0:T(8,128)(2,1)} %bitcast.358), kind=kOutput, calls=%fused_computation.10 | convolution fusion | flops 8633974784 | bytes 25169920 | tf_op jit(solution)/shard_map/dot_general | solution.py:703
  236.9 13.0 %convolution_convert_fusion.1 = bf16[2048,1024]{1,0:T(8,128)(2,1)} fusion(bf16[2048,2048]{1,0:T(8,128)(2,1)} %bitcast.393, bf16[2048,1024]{1,0:T(8,128)(2,1)S(1)} %fusion.6), kind=kOutput, calls=%fused_computation.23 | convolution fusion | flops 8592031744 | bytes 16777216 | tf_op jit(solution)/shard_map/dot_general | solution.py:706
  249.9 5.5 collective-permute-start.8
  261.7 11.7 %fusion.61 = f32[2048,2048]{1,0:T(8,128)} fusion(bf16[2048,1024]{1,0:T(8,128)(2,1)S(1)} %copy-done.61, bf16[1024,2048]{1,0:T(8,128)(2,1)S(1)} %bitcast.359), kind=kOutput, calls=%fused_computation.212 | convolution fusion | flops 8589934592 | bytes 25165824 | tf_op jit(solution)/shard_map/dot_general | solution.py:828
  275.8 3.2 collective-permute-done.9
  279.0 4.6 collective-permute-done.10
  283.7 2.1 fusion.38
  287.1 4.0 collective-permute-start.14
  292.7 3.2 collective-permute-start.13
  296.0 11.7 %fusion.62 = f32[2048,2048]{1,0:T(8,128)} fusion(bf16[2048,1024]{1,0:T(8,128)(2,1)S(1)} %fusion.6, bf16[2048,1024]{1,0:T(8,128)(2,1)S(1)} %bitcast.326), kind=kOutput, calls=%fused_computation.213 | convolution fusion | flops 8589934592 | bytes 25165824 | tf_op jit(solution)/shard_map/dot_general | solution.py:703
  310.7 2.5 collective-permute-done.13
  316.2 2.4 copy-done.15
  318.6 4.1 fusion.37
  322.7 4.1 collective-permute-start.17
  326.8 2.1 collective-permute-start.16
  328.9 9.2 %broadcast_add_fusion = f32[2048,768]{1,0:T(8,128)S(1)} fusion(f32[768]{0:T(1024)S(1)} %add.389, bf16[2048,2048]{1,0:T(8,128)(2,1)} %bitcast.394, bf16[2048,768]{1,0:T(8,128)(2,1)S(1)} %bitcast.366), kind=kOutput, calls=%fused_computation.28 | convolution fusion | flops 6444023808 | bytes 17828864 | tf_op jit(solution)/shard_map/dot_general | solution.py:779
  338.1 2.5 convolution_convert_fusion.4
  342.5 22.4 %shard_map.229 = (bf16[1,8,128,256]{3,2,1,0:T(8,128)(2,1)S(1)}, bf16[1,8,128,256]{3,2,1,0:T(8,128)(2,1)S(1)}, bf16[1,8,128,256]{3,2,1,0:T(8,128)(2,1)S(1)}, bf16[1,8,128,256]{3,2,1,0:T(8,128)(2,1)S(1)}) custom-call(s32[1,2]{1,0:T(1,128)S(1)} %get-tuple-element.275.starts_ref, f32[1024,128]{1,0:T(8,128)S(1)} %concatenate.85.cos_ref, ...), custom_call_target="tpu_custom_call" | custom-call | flops 5368709120 | bytes 5767168 | tf_op jit(solution)/shard_map/pallas_call | solution.py:202
  365.1 3.2 fusion.36
  369.6 4.0 collective-permute-start.18
  375.4 22.7 %shard_map.230 = (bf16[1,8,128,256]{3,2,1,0:T(8,128)(2,1)S(1)}, bf16[1,8,128,256]{3,2,1,0:T(8,128)(2,1)S(1)}, bf16[1,8,128,256]{3,2,1,0:T(8,128)(2,1)S(1)}, bf16[1,8,128,256]{3,2,1,0:T(8,128)(2,1)S(1)}) custom-call(s32[1,2]{1,0:T(1,128)S(1)} %get-tuple-element.274.starts_ref, f32[1024,128]{1,0:T(8,128)S(1)} %concatenate.85.cos_ref, ...), custom_call_target="tpu_custom_call" | custom-call | flops 5368709120 | bytes 5767168 | tf_op jit(solution)/shard_map/pallas_call | solution.py:202
  400.7 5.7 convolution_convert_fusion.3
  407.9 4.7 fusion.32
  412.5 2.3 collective-permute-start.27
  414.9 3.1 collective-permute-start.26
  418.0 12.5 %add_convert_fusion = bf16[2048,2048]{1,0:T(8,128)(2,1)} fusion(f32[2048,2048]{1,0:T(8,128)} %fusion.62, bf16[2048,768]{1,0:T(8,128)(2,1)S(1)} %bitcast.349, bf16[2048,768]{1,0:T(8,128)(2,1)S(1)} %bitcast.367), kind=kOutput, calls=%fused_computation | convolution fusion | flops 6450839552 | bytes 31457280 | tf_op jit(solution)/shard_map/dot_general | solution.py:703
  430.5 8.2 %add_convert_fusion.1 = bf16[2048,2048]{1,0:T(8,128)(2,1)S(1)} fusion(f32[2048,2048]{1,0:T(8,128)} %fusion.61, bf16[2048,256]{1,0:T(8,128)(2,1)S(1)} %bitcast.343, bf16[256,2048]{1,0:T(8,128)(2,1)S(1)} %bitcast.362), kind=kOutput, calls=%fused_computation.1 | convolution fusion | flops 2155872256 | bytes 27262976 | tf_op jit(solution)/shard_map/dot_general | solution.py:827
  438.7 2.5 fusion.57
  445.7 9.4 %convolution_convert_fusion.2 = bf16[2048,768]{1,0:T(8,128)(2,1)S(1)} fusion(bf16[2048,2048]{1,0:T(8,128)(2,1)} %bitcast.395, bf16[2048,768]{1,0:T(8,128)(2,1)S(1)} %bitcast.350), kind=kOutput, calls=%fused_computation.24 | convolution fusion | flops 6444023808 | bytes 14680064 | tf_op jit(solution)/shard_map/dot_general | solution.py:706
  455.1 3.5 fusion.29
  458.6 12.1 %all-to-all-start.1 = ((bf16[8,64,1024]{2,1,0:T(8,128)(2,1)}), bf16[8,64,1024]{2,1,0:T(8,128)(2,1)}, u32[]{:S(2)}, u32[]{:S(2)}) async-start(bf16[8,64,1024]{2,1,0:T(8,128)(2,1)} %fusion.29), calls=%async_computation.1 | async-start | bytes 2097152 | tf_op jit(solution)/shard_map/all_to_all | solution.py:817
  472.3 2.0 dynamic-slice_bitcast_fusion.12
  482.7 3.1 fusion.27
  491.1 11.1 %collective-permute-done.28 = bf16[8,64,1024]{2,1,0:T(8,128)(2,1)} collective-permute-done((bf16[8,64,1024]{2,1,0:T(8,128)(2,1)}, bf16[8,64,1024]{2,1,0:T(8,128)(2,1)}, u32[]{:S(2)}, u32[]{:S(2)}) %collective-permute-start.28) | collective-permute-done | bytes 1048608 | tf_op jit(solution)/shard_map/ppermute | solution.py:606
  503.7 4.7 collective-permute-start.42
  508.4 4.0 fusion.56
  519.4 2.7 fusion.10
  522.6 2.6 fusion.9
  525.3 4.3 collective-permute-done.42
  530.3 12.3 %collective-permute-done.44 = bf16[8,64,1024]{2,1,0:T(8,128)(2,1)S(1)} collective-permute-done((bf16[8,64,1024]{2,1,0:T(8,128)(2,1)S(1)}, bf16[8,64,1024]{2,1,0:T(8,128)(2,1)S(1)}, u32[]{:S(2)}, u32[]{:S(2)}) %collective-permute-start.44) | collective-permute-done | bytes 1048608 | tf_op jit(solution)/shard_map/ppermute | solution.py:611
  544.8 2.2 collective-permute-done.21
  547.1 2.2 collective-permute-start.45
  555.2 8.6 %collective-permute-done.22 = bf16[2,128,1024]{2,1,0:T(8,128)(2,1)S(1)} collective-permute-done((bf16[2,128,1024]{2,1,0:T(8,128)(2,1)S(1)}, bf16[2,128,1024]{2,1,0:T(8,128)(2,1)S(1)}, u32[]{:S(2)}, u32[]{:S(2)}) %collective-permute-start.22) | collective-permute-done | bytes 524320 | tf_op jit(solution)/shard_map/ppermute | solution.py:25
  565.2 21.1 %collective-permute-done.34 = bf16[2,2,128,1024]{3,2,0,1:T(8,128)(2,1)S(1)} collective-permute-done((bf16[2,2,128,1024]{3,2,0,1:T(8,128)(2,1)S(1)}, bf16[2,2,128,1024]{3,2,0,1:T(8,128)(2,1)S(1)}, u32[]{:S(2)}, u32[]{:S(2)}) %collective-permute-start.34) | collective-permute-done | bytes 1048608 | tf_op jit(solution)/shard_map/ppermute | solution.py:25
  591.8 9.3 %all-to-all-start = ((bf16[8,64,768]{2,1,0:T(8,128)(2,1)}), bf16[8,64,768]{2,1,0:T(8,128)(2,1)}, u32[]{:S(2)}, u32[]{:S(2)}) async-start(bf16[8,64,768]{2,1,0:T(8,128)(2,1)} %slice.229), calls=%async_computation | async-start | bytes 1572864 | tf_op jit(solution)/shard_map/all_to_all | solution.py:817
  606.1 2.4 fusion.43
  608.4 2.9 collective-permute-done.36
  613.4 3.5 reshape.373
  616.9 2.7 copy.193
  621.2 2.5 collective-permute-start.38
  624.6 2.4 collective-permute-start.39
  628.5 2.3 fusion.24
  (342 shorter events, 113.6 us)
Async XLA Ops:
  13.2 125.3 %copy-start.4 = (bf16[2,1,128,2048]{3,2,1,0:T(8,128)(2,1)S(1)}, bf16[2,1,128,2048]{3,2,1,0:T(8,128)(2,1)}, u32[]{:S(2)}) copy-start(bf16[2,1,128,2048]{3,2,1,0:T(8,128)(2,1)} %param.25) | copy-start | bytes 3145732
  132.4 45.9 %collective-permute-start = (bf16[256,2048]{1,0:T(8,128)(2,1)}, bf16[256,2048]{1,0:T(8,128)(2,1)}, u32[]{:S(2)}, u32[]{:S(2)}) collective-permute-start(bf16[256,2048]{1,0:T(8,128)(2,1)} %get-tuple-element.93), channel_id=1, source_target_pairs={{1,2},{2,3},{5,6},{6,7},{9,10},{10,11},{13,14},{14,15},{17,18},{18... | collective-permute-start | bytes 3145736 | tf_op jit(solution)/shard_map/ppermute | solution.py:606
  136.3 42.1 %collective-permute-start.1 = (bf16[256,2048]{1,0:T(8,128)(2,1)S(1)}, bf16[256,2048]{1,0:T(8,128)(2,1)}, u32[]{:S(2)}, u32[]{:S(2)}) collective-permute-start(bf16[256,2048]{1,0:T(8,128)(2,1)S(1)} %get-tuple-element.98), channel_id=1, source_target_pairs={{2,1},{1,0},{6,5},{5,4},{10,9},{9,8},{14,13},{13,12},{18,17},{17,1... | collective-permute-start | bytes 3145736 | tf_op jit(solution)/shard_map/ppermute | solution.py:611
  165.0 13.2 %copy-start.60 = (bf16[2048,1024]{1,0:T(8,128)(2,1)}, bf16[2048,1024]{1,0:T(8,128)(2,1)S(1)}, u32[]{:S(2)}) copy-start(bf16[2048,1024]{1,0:T(8,128)(2,1)S(1)} %get-tuple-element.133) | copy-start | bytes 12582916
  178.3 105.4 %copy-start.14 = (bf16[1024,2048]{1,0:T(8,128)(2,1)}, bf16[1024,2048]{1,0:T(8,128)(2,1)S(1)}, u32[]{:S(2)}) copy-start(bf16[1024,2048]{1,0:T(8,128)(2,1)S(1)} %convolution_convert_fusion) | copy-start | bytes 12582916
  178.3 6.2 collective-permute-start.2
  179.2 23.3 %collective-permute-start.3 = (bf16[256,2048]{1,0:T(8,128)(2,1)}, bf16[256,2048]{1,0:T(8,128)(2,1)S(1)}, u32[]{:S(2)}, u32[]{:S(2)}) collective-permute-start(bf16[256,2048]{1,0:T(8,128)(2,1)} %collective-permute-done.1), channel_id=1, source_target_pairs={{1,0},{5,4},{9,8},{13,12},{17,16},{21,20},{25,24},{29,28}} | collective-permute-start | bytes 3145736 | tf_op jit(solution)/shard_map/ppermute | solution.py:611
  181.0 32.1 %copy-start.7 = (bf16[256,2048]{1,0:T(8,128)(2,1)S(1)}, bf16[256,2048]{1,0:T(8,128)(2,1)}, u32[]{:S(2)}) copy-start(bf16[256,2048]{1,0:T(8,128)(2,1)} %two_ref.1) | copy-start | bytes 3145732
  181.0 21.5 %collective-permute-start.5 = (bf16[256,2048]{1,0:T(8,128)(2,1)S(1)}, bf16[256,2048]{1,0:T(8,128)(2,1)S(1)}, u32[]{:S(2)}, u32[]{:S(2)}) collective-permute-start(bf16[256,2048]{1,0:T(8,128)(2,1)S(1)} %get-tuple-element.245), channel_id=1, source_target_pairs={{3,2},{7,6},{11,10},{15,14},{19,18},{23,22},{27,26},{31,30}} | collective-permute-start | bytes 3145736 | tf_op jit(solution)/shard_map/ppermute | solution.py:611
  181.8 25.4 %collective-permute-start.4 = (bf16[256,2048]{1,0:T(8,128)(2,1)S(1)}, bf16[256,2048]{1,0:T(8,128)(2,1)S(1)}, u32[]{:S(2)}, u32[]{:S(2)}) collective-permute-start(bf16[256,2048]{1,0:T(8,128)(2,1)S(1)} %get-tuple-element.246), channel_id=1, source_target_pairs={{0,1},{4,5},{8,9},{12,13},{16,17},{20,21},{24,25},{28,29}} | collective-permute-start | bytes 3145736 | tf_op jit(solution)/shard_map/ppermute | solution.py:606
  207.2 42.7 %collective-permute-start.7 = (bf16[8,64,1024]{2,1,0:T(8,128)(2,1)S(1)}, bf16[8,64,1024]{2,1,0:T(8,128)(2,1)}, u32[]{:S(2)}, u32[]{:S(2)}) collective-permute-start(bf16[8,64,1024]{2,1,0:T(8,128)(2,1)S(1)} %get-tuple-element.91), channel_id=1, source_target_pairs={{3,2},{2,1},{1,0},{7,6},{6,5},{5,4},{11,10},{10,9},{9,8},{15,14},{... | collective-permute-start | bytes 3145736 | tf_op jit(solution)/shard_map/ppermute | solution.py:611
  209.1 40.8 %collective-permute-start.6 = (bf16[8,64,1024]{2,1,0:T(8,128)(2,1)S(1)}, bf16[8,64,1024]{2,1,0:T(8,128)(2,1)}, u32[]{:S(2)}, u32[]{:S(2)}) collective-permute-start(bf16[8,64,1024]{2,1,0:T(8,128)(2,1)S(1)} %get-tuple-element.91), channel_id=1, source_target_pairs={{0,1},{1,2},{2,3},{4,5},{5,6},{6,7},{8,9},{9,10},{10,11},{12,13},{... | collective-permute-start | bytes 3145736 | tf_op jit(solution)/shard_map/ppermute | solution.py:606
  236.9 24.7 %copy-start.61 = (bf16[2048,1024]{1,0:T(8,128)(2,1)S(1)}, bf16[2048,1024]{1,0:T(8,128)(2,1)}, u32[]{:S(2)}) copy-start(bf16[2048,1024]{1,0:T(8,128)(2,1)} %copy-done.60) | copy-start | bytes 12582916
  249.9 25.9 %collective-permute-start.8 = (bf16[8,64,1024]{2,1,0:T(8,128)(2,1)}, bf16[8,64,1024]{2,1,0:T(8,128)(2,1)}, u32[]{:S(2)}, u32[]{:S(2)}) collective-permute-start(bf16[8,64,1024]{2,1,0:T(8,128)(2,1)} %collective-permute-done.6), channel_id=1, source_target_pairs={{1,2},{2,3},{5,6},{6,7},{9,10},{10,11},{13,14},{14,15},{17,18},{18... | collective-permute-start | bytes 3145736 | tf_op jit(solution)/shard_map/ppermute | solution.py:606
  255.4 23.6 %collective-permute-start.9 = (bf16[8,64,1024]{2,1,0:T(8,128)(2,1)}, bf16[8,64,1024]{2,1,0:T(8,128)(2,1)}, u32[]{:S(2)}, u32[]{:S(2)}) collective-permute-start(bf16[8,64,1024]{2,1,0:T(8,128)(2,1)} %collective-permute-done.7), channel_id=1, source_target_pairs={{2,1},{1,0},{6,5},{5,4},{10,9},{9,8},{14,13},{13,12},{18,17},{17,1... | collective-permute-start | bytes 3145736 | tf_op jit(solution)/shard_map/ppermute | solution.py:611
  259.2 19.9 %collective-permute-start.11 = (bf16[8,64,1024]{2,1,0:T(8,128)(2,1)S(1)}, bf16[8,64,1024]{2,1,0:T(8,128)(2,1)S(1)}, u32[]{:S(2)}, u32[]{:S(2)}) collective-permute-start(bf16[8,64,1024]{2,1,0:T(8,128)(2,1)S(1)} %get-tuple-element.243), channel_id=1, source_target_pairs={{3,2},{7,6},{11,10},{15,14},{19,18},{23,22},{27,26},{31,30}} | collective-permute-start | bytes 3145736 | tf_op jit(solution)/shard_map/ppermute | solution.py:611
  260.4 23.3 %collective-permute-start.10 = (bf16[8,64,1024]{2,1,0:T(8,128)(2,1)S(1)}, bf16[8,64,1024]{2,1,0:T(8,128)(2,1)S(1)}, u32[]{:S(2)}, u32[]{:S(2)}) collective-permute-start(bf16[8,64,1024]{2,1,0:T(8,128)(2,1)S(1)} %get-tuple-element.244), channel_id=1, source_target_pairs={{0,1},{4,5},{8,9},{12,13},{16,17},{20,21},{24,25},{28,29}} | collective-permute-start | bytes 3145736 | tf_op jit(solution)/shard_map/ppermute | solution.py:606
  275.8 20.1 %copy-start.12 = (bf16[8,4,64,1024]{3,2,1,0:T(8,128)(2,1)S(1)}, bf16[8,4,64,1024]{3,2,1,0:T(8,128)(2,1)}, u32[]{:S(2)}) copy-start(bf16[8,4,64,1024]{3,2,1,0:T(8,128)(2,1)} %copy-done.11) | copy-start | bytes 12582916
  285.8 24.9 %collective-permute-start.15 = (bf16[256,2048]{1,0:T(8,128)(2,1)}, bf16[256,2048]{1,0:T(8,128)(2,1)}, u32[]{:S(2)}, u32[]{:S(2)}) collective-permute-start(bf16[256,2048]{1,0:T(8,128)(2,1)} %get-tuple-element.241), channel_id=1, source_target_pairs={{3,2},{2,1},{7,6},{6,5},{11,10},{10,9},{15,14},{14,13},{19,18},{18... | collective-permute-start | bytes 3145736 | tf_op jit(solution)/shard_map/ppermute | solution.py:611
  287.1 23.6 %collective-permute-start.14 = (bf16[256,2048]{1,0:T(8,128)(2,1)}, bf16[256,2048]{1,0:T(8,128)(2,1)}, u32[]{:S(2)}, u32[]{:S(2)}) collective-permute-start(bf16[256,2048]{1,0:T(8,128)(2,1)} %get-tuple-element.242), channel_id=1, source_target_pairs={{0,1},{1,2},{4,5},{5,6},{8,9},{9,10},{12,13},{13,14},{16,17},{17,1... | collective-permute-start | bytes 3145736 | tf_op jit(solution)/shard_map/ppermute | solution.py:606
  291.1 19.6 %collective-permute-start.12 = (bf16[8,64,1024]{2,1,0:T(8,128)(2,1)}, bf16[8,64,1024]{2,1,0:T(8,128)(2,1)}, u32[]{:S(2)}, u32[]{:S(2)}) collective-permute-start(bf16[8,64,1024]{2,1,0:T(8,128)(2,1)} %collective-permute-done.8), channel_id=1, source_target_pairs={{2,3},{6,7},{10,11},{14,15},{18,19},{22,23},{26,27},{30,31}} | collective-permute-start | bytes 3145736 | tf_op jit(solution)/shard_map/ppermute | solution.py:606
  292.7 20.5 %collective-permute-start.13 = (bf16[8,64,1024]{2,1,0:T(8,128)(2,1)}, bf16[8,64,1024]{2,1,0:T(8,128)(2,1)}, u32[]{:S(2)}, u32[]{:S(2)}) collective-permute-start(bf16[8,64,1024]{2,1,0:T(8,128)(2,1)} %collective-permute-done.9), channel_id=1, source_target_pairs={{1,0},{5,4},{9,8},{13,12},{17,16},{21,20},{25,24},{29,28}} | collective-permute-start | bytes 3145736 | tf_op jit(solution)/shard_map/ppermute | solution.py:611
  315.4 22.7 %copy-start.36 = (bf16[8,4,64,768]{3,2,1,0:T(8,128)(2,1)}, bf16[8,4,64,768]{3,2,1,0:T(8,128)(2,1)S(1)}, u32[]{:S(2)}) copy-start(bf16[8,4,64,768]{3,2,1,0:T(8,128)(2,1)S(1)} %fusion.46) | copy-start | bytes 9437188
  318.6 19.5 %copy-start.27 = (bf16[32,8,8,256]{3,1,2,0:T(8,128)(2,1)}, bf16[32,8,8,256]{3,1,2,0:T(8,128)(2,1)S(1)}, u32[]{:S(2)}) copy-start(bf16[32,8,8,256]{3,1,2,0:T(8,128)(2,1)S(1)} %copy.204) | copy-start | bytes 3145732
  318.6 19.5 %slice-start.2 = ((s8[8388608]{0:T(1024)(128)(4,1)}), s8[4194304]{0:T(1024)(128)(4,1)S(1)}, s32[]{:S(2)}) async-start(s8[8388608]{0:T(1024)(128)(4,1)} %bitcast.333), calls=%async_computation.4 | async-start | bytes 8388608
  322.7 42.3 %collective-permute-start.17 = (bf16[256,2048]{1,0:T(8,128)(2,1)}, bf16[256,2048]{1,0:T(8,128)(2,1)S(1)}, u32[]{:S(2)}, u32[]{:S(2)}) collective-permute-start(bf16[256,2048]{1,0:T(8,128)(2,1)} %get-tuple-element.239), channel_id=1, source_target_pairs={{3,2},{2,1},{1,0},{7,6},{6,5},{5,4},{11,10},{10,9},{9,8},{15,14},{... | collective-permute-start | bytes 3145736 | tf_op jit(solution)/shard_map/ppermute | solution.py:611
  326.8 38.2 %collective-permute-start.16 = (bf16[256,2048]{1,0:T(8,128)(2,1)}, bf16[256,2048]{1,0:T(8,128)(2,1)S(1)}, u32[]{:S(2)}, u32[]{:S(2)}) collective-permute-start(bf16[256,2048]{1,0:T(8,128)(2,1)} %get-tuple-element.240), channel_id=1, source_target_pairs={{0,1},{1,2},{2,3},{4,5},{5,6},{6,7},{8,9},{9,10},{10,11},{12,13},{... | collective-permute-start | bytes 3145736 | tf_op jit(solution)/shard_map/ppermute | solution.py:606
  342.5 22.5 %copy-start.46 = (bf16[8,64,1024]{2,1,0:T(8,128)(2,1)S(1)}, bf16[8,64,1024]{2,1,0:T(8,128)(2,1)}, u32[]{:S(2)}) copy-start(bf16[8,64,1024]{2,1,0:T(8,128)(2,1)} %copy-done.45) | copy-start | bytes 3145732
  342.5 22.6 %copy-start.48 = (bf16[8,64,1024]{2,1,0:T(8,128)(2,1)S(1)}, bf16[8,64,1024]{2,1,0:T(8,128)(2,1)}, u32[]{:S(2)}) copy-start(bf16[8,64,1024]{2,1,0:T(8,128)(2,1)} %copy-done.47) | copy-start | bytes 3145732
  368.3 30.2 %collective-permute-start.19 = (bf16[8,64,1024]{2,1,0:T(8,128)(2,1)S(1)}, bf16[8,64,1024]{2,1,0:T(8,128)(2,1)}, u32[]{:S(2)}, u32[]{:S(2)}) collective-permute-start(bf16[8,64,1024]{2,1,0:T(8,128)(2,1)S(1)} %get-tuple-element.237), channel_id=1, source_target_pairs={{3,2},{2,1},{7,6},{6,5},{11,10},{10,9},{15,14},{14,13},{19,18},{18... | collective-permute-start | bytes 3145736 | tf_op jit(solution)/shard_map/ppermute | solution.py:611
  369.6 28.9 %collective-permute-start.18 = (bf16[8,64,1024]{2,1,0:T(8,128)(2,1)S(1)}, bf16[8,64,1024]{2,1,0:T(8,128)(2,1)}, u32[]{:S(2)}, u32[]{:S(2)}) collective-permute-start(bf16[8,64,1024]{2,1,0:T(8,128)(2,1)S(1)} %get-tuple-element.238), channel_id=1, source_target_pairs={{0,1},{1,2},{4,5},{5,6},{8,9},{9,10},{12,13},{13,14},{16,17},{17,1... | collective-permute-start | bytes 3145736 | tf_op jit(solution)/shard_map/ppermute | solution.py:606
  412.5 42.5 %collective-permute-start.27 = (bf16[8,64,1024]{2,1,0:T(8,128)(2,1)}, bf16[8,64,1024]{2,1,0:T(8,128)(2,1)}, u32[]{:S(2)}, u32[]{:S(2)}) collective-permute-start(bf16[8,64,1024]{2,1,0:T(8,128)(2,1)} %get-tuple-element.231), channel_id=1, source_target_pairs={{3,2},{2,1},{1,0},{7,6},{6,5},{5,4},{11,10},{10,9},{9,8},{15,14},{... | collective-permute-start | bytes 3145736 | tf_op jit(solution)/shard_map/ppermute | solution.py:611
  414.8 15.7 %copy-start.28 = (bf16[32,8,8,256]{3,1,2,0:T(8,128)(2,1)S(1)}, bf16[32,8,8,256]{3,1,2,0:T(8,128)(2,1)}, u32[]{:S(2)}) copy-start(bf16[32,8,8,256]{3,1,2,0:T(8,128)(2,1)} %copy-done.27) | copy-start | bytes 3145732
  414.9 40.2 %collective-permute-start.26 = (bf16[8,64,1024]{2,1,0:T(8,128)(2,1)}, bf16[8,64,1024]{2,1,0:T(8,128)(2,1)}, u32[]{:S(2)}, u32[]{:S(2)}) collective-permute-start(bf16[8,64,1024]{2,1,0:T(8,128)(2,1)} %get-tuple-element.232), channel_id=1, source_target_pairs={{0,1},{1,2},{2,3},{4,5},{5,6},{6,7},{8,9},{9,10},{10,11},{12,13},{... | collective-permute-start | bytes 3145736 | tf_op jit(solution)/shard_map/ppermute | solution.py:606
  458.6 29.5 %all-to-all-start.1 = ((bf16[8,64,1024]{2,1,0:T(8,128)(2,1)}), bf16[8,64,1024]{2,1,0:T(8,128)(2,1)}, u32[]{:S(2)}, u32[]{:S(2)}) async-start(bf16[8,64,1024]{2,1,0:T(8,128)(2,1)} %fusion.29), calls=%async_computation.1 | async-start | bytes 2097152 | tf_op jit(solution)/shard_map/all_to_all | solution.py:817
  475.5 26.7 %collective-permute-start.28 = (bf16[8,64,1024]{2,1,0:T(8,128)(2,1)}, bf16[8,64,1024]{2,1,0:T(8,128)(2,1)}, u32[]{:S(2)}, u32[]{:S(2)}) collective-permute-start(bf16[8,64,1024]{2,1,0:T(8,128)(2,1)} %pad_maximum_fusion.2), channel_id=1, source_target_pairs={{0,1},{4,5},{8,9},{12,13},{16,17},{20,21},{24,25},{28,29}} | collective-permute-start | bytes 3145736 | tf_op jit(solution)/shard_map/ppermute | solution.py:606
  478.0 24.2 %collective-permute-start.29 = (bf16[8,64,1024]{2,1,0:T(8,128)(2,1)}, bf16[8,64,1024]{2,1,0:T(8,128)(2,1)}, u32[]{:S(2)}, u32[]{:S(2)}) collective-permute-start(bf16[8,64,1024]{2,1,0:T(8,128)(2,1)} %pad_maximum_fusion.3), channel_id=1, source_target_pairs={{3,2},{7,6},{11,10},{15,14},{19,18},{23,22},{27,26},{31,30}} | collective-permute-start | bytes 3145736 | tf_op jit(solution)/shard_map/ppermute | solution.py:611
  481.9 36.5 %collective-permute-start.20 = (bf16[2,2,2,128,1024]{4,3,0,1,2:T(8,128)(2,1)}, bf16[2,2,2,128,1024]{4,3,0,1,2:T(8,128)(2,1)}, u32[]{:S(2)}, u32[]{:S(2)}) collective-permute-start(bf16[2,2,2,128,1024]{4,3,0,1,2:T(8,128)(2,1)} %bitcast.314), channel_id=1, source_target_pairs={{0,4},{4,0},{8,12},{12,8},{16,20},{20,16},{24,28},{28,24},{1,5},{5... | collective-permute-start | bytes 6291464 | tf_op jit(solution)/shard_map/ppermute | solution.py:25
  482.2 40.0 %collective-permute-start.23 = (bf16[2,2,2,128,1024]{4,3,0,2,1:T(8,128)(2,1)}, bf16[2,2,2,128,1024]{4,3,0,2,1:T(8,128)(2,1)}, u32[]{:S(2)}, u32[]{:S(2)}) collective-permute-start(bf16[2,2,2,128,1024]{4,3,0,2,1:T(8,128)(2,1)} %bitcast.313), channel_id=1, source_target_pairs={{0,4},{4,0},{8,12},{12,8},{16,20},{20,16},{24,28},{28,24},{1,5},{5... | collective-permute-start | bytes 6291464 | tf_op jit(solution)/shard_map/ppermute | solution.py:25
  488.1 14.1 %copy-start.33 = (bf16[8,64,768]{2,1,0:T(8,128)(2,1)S(1)}, bf16[8,64,768]{2,1,0:T(8,128)(2,1)}, u32[]{:S(2)}) copy-start(bf16[8,64,768]{2,1,0:T(8,128)(2,1)} %get-tuple-element.250) | copy-start | bytes 2359300
  488.1 14.1 %copy-start.40 = (bf16[1,64,8,256]{3,1,2,0:T(8,128)(2,1)S(1)}, bf16[1,64,8,256]{3,1,2,0:T(8,128)(2,1)}, u32[]{:S(2)}) copy-start(bf16[1,64,8,256]{3,1,2,0:T(8,128)(2,1)} %copy.248) | copy-start | bytes 786436
  503.7 25.9 %collective-permute-start.42 = (bf16[8,64,1024]{2,1,0:T(8,128)(2,1)S(1)}, bf16[8,64,1024]{2,1,0:T(8,128)(2,1)S(1)}, u32[]{:S(2)}, u32[]{:S(2)}) collective-permute-start(bf16[8,64,1024]{2,1,0:T(8,128)(2,1)S(1)} %add_convert_fusion.5), channel_id=1, source_target_pairs={{0,1},{1,2},{4,5},{5,6},{8,9},{9,10},{12,13},{13,14},{16,17},{17,1... | collective-permute-start | bytes 3145736 | tf_op jit(solution)/shard_map/ppermute | solution.py:606
  513.2 36.5 %collective-permute-start.33 = (bf16[2,2,2,128,1024]{4,3,0,2,1:T(8,128)(2,1)S(1)}, bf16[2,2,2,128,1024]{4,3,0,2,1:T(8,128)(2,1)S(1)}, u32[]{:S(2)}, u32[]{:S(2)}) collective-permute-start(bf16[2,2,2,128,1024]{4,3,0,2,1:T(8,128)(2,1)S(1)} %bitcast.369), channel_id=1, source_target_pairs={{0,4},{4,0},{8,12},{12,8},{16,20},{20,16},{24,28},{28,24},{1,5},{5... | collective-permute-start | bytes 6291464 | tf_op jit(solution)/shard_map/ppermute | solution.py:25
  516.9 25.6 %collective-permute-start.44 = (bf16[8,64,1024]{2,1,0:T(8,128)(2,1)S(1)}, bf16[8,64,1024]{2,1,0:T(8,128)(2,1)S(1)}, u32[]{:S(2)}, u32[]{:S(2)}) collective-permute-start(bf16[8,64,1024]{2,1,0:T(8,128)(2,1)S(1)} %add_convert_fusion.3), channel_id=1, source_target_pairs={{3,2},{2,1},{7,6},{6,5},{11,10},{10,9},{15,14},{14,13},{19,18},{18... | collective-permute-start | bytes 3145736 | tf_op jit(solution)/shard_map/ppermute | solution.py:611
  518.4 32.7 %collective-permute-start.30 = (bf16[2,2,2,128,1024]{4,3,0,1,2:T(8,128)(2,1)S(1)}, bf16[2,2,2,128,1024]{4,3,0,1,2:T(8,128)(2,1)S(1)}, u32[]{:S(2)}, u32[]{:S(2)}) collective-permute-start(bf16[2,2,2,128,1024]{4,3,0,1,2:T(8,128)(2,1)S(1)} %bitcast.370), channel_id=1, source_target_pairs={{0,4},{4,0},{8,12},{12,8},{16,20},{20,16},{24,28},{28,24},{1,5},{5... | collective-permute-start | bytes 6291464 | tf_op jit(solution)/shard_map/ppermute | solution.py:25
  522.2 24.8 %collective-permute-start.21 = (bf16[2,2,128,1024]{3,2,0,1:T(8,128)(2,1)S(1)}, bf16[2,2,128,1024]{3,2,0,1:T(8,128)(2,1)S(1)}, u32[]{:S(2)}, u32[]{:S(2)}) collective-permute-start(bf16[2,2,128,1024]{3,2,0,1:T(8,128)(2,1)S(1)} %dynamic-slice_bitcast_fusion.3), channel_id=1, source_target_pairs={{0,8},{4,12},{8,0},{12,4},{16,24},{20,28},{24,16},{28,20},{1,9},{5... | collective-permute-start | bytes 3145736 | tf_op jit(solution)/shard_map/ppermute | solution.py:25
  525.2 19.3 %copy-start.30 = (bf16[8,64,768]{2,1,0:T(8,128)(2,1)S(1)}, bf16[8,64,768]{2,1,0:T(8,128)(2,1)}, u32[]{:S(2)}) copy-start(bf16[8,64,768]{2,1,0:T(8,128)(2,1)} %get-tuple-element.249) | copy-start | bytes 2359300
  529.7 23.9 %collective-permute-start.24 = (bf16[2,2,128,1024]{3,2,0,1:T(8,128)(2,1)S(1)}, bf16[2,2,128,1024]{3,2,0,1:T(8,128)(2,1)S(1)}, u32[]{:S(2)}, u32[]{:S(2)}) collective-permute-start(bf16[2,2,128,1024]{3,2,0,1:T(8,128)(2,1)S(1)} %dynamic-slice_bitcast_fusion.2), channel_id=1, source_target_pairs={{0,16},{4,20},{8,24},{12,28},{16,0},{20,4},{24,8},{28,12},{1,17},{... | collective-permute-start | bytes 3145736 | tf_op jit(solution)/shard_map/ppermute | solution.py:25
  542.6 46.3 %collective-permute-start.43 = (bf16[8,64,1024]{2,1,0:T(8,128)(2,1)S(1)}, bf16[8,64,1024]{2,1,0:T(8,128)(2,1)S(1)}, u32[]{:S(2)}, u32[]{:S(2)}) collective-permute-start(bf16[8,64,1024]{2,1,0:T(8,128)(2,1)S(1)} %add_convert_fusion.4), channel_id=1, source_target_pairs={{0,1},{1,2},{2,3},{4,5},{5,6},{6,7},{8,9},{9,10},{10,11},{12,13},{... | collective-permute-start | bytes 3145736 | tf_op jit(solution)/shard_map/ppermute | solution.py:606
  547.1 41.8 %collective-permute-start.45 = (bf16[8,64,1024]{2,1,0:T(8,128)(2,1)S(1)}, bf16[8,64,1024]{2,1,0:T(8,128)(2,1)S(1)}, u32[]{:S(2)}, u32[]{:S(2)}) collective-permute-start(bf16[8,64,1024]{2,1,0:T(8,128)(2,1)S(1)} %add_convert_fusion.2), channel_id=1, source_target_pairs={{3,2},{2,1},{1,0},{7,6},{6,5},{5,4},{11,10},{10,9},{9,8},{15,14},{... | collective-permute-start | bytes 3145736 | tf_op jit(solution)/shard_map/ppermute | solution.py:611
  549.7 14.1 %collective-permute-start.22 = (bf16[2,128,1024]{2,1,0:T(8,128)(2,1)S(1)}, bf16[2,128,1024]{2,1,0:T(8,128)(2,1)S(1)}, u32[]{:S(2)}, u32[]{:S(2)}) collective-permute-start(bf16[2,128,1024]{2,1,0:T(8,128)(2,1)S(1)} %dynamic-slice_bitcast_fusion.18), channel_id=1, source_target_pairs={{0,16},{4,20},{8,24},{12,28},{16,0},{20,4},{24,8},{28,12},{1,17},{... | collective-permute-start | bytes 1572872 | tf_op jit(solution)/shard_map/ppermute | solution.py:25
  551.2 35.2 %collective-permute-start.34 = (bf16[2,2,128,1024]{3,2,0,1:T(8,128)(2,1)S(1)}, bf16[2,2,128,1024]{3,2,0,1:T(8,128)(2,1)S(1)}, u32[]{:S(2)}, u32[]{:S(2)}) collective-permute-start(bf16[2,2,128,1024]{3,2,0,1:T(8,128)(2,1)S(1)} %dynamic-slice_bitcast_fusion), channel_id=1, source_target_pairs={{0,16},{4,20},{8,24},{12,28},{16,0},{20,4},{24,8},{28,12},{1,17},{... | collective-permute-start | bytes 3145736 | tf_op jit(solution)/shard_map/ppermute | solution.py:25
  553.5 33.7 %collective-permute-start.31 = (bf16[2,2,128,1024]{3,2,0,1:T(8,128)(2,1)S(1)}, bf16[2,2,128,1024]{3,2,0,1:T(8,128)(2,1)S(1)}, u32[]{:S(2)}, u32[]{:S(2)}) collective-permute-start(bf16[2,2,128,1024]{3,2,0,1:T(8,128)(2,1)S(1)} %dynamic-slice_bitcast_fusion.1), channel_id=1, source_target_pairs={{0,8},{4,12},{8,0},{12,4},{16,24},{20,28},{24,16},{28,20},{1,9},{5... | collective-permute-start | bytes 3145736 | tf_op jit(solution)/shard_map/ppermute | solution.py:25
  554.3 32.5 %copy-start.25 = (bf16[2,2,128,1024]{3,2,0,1:T(8,128)(2,1)}, bf16[2,2,128,1024]{3,2,0,1:T(8,128)(2,1)S(1)}, u32[]{:S(2)}) copy-start(bf16[2,2,128,1024]{3,2,0,1:T(8,128)(2,1)S(1)} %fusion.34) | copy-start | bytes 3145732
  563.8 42.3 %collective-permute-start.25 = (bf16[2,128,1024]{2,1,0:T(8,128)(2,1)}, bf16[2,128,1024]{2,1,0:T(8,128)(2,1)}, u32[]{:S(2)}, u32[]{:S(2)}) collective-permute-start(bf16[2,128,1024]{2,1,0:T(8,128)(2,1)} %dynamic-slice_bitcast_fusion.17), channel_id=1, source_target_pairs={{0,8},{4,12},{8,0},{12,4},{16,24},{20,28},{24,16},{28,20},{1,9},{5... | collective-permute-start | bytes 1572872 | tf_op jit(solution)/shard_map/ppermute | solution.py:25
  586.8 14.2 %collective-permute-start.35 = (bf16[2,128,1024]{2,1,0:T(8,128)(2,1)S(1)}, bf16[2,128,1024]{2,1,0:T(8,128)(2,1)}, u32[]{:S(2)}, u32[]{:S(2)}) collective-permute-start(bf16[2,128,1024]{2,1,0:T(8,128)(2,1)S(1)} %dynamic-slice_bitcast_fusion.15), channel_id=1, source_target_pairs={{0,8},{4,12},{8,0},{12,4},{16,24},{20,28},{24,16},{28,20},{1,9},{5... | collective-permute-start | bytes 1572872 | tf_op jit(solution)/shard_map/ppermute | solution.py:25
  588.5 13.8 %collective-permute-start.32 = (bf16[2,128,1024]{2,1,0:T(8,128)(2,1)}, bf16[2,128,1024]{2,1,0:T(8,128)(2,1)}, u32[]{:S(2)}, u32[]{:S(2)}) collective-permute-start(bf16[2,128,1024]{2,1,0:T(8,128)(2,1)} %dynamic-slice_bitcast_fusion.16), channel_id=1, source_target_pairs={{0,16},{4,20},{8,24},{12,28},{16,0},{20,4},{24,8},{28,12},{1,17},{... | collective-permute-start | bytes 1572872 | tf_op jit(solution)/shard_map/ppermute | solution.py:25
  591.8 21.6 %all-to-all-start = ((bf16[8,64,768]{2,1,0:T(8,128)(2,1)}), bf16[8,64,768]{2,1,0:T(8,128)(2,1)}, u32[]{:S(2)}, u32[]{:S(2)}) async-start(bf16[8,64,768]{2,1,0:T(8,128)(2,1)} %slice.229), calls=%async_computation | async-start | bytes 1572864 | tf_op jit(solution)/shard_map/all_to_all | solution.py:817
  605.8 5.6 collective-permute-start.36
  611.4 9.8 %collective-permute-start.37 = (f32[2,4,640]{2,1,0:T(4,128)S(1)}, f32[2,4,640]{2,1,0:T(4,128)S(1)}, u32[]{:S(2)}, u32[]{:S(2)}) collective-permute-start(f32[2,4,640]{2,1,0:T(4,128)S(1)} %slice.196), channel_id=1, source_target_pairs={{0,8},{4,12},{8,0},{12,4},{16,24},{20,28},{24,16},{28,20},{1,9},{5... | collective-permute-start | bytes 61448 | tf_op jit(solution)/shard_map/ppermute | solution.py:25
  621.2 3.4 collective-permute-start.38
  624.6 6.2 collective-permute-start.39
  627.1 3.8 collective-permute-start.41
  627.1 3.8 collective-permute-start.40
  (50 other events, 255.4 us)

commit v3 on v2

--- a/solution.py
+++ b/solution.py
@@ -3,6 +3,7 @@
 
 import jax
 import jax.numpy as jnp
+import numpy as np
 from jax import lax
 from jax.experimental import pallas as pl
 from jax.experimental.pallas import tpu as pltpu
@@ -25,6 +26,13 @@
     return lax.ppermute(value, "seq", [(i, i ^ bit) for i in range(size)])
 
 
+def store_index(block):
+    half = lax.axis_size("seq") // 2
+    if isinstance(block, int):
+        return block % 2 * half + block // 2
+    return (block & 1) * half + (block >> 1)
+
+
 def scatter_seq(terms):
     size = lax.axis_size("seq")
     me = lax.axis_index("seq")
@@ -43,38 +51,12 @@
     sums = []
     for cols, order in ((slice(0, half), bits), (slice(half, width), bits[::-1])):
         held = terms[..., cols].reshape((micro,) + (2,) * count + (length, half))
-        left = list(range(count))[::-1]
+        left = [0] + bits[::-1]
         for bit in [0] + order:
             held = exchange(held, bit, 1 + left.index(bit))
             left.remove(bit)
         sums.append(held)
     return jnp.concatenate(sums, axis=-1)
-
-
-def by_index(blocks):
-    me = lax.axis_index("seq")
-    shape = blocks.shape
-    for bit in range(shape[0].bit_length() - 1):
-        split = blocks.reshape((-1, 2, 1 << bit) + shape[1:])
-        blocks = jnp.where((me >> bit) & 1 == 1, split[:, ::-1], split).reshape(shape)
-    return blocks
-
-
-def scatter_small(terms):
-    size, depth = lax.axis_size("seq"), lax.axis_size("fsdp")
-    held = by_index(terms)
-    for bit in reversed(range(size.bit_length() - 1)):
-        n = held.shape[0] // 2
-        held = held[:n] + swap(held[n:], 1 << bit)
-    at = lax.axis_index("fsdp")
-    held = held[0]
-    total = lax.dynamic_index_in_dim(held, at, 0, keepdims=False)
-    for step in range(1, depth):
-        away = lax.dynamic_index_in_dim(held, (at + step) % depth, 0, keepdims=False)
-        total = total + lax.ppermute(
-            away, "fsdp", [(i, (i + step) % depth) for i in range(depth)]
-        )
-    return total
 
 
 def attention_kernel(
@@ -114,7 +96,7 @@
         return value * cosine + other * sine
 
     for block in range(blocks):
-        source = block
+        source = store_index(block)
         at = slice(block * length, (block + 1) * length)
         cosine, sine = cos_ref[at, :], sin_ref[at, :]
         q_s[at, :] = (turn(q_ref[0, source], cosine, sine)).astype(BF) * jnp.asarray(SCALE, BF)
@@ -172,25 +154,30 @@
             block = first // length + part
             here = slice(part * length, (part + 1) * length)
             at = slice(block * length, (block + 1) * length)
-            mixed_ref[0, block] = mixed[here].astype(BF)
-            dq_ref[0, block] = turn(dq[here], cos_ref[at, :], -sin_ref[at, :]).astype(BF)
+            mixed_ref[0, store_index(block)] = mixed[here].astype(BF)
+            dq_ref[0, store_index(block)] = turn(dq[here], cos_ref[at, :], -sin_ref[at, :]).astype(BF)
     for block in range(blocks):
         at = slice(block * length, (block + 1) * length)
-        dk_ref[0, block] = turn(dk_s[at, :], cos_ref[at, :], -sin_ref[at, :]).astype(BF)
-        dv_ref[0, block] = dv_s[at, :].astype(BF)
+        dk_ref[0, store_index(block)] = turn(dk_s[at, :], cos_ref[at, :], -sin_ref[at, :]).astype(BF)
+        dv_ref[0, store_index(block)] = dv_s[at, :].astype(BF)
+
+
+def tables(total):
+    half = ROT // 2
+    frequency = (10000.0 ** (-2.0 * np.arange(half) / ROT)).astype(np.float32)
+    angles = np.arange(total, dtype=np.float32)[:, None] * frequency[None, :]
+    cosine, sine = np.cos(angles), np.sin(angles)
+    ones = np.ones((total, HEAD_DIM - ROT), np.float32)
+    cosine = np.concatenate([cosine, cosine, ones] * 2, axis=1)
+    sine = np.concatenate([-sine, sine, 0 * ones] * 2, axis=1)
+    return jnp.asarray(cosine), jnp.asarray(sine)
 
 
 def attention(starts, projected, mixed_grad):
     micro, blocks, length, cols = mixed_grad.shape
     total = blocks * length
     groups = cols // LANES
-    half = ROT // 2
-    frequency = 10000.0 ** (-2.0 * jnp.arange(half, dtype=F32) / ROT)
-    angles = jnp.arange(total, dtype=jnp.int32).astype(F32)[:, None] * frequency[None, :]
-    cosine, sine = jnp.cos(angles), jnp.sin(angles)
-    ones = jnp.ones((total, HEAD_DIM - ROT), F32)
-    cosine = jnp.concatenate([cosine, cosine, ones] * 2, axis=1)
-    sine = jnp.concatenate([-sine, sine, 0 * ones] * 2, axis=1)
+    cosine, sine = tables(total)
 
     def spec(offset):
         return pl.BlockSpec(
@@ -228,6 +215,166 @@
 MESH = pl.DeviceIdType.MESH
 
 
+def remote(src, dst, send, recv, device):
+    return pltpu.make_async_remote_copy(
+        src_ref=src,
+        dst_ref=dst,
+        send_sem=send,
+        recv_sem=recv,
+        device_id=device,
+        device_id_type=MESH,
+    )
+
+
+def greet(size, depth):
+    me, at = lax.axis_index("seq"), lax.axis_index("fsdp")
+    barrier = pltpu.get_barrier_semaphore()
+    for step in range(1, size):
+        pl.semaphore_signal(barrier, inc=1, device_id={"seq": me ^ step}, device_id_type=MESH)
+    for step in range(1, depth):
+        pl.semaphore_signal(
+            barrier, inc=1, device_id={"fsdp": lax.rem(at + step, depth)}, device_id_type=MESH
+        )
+    pl.semaphore_wait(barrier, size + depth - 2)
+
+
+class LineGather:
+    def __init__(self, depth, source, target, send, recv):
+        self.depth, self.source, self.target = depth, source, target
+        self.send, self.recv = send, recv
+
+    def copy(self, step, way):
+        at = lax.axis_index("fsdp")
+        origin = jnp.clip(at - way * (step - 1), 0, self.depth - 1)
+        number = step * 2 + (way > 0)
+        return remote(
+            self.source(origin, step),
+            self.target(origin),
+            self.send.at[number],
+            self.recv.at[number],
+            {"fsdp": jnp.clip(at + way, 0, self.depth - 1)},
+        )
+
+    def sends(self, step, way):
+        at = lax.axis_index("fsdp")
+        origin = at - way * (step - 1)
+        return (at + way >= 0) & (at + way < self.depth) & (origin >= 0) & (origin < self.depth)
+
+    def start(self, step):
+        for way in (1, -1):
+
+            @pl.when(self.sends(step, way))
+            def _():
+                self.copy(step, way).start()
+
+    def arrive(self, step):
+        at = lax.axis_index("fsdp")
+        for way in (1, -1):
+            origin = at - way * step
+
+            @pl.when((origin >= 0) & (origin < self.depth))
+            def _():
+                self.copy(step, way).wait_recv()
+
+    def sent(self, step):
+        for way in (1, -1):
+
+            @pl.when(self.sends(step, way))
+            def _():
+                self.copy(step, way).wait_send()
+
+
+class LineSum:
+    def __init__(self, depth, chunk, landing, own, held, out, load, send, recv):
+        self.depth, self.chunk, self.landing = depth, chunk, landing
+        self.own, self.held, self.out = own, held, out
+        self.load, self.send, self.recv = load, send, recv
+
+    def place(self, way):
+        at = lax.axis_index("fsdp")
+        return at if way > 0 else self.depth - 1 - at
+
+    def copy(self, step, way, src):
+        number = step * 2 + (way > 0)
+        at = lax.axis_index("fsdp")
+        return remote(
+            src,
+            self.landing(step, way),
+            self.send.at[number],
+            self.recv.at[number],
+            {"fsdp": jnp.clip(at + way, 0, self.depth - 1)},
+        )
+
+    def start(self, step, here=True):
+        for way in (1, -1):
+            place = self.place(way)
+            away = jnp.clip(self.depth - step + place, 0, self.depth - 1)
+            origin = away if way > 0 else self.depth - 1 - away
+
+            @pl.when(place == 0)
+            def _():
+                self.copy(step, way, self.chunk(origin)).start()
+
+            if step > 1:
+
+                @pl.when((place >= 1) & (place <= step - 1) & (place < self.depth - 1))
+                def _():
+                    mine = pltpu.make_async_copy(self.chunk(origin), self.own, self.load.at[0])
+                    mine.start()
+                    if here:
+                        self.copy(step - 1, way, self.out(step, way)).wait_recv()
+                    came = pltpu.make_async_copy(
+                        self.landing(step - 1, way), self.held, self.load.at[1]
+                    )
+                    came.start()
+                    mine.wait()
+                    came.wait()
+                    target = self.out(step, way)
+                    target[...] = (self.own[...].astype(F32) + self.held[...].astype(F32)).astype(
+                        BF
+                    )
+                    self.copy(step, way, target).start()
+
+    def arrive(self, step, consumed):
+        for way in (1, -1):
+            place = self.place(way)
+            ok = (place >= 1) & (place <= step)
+            if consumed:
+                ok = ok & (place == self.depth - 1)
+
+            @pl.when(ok)
+            def _():
+                self.copy(step, way, self.out(step, way)).wait_recv()
+
+    def total(self, last, right, left):
+        mine = pltpu.make_async_copy(self.chunk(lax.axis_index("fsdp")), self.own, self.load.at[0])
+        mine.start()
+        for way, target in ((1, right), (-1, left)):
+            place = self.place(way)
+
+            @pl.when(place >= 1)
+            def _():
+                self.copy(last, way, self.out(last, way)).wait_recv()
+                came = pltpu.make_async_copy(self.landing(last, way), target, self.load.at[1])
+                came.start()
+                came.wait()
+
+            @pl.when(place == 0)
+            def _():
+                target[...] = jnp.zeros_like(target)
+
+        mine.wait()
+        return self.own[...].astype(F32) + right[...].astype(F32) + left[...].astype(F32)
+
+    def sent(self, step):
+        for way in (1, -1):
+            place = self.place(way)
+
+            @pl.when((place == 0) | ((place <= step - 1) & (place < self.depth - 1)))
+            def _():
+                self.copy(step, way, self.out(step, way)).wait_send()
+
+
 def load_kernel(
     dims,
     tokens_ref,
@@ -240,8 +387,7 @@
     normed_ref,
     all_up_ref,
     my_one_ref,
-    two_right_ref,
-    two_left_ref,
+    my_two_ref,
     attn_ref,
     full_ref,
     gathered,
@@ -269,22 +415,7 @@
     def line(step):
         return {"fsdp": lax.rem(at + step, depth)}
 
-    barrier = pltpu.get_barrier_semaphore()
-    for step in range(1, size):
-        pl.semaphore_signal(barrier, inc=1, device_id=seq(step), device_id_type=MESH)
-    for step in range(1, depth):
-        pl.semaphore_signal(barrier, inc=1, device_id=line(step), device_id_type=MESH)
-    pl.semaphore_wait(barrier, size + depth - 2)
-
-    def remote(src, dst, send, recv, device):
-        return pltpu.make_async_remote_copy(
-            src_ref=src,
-            dst_ref=dst,
-            send_sem=send,
-            recv_sem=recv,
-            device_id=device,
-            device_id_type=MESH,
-        )
+    greet(size, depth)
 
     def vec_seq_copy(step):
         return remote(
@@ -326,12 +457,12 @@
         ),
         pltpu.make_async_copy(
             tokens_ref,
-            gathered.at[:, me],
+            gathered.at[:, store_index(me)],
             local_sem.at[1],
         ),
         pltpu.make_async_copy(
             up_ref,
-            all_up_ref.at[:, me],
+            all_up_ref.at[:, store_index(me)],
             local_sem.at[2],
         ),
     ]
@@ -343,12 +474,13 @@
                 local_sem.at[3 + part],
             )
         )
+    local.append(pltpu.make_async_copy(two_ref, my_two_ref.at[at], local_sem.at[6]))
     for peer in range(size):
         local.append(
             pltpu.make_async_copy(
                 out_ref.at[:, pl.ds(peer * cols, cols)],
                 attn_ref.at[peer, :, pl.ds(3 * cols, cols)],
-                local_sem.at[6 + peer],
+                local_sem.at[7 + peer],
             )
         )
 
@@ -375,7 +507,7 @@
         number = way > 0
         return ok, remote(
             two_ref,
-            two_right_ref if way > 0 else two_left_ref,
+            my_two_ref.at[at],
             line_send.at[int(number)],
             line_recv.at[int(number)],
             {"fsdp": jnp.clip(at + way, 0, depth - 1)},
@@ -411,7 +543,7 @@
 
     def row_copy(which, part, mask, bit):
         columns = slice(part * half, (part + 1) * half)
-        block = me ^ mask
+        block = store_index(me ^ mask)
         if mask == 0:
             src = sources[which].at[:, :, columns]
         else:
@@ -554,13 +686,12 @@
     return pl.pallas_call(
         functools.partial(load_kernel, dims),
         in_specs=[hbm] * 6 + [vmem],
-        out_specs=[vmem] + [hbm] * 5 + [vmem],
+        out_specs=[vmem] + [hbm] * 4 + [vmem],
         out_shape=[
             jax.ShapeDtypeStruct(gathered, BF),
             jax.ShapeDtypeStruct(gathered, BF),
             jax.ShapeDtypeStruct((size, depth, rows, units), BF),
-            jax.ShapeDtypeStruct(w_fc2.shape, BF),
-            jax.ShapeDtypeStruct(w_fc2.shape, BF),
+            jax.ShapeDtypeStruct((depth,) + w_fc2.shape, BF),
             jax.ShapeDtypeStruct((size, rows, 4 * cols), BF),
             jax.ShapeDtypeStruct(vectors.shape, F32),
         ],
@@ -569,7 +700,7 @@
             pltpu.VMEM((size,) + vectors.shape, BF),
             pltpu.VMEM(vectors.shape, BF),
             pltpu.VMEM((depth,) + vectors.shape, BF),
-            dma((6 + size,)),
+            dma((7 + size,)),
             dma((size + depth,)),
             dma((size + depth,)),
             dma((4 * size,)),
@@ -588,6 +719,1157 @@
     )(tokens, upstream, w_fc1, w_fc2, w_qkv, w_out, vectors)
 
 
+def ffn_kernel(
+    dims,
+    normed_hbm,
+    up_hbm,
+    one_hbm,
+    two_hbm,
+    cols_hbm,
+    full_ref,
+    hidden_hbm,
+    pre_hbm,
+    all_two_hbm,
+    attn_hbm,
+    grad_two_hbm,
+    grad_one_hbm,
+    land_two,
+    land_one,
+    bone_ref,
+    normed_v,
+    up_v,
+    one_v,
+    two_v,
+    hidden_v,
+    pre_v,
+    grad_two_v,
+    grad_one_v,
+    own_two,
+    held_two,
+    out_two,
+    load_sem,
+    line_load,
+    store_sem,
+    two_send,
+    two_recv,
+    attn_send,
+    attn_recv,
+    sum_two_send,
+    sum_two_recv,
+    sum_one_send,
+    sum_one_recv,
+):
+    size, depth, micro, length, width, units, cols = dims
+    me, at = lax.axis_index("seq"), lax.axis_index("fsdp")
+    count = micro * size * length
+    tile = 512
+    group = units // depth
+
+    loads = [
+        pltpu.make_async_copy(src, dst, load_sem.at[n])
+        for n, (src, dst) in enumerate(
+            ((normed_hbm, normed_v), (one_hbm, one_v), (up_hbm, up_v))
+        )
+    ]
+    for load in loads:
+        load.start()
+
+    def two_load(way):
+        origin = jnp.clip(at + way, 0, depth - 1)
+        return (at + way >= 0) & (at + way < depth), pltpu.make_async_copy(
+            two_hbm.at[origin], two_v.at[origin], load_sem.at[4 + way]
+        )
+
+    for way in (0, 1, -1):
+        ok, copy = two_load(way)
+
+        @pl.when(ok)
+        def _():
+            copy.start()
+
+    own_attn = pltpu.make_async_copy(cols_hbm, attn_hbm.at[:, at], store_sem.at[0])
+    own_attn.start()
+    greet(size, depth)
+
+    two = LineGather(
+        depth,
+        lambda o, step: two_hbm.at[o] if step == 2 else two_v.at[o],
+        lambda o: two_v.at[o],
+        two_send,
+        two_recv,
+    )
+    attn = LineGather(
+        depth,
+        lambda o, step: cols_hbm if step == 1 else attn_hbm.at[:, o],
+        lambda o: attn_hbm.at[:, o],
+        attn_send,
+        attn_recv,
+    )
+    sum_two = LineSum(
+        depth,
+        lambda o: grad_two_v.at[o],
+        lambda step, way: land_two.at[(step - 1) * 2 + (way > 0)],
+        own_two,
+        held_two,
+        lambda step, way: out_two.at[int(way > 0)],
+        line_load,
+        sum_two_send,
+        sum_two_recv,
+    )
+    sum_one = LineSum(
+        depth,
+        lambda o: grad_one_v.at[:, o],
+        lambda step, way: land_one.at[(step - 1) * 2 + (way > 0)],
+        own_two,
+        held_two,
+        lambda step, way: grad_one_v.at[:, 0],
+        line_load,
+        sum_one_send,
+        sum_one_recv,
+    )
+    two.start(2)
+
+    for load in loads[:2]:
+        load.wait()
+    root = math.sqrt(2.0 / math.pi)
+    flat = me * units
+    bias_row = 6 + flat // width
+    bias_at = pl.multiple_of(lax.rem(flat, width), units)
+    bias = full_ref[pl.ds(bias_row, 1), pl.ds(bias_at, units)]
+    bone_ref[...] = bias
+
+    @pl.loop(0, count // tile)
+    def _(r):
+        rows = pl.ds(pl.multiple_of(r * tile, tile), tile)
+        a = normed_v[rows, :]
+        for o in range(depth):
+            columns = slice(o * group, (o + 1) * group)
+            w = one_v[:, :, :, columns].reshape(width, group)
+            v = jnp.dot(a, w, preferred_element_type=F32) + bone_ref[:, columns]
+            square = v * v
+            t = jnp.tanh(root * v * (1.0 + 0.044715 * square))
+            hidden_v[rows, columns] = (0.5 * v * (1.0 + t)).astype(BF)
+            slope = 0.5 * (1.0 + t) + 0.5 * root * v * (1.0 - t * t) * (
+                1.0 + 3 * 0.044715 * square
+            )
+            pre_v[rows, columns] = slope.astype(BF)
+
+    loads[2].wait()
+    hidden_out = pltpu.make_async_copy(hidden_v, hidden_hbm, store_sem.at[1])
+    hidden_out.start()
+    over_first = (((0,), (0,)), ((), ()))
+    over_last = (((1,), (1,)), ((), ()))
+
+    @pl.loop(0, depth)
+    def _(o):
+        columns = pl.ds(pl.multiple_of(o * group, group), group)
+        y = lax.dot_general(hidden_v[:, columns], up_v[...], over_first, preferred_element_type=F32)
+        grad_two_v[o] = y.astype(BF)
+
+    two.arrive(2)
+    two.start(3)
+    sum_two.start(1)
+    grad_two_out = pltpu.make_async_copy(grad_two_v, grad_two_hbm, store_sem.at[2])
+    grad_two_out.start()
+    bone_ref[...] = jnp.zeros_like(bone_ref)
+
+    def piece(o):
+        columns = pl.ds(pl.multiple_of(o * group, group), group)
+
+        @pl.loop(0, count // tile)
+        def _(r):
+            rows = pl.ds(pl.multiple_of(r * tile, tile), tile)
+            y = lax.dot_general(up_v[rows, :], two_v[o], over_last, preferred_element_type=F32)
+            y = (y * pre_v[rows, columns].astype(F32)).astype(BF)
+            pre_v[rows, columns] = y
+            bone_ref[:, columns] += jnp.sum(y.astype(F32), axis=0, keepdims=True)
+
+        wide = 1024
+        per = width // size
+
+        @pl.loop(0, width // wide)
+        def _(d):
+            rows = pl.ds(pl.multiple_of(d * wide, wide), wide)
+            y = lax.dot_general(
+                normed_v[:, rows], pre_v[:, columns], over_first, preferred_element_type=F32
+            )
+            n = wide // per
+            y = y.astype(BF).reshape(n, depth, per // depth, group)
+            grad_one_v[pl.ds(d * n, n), :, :, columns] = y
+
+    for way in (0, 1, -1):
+        ok, copy = two_load(way)
+
+        @pl.when(ok)
+        def _():
+            copy.wait()
+
+    @pl.loop(0, 2 * depth - 3)
+    def _(number):
+        distance = (number + 1) // 2
+        origin = jnp.where(lax.rem(number, 2) == 1, at - distance, at + distance)
+
+        @pl.when((origin >= 0) & (origin < depth))
+        def _():
+            piece(jnp.clip(origin, 0, depth - 1))
+
+    two.arrive(3)
+    attn.start(1)
+
+    @pl.loop(2 * depth - 3, 2 * depth - 1)
+    def _(number):
+        distance = (number + 1) // 2
+        origin = jnp.where(lax.rem(number, 2) == 1, at - distance, at + distance)
+
+        @pl.when((origin >= 0) & (origin < depth))
+        def _():
+            piece(jnp.clip(origin, 0, depth - 1))
+
+    stores = [
+        pltpu.make_async_copy(pre_v, pre_hbm, store_sem.at[3]),
+        pltpu.make_async_copy(two_v, all_two_hbm, store_sem.at[4]),
+        pltpu.make_async_copy(grad_one_v, grad_one_hbm, store_sem.at[5]),
+    ]
+    for store in stores:
+        store.start()
+    attn.arrive(1)
+    attn.start(2)
+    sum_one.start(1)
+    attn.arrive(2)
+    attn.start(3)
+    sum_two.start(2)
+    own_attn.wait()
+    hidden_out.wait()
+    grad_two_out.wait()
+    for store in stores:
+        store.wait()
+    attn.arrive(3)
+    sum_two.arrive(1, True)
+    sum_two.arrive(2, False)
+    sum_one.arrive(1, False)
+    for step in (2, 3):
+        two.sent(step)
+    for step in (1, 2, 3):
+        attn.sent(step)
+    sum_two.sent(1)
+    sum_two.sent(2)
+    sum_one.sent(1)
+
+
+def feed_forward(normed, up, one, two, columns, full):
+    size, depth = lax.axis_size("seq"), lax.axis_size("fsdp")
+    micro, _, length, width = normed.shape
+    units, cols = one.shape[-1], width // size
+    rows = width // (size * depth)
+    count = micro * size * length
+    dims = (size, depth, micro, length, width, units, cols)
+    hbm = pl.BlockSpec(memory_space=pl.ANY)
+    vmem = pl.BlockSpec(memory_space=pltpu.VMEM)
+    dma = pltpu.SemaphoreType.DMA
+    sums = dma((2 * depth,))
+    shape = jax.ShapeDtypeStruct
+    tall, deep = (depth, units // depth, width), (size, depth, rows, units)
+    return pl.pallas_call(
+        functools.partial(ffn_kernel, dims),
+        in_specs=[hbm] * 5 + [vmem],
+        out_specs=[hbm] * 8 + [vmem],
+        out_shape=[
+            shape((count, units), BF),
+            shape((count, units), BF),
+            shape(tall, BF),
+            shape((size, depth, rows, 4 * cols), BF),
+            shape(tall, BF),
+            shape(deep, BF),
+            shape((4,) + tall[1:], BF),
+            shape((2, size, rows, units), BF),
+            shape((1, units), F32),
+        ],
+        scratch_shapes=[
+            pltpu.VMEM((count, width), BF),
+            pltpu.VMEM((count, width), BF),
+            pltpu.VMEM(deep, BF),
+            pltpu.VMEM(tall, BF),
+            pltpu.VMEM((count, units), BF),
+            pltpu.VMEM((count, units), BF),
+            pltpu.VMEM(tall, BF),
+            pltpu.VMEM(deep, BF),
+            pltpu.VMEM(tall[1:], BF),
+            pltpu.VMEM(tall[1:], BF),
+            pltpu.VMEM((2,) + tall[1:], BF),
+            dma((6,)),
+            dma((2,)),
+            dma((6,)),
+        ]
+        + [sums] * 8,
+        compiler_params=pltpu.CompilerParams(
+            collective_id=2, has_side_effects=True, vmem_limit_bytes=60 * 1024 * 1024
+        ),
+        cost_estimate=pl.CostEstimate(
+            flops=34 * 1000**3, bytes_accessed=300 * 1000 * 1000, transcendentals=0
+        ),
+    )(normed.reshape(count, width), up.reshape(count, width), one, two, columns, full)
+
+
+def attn_layer_kernel(
+    dims,
+    starts_ref,
+    cos_ref,
+    sin_ref,
+    normed_hbm,
+    up_hbm,
+    attn_hbm,
+    grad_two_hbm,
+    grad_one_hbm,
+    old_two,
+    old_one,
+    full_ref,
+    turned_hbm,
+    mixed_hbm,
+    grads_hbm,
+    one_hbm,
+    land_two,
+    land_one,
+    bqkv_ref,
+    two_ref,
+    normed_v,
+    up_v,
+    attn_v,
+    natural_v,
+    turned_v,
+    mixed_v,
+    grads_v,
+    dk_s,
+    dv_s,
+    bias_s,
+    own_two,
+    held_two,
+    out_two,
+    own_one,
+    held_one,
+    out_one,
+    load_sem,
+    line_load,
+    store_sem,
+    sum_two_send,
+    sum_two_recv,
+    sum_one_send,
+    sum_one_recv,
+):
+    size, depth, micro, length, width, units, cols = dims
+    me = lax.axis_index("seq")
+    chips = size // 2
+    groups = cols // LANES
+    total = size * length
+    count = micro * total
+    per = width // size
+    loads = [
+        pltpu.make_async_copy(src, dst, load_sem.at[n])
+        for n, (src, dst) in enumerate(
+            ((normed_hbm, normed_v), (attn_hbm, attn_v), (up_hbm, up_v))
+        )
+    ]
+    for load in loads:
+        load.start()
+    greet(size, depth)
+    sum_two = LineSum(
+        depth,
+        lambda o: grad_two_hbm.at[o],
+        lambda step, way: (
+            old_two.at[(step - 1) * 2 + (way > 0)] if step < 3 else land_two.at[int(way > 0)]
+        ),
+        own_two,
+        held_two,
+        lambda step, way: out_two.at[int(way > 0)],
+        line_load,
+        sum_two_send,
+        sum_two_recv,
+    )
+    sum_one = LineSum(
+        depth,
+        lambda o: grad_one_hbm.at[:, o],
+        lambda step, way: (
+            old_one.at[int(way > 0)] if step < 2 else land_one.at[(step - 2) * 2 + (way > 0)]
+        ),
+        own_one,
+        held_one,
+        lambda step, way: out_one.at[(step - 2) * 2 + (way > 0)],
+        line_load,
+        sum_one_send,
+        sum_one_recv,
+    )
+    sum_two.start(3, here=False)
+    sum_one.start(2, here=False)
+    for load in loads:
+        load.wait()
+
+    lane = lax.broadcasted_iota(jnp.int32, (1, LANES), 1)
+    low_lane = (lane % HEAD_DIM) < (ROT // 2)
+    over_first = (((0,), (0,)), ((), ()))
+    over_last = (((1,), (1,)), ((), ()))
+
+    def turn(value, cosine, sine):
+        other = jnp.where(
+            low_lane,
+            pltpu.roll(value, LANES - ROT // 2, 1),
+            pltpu.roll(value, ROT // 2, 1),
+        )
+        return value * cosine + other * sine
+
+    high = chips * length
+
+    @pl.loop(0, micro * 2)
+    def _(r):
+        m, parity = r // 2, lax.rem(r, 2)
+        rows = pl.ds(pl.multiple_of(r * high, high), high)
+        a = normed_v[rows, :]
+        u = up_v[rows, :]
+        for part in range(3):
+            w = attn_v[:, :, :, part * cols : (part + 1) * cols].reshape(width, cols)
+            y = jnp.dot(a, w, preferred_element_type=F32)
+            y = y + full_ref[2 + part : 3 + part, pl.ds(pl.multiple_of(me * cols, cols), cols)]
+            for block in range(chips):
+                at = pl.ds(pl.multiple_of((block * 2 + parity) * length, length), length)
+                cosine, sine = cos_ref[at, :], sin_ref[at, :]
+                for g in range(groups):
+                    v = y[block * length : (block + 1) * length, g * LANES : (g + 1) * LANES]
+                    if part < 2:
+                        v = turn(v, cosine, sine)
+                    v = v.astype(BF)
+                    if part == 0:
+                        v = v * jnp.asarray(SCALE, BF)
+                    natural_v[part, m, g, at, :] = v
+        y = jnp.zeros((high, cols), F32)
+        for s in range(size):
+            w = attn_v[s, :, :, 3 * cols :].reshape(cols, cols)
+            y = y + lax.dot_general(
+                u[:, s * per : (s + 1) * per], w, over_last, preferred_element_type=F32
+            )
+        for block in range(chips):
+            at = pl.ds(pl.multiple_of((block * 2 + parity) * length, length), length)
+            for g in range(groups):
+                v = y[block * length : (block + 1) * length, g * LANES : (g + 1) * LANES]
+                natural_v[3, m, g, at, :] = v.astype(BF)
+
+    tile = 256
+
+    @pl.loop(0, micro * groups)
+    def _(index):
+        m, g = index // groups, lax.rem(index, groups)
+
+        @pl.when(index == micro * groups - 1)
+        def _():
+            sum_one.start(3)
+
+        def label(positions):
+            found = jnp.full(positions.shape, -1, jnp.int32)
+            for piece in range(PIECES):
+                start = starts_ref[m, piece]
+                found = jnp.where((positions >= start) & (positions < start + IMG), piece, found)
+            return found
+
+        def put(target, at, columns, value):
+            for part in range(value.shape[0] // length):
+                block = at // length + part
+                rows = m * total + store_index(block) * length
+                target[pl.ds(pl.multiple_of(rows, length), length), columns] = value[
+                    part * length : (part + 1) * length
+                ].astype(BF)
+
+        def columns_of(part):
+            return pl.ds(pl.multiple_of(part * cols + g * LANES, LANES), LANES)
+
+        dk_s[...] = jnp.zeros_like(dk_s)
+        dv_s[...] = jnp.zeros_like(dv_s)
+        for first in range(0, total, tile):
+            last = min(total, first + tile + IMG)
+            qpos = first + lax.broadcasted_iota(jnp.int32, (tile, 1), 0)
+            kpos = first + lax.broadcasted_iota(jnp.int32, (1, last - first), 1)
+            qlab, klab = label(qpos), label(kpos)
+            allowed = (kpos <= qpos) | ((qlab == klab) & (qlab >= 0))
+            bias_s[:, : last - first] = jnp.where(allowed, 0.0, -1e30)
+            rows = slice(first, first + tile)
+            keys = natural_v[1, m, g, :last, :]
+            values = natural_v[2, m, g, :last, :]
+            mixed = jnp.zeros((tile, LANES), F32)
+            dq = jnp.zeros((tile, LANES), F32)
+            for head in range(LANES // HEAD_DIM):
+                mine = (lane // HEAD_DIM) == head
+                q = jnp.where(mine, natural_v[0, m, g, rows, :], 0)
+                do = jnp.where(mine, natural_v[3, m, g, rows, :], 0)
+                s = lax.dot_general(q, keys, over_last, preferred_element_type=F32)
+                if first:
+                    s = jnp.concatenate(
+                        [s[:, :first], s[:, first:] + bias_s[:, : last - first]], axis=1
+                    )
+                else:
+                    s = s + bias_s[:, : last - first]
+                p = jnp.exp(s - jnp.max(s, axis=1, keepdims=True))
+                p = p * (1.0 / jnp.sum(p, axis=1, keepdims=True))
+                probs = p.astype(BF)
+                att = jnp.dot(probs, values, preferred_element_type=F32)
+                mixed = jnp.where(mine, att, mixed)
+                dp = lax.dot_general(do, values, over_last, preferred_element_type=F32)
+                delta = jnp.sum(p * dp, axis=1, keepdims=True)
+                ds = (p * (dp - delta)).astype(BF)
+                dq = jnp.where(mine, jnp.dot(ds, keys, preferred_element_type=F32), dq)
+                dk_s[:last, :] += lax.dot_general(ds, q, over_first, preferred_element_type=F32)
+                dv_s[:last, :] += lax.dot_general(
+                    probs, do, over_first, preferred_element_type=F32
+                )
+            put(mixed_v, first, pl.ds(pl.multiple_of(g * LANES, LANES), LANES), mixed)
+            dq = turn(dq * SCALE, cos_ref[rows, :], -sin_ref[rows, :])
+            put(turned_v, first, columns_of(0), dq)
+        put(turned_v, 0, columns_of(1), turn(dk_s[...], cos_ref[...], -sin_ref[...]))
+        put(turned_v, 0, columns_of(2), dv_s[...])
+
+    stores = [
+        pltpu.make_async_copy(turned_v, turned_hbm, store_sem.at[0]),
+        pltpu.make_async_copy(mixed_v, mixed_hbm, store_sem.at[1]),
+    ]
+    for store in stores:
+        store.start()
+
+    wide = 512
+
+    @pl.loop(0, width // wide)
+    def _(d):
+        rows = pl.ds(pl.multiple_of(d * wide, wide), wide)
+        y = lax.dot_general(normed_v[:, rows], turned_v[...], over_first, preferred_element_type=F32)
+        n = wide // per
+        grads_v[pl.ds(d * n, n), :, :, : 3 * cols] = y.astype(BF).reshape(
+            n, depth, per // depth, 3 * cols
+        )
+        y = lax.dot_general(mixed_v[...], up_v[:, rows], over_first, preferred_element_type=F32)
+        y = y.astype(BF)
+        for k in range(n):
+            grads_v[d * n + k, :, :, 3 * cols :] = y[:, k * per : (k + 1) * per].reshape(
+                depth, cols // depth, per
+            )
+
+    grads_out = pltpu.make_async_copy(grads_v, grads_hbm, store_sem.at[2])
+    grads_out.start()
+    bqkv_ref[...] = jnp.sum(turned_v[...].astype(F32), axis=0, keepdims=True)
+    sum_two.sent(3)
+    two_ref[...] = sum_two.total(3, held_two, out_two.at[0])
+    sum_one.sent(2)
+    one_sum = sum_one.total(3, held_one, out_one.at[0])
+    out_one[1] = one_sum.astype(BF)
+    one_out = pltpu.make_async_copy(out_one.at[1], one_hbm, store_sem.at[3])
+    one_out.start()
+    for store in stores:
+        store.wait()
+    grads_out.wait()
+    one_out.wait()
+    sum_one.sent(3)
+
+
+def attention_layer(starts, normed, up, attn, grad_two, grad_one, old_two, old_one, full):
+    size, depth, rows, units = grad_one.shape
+    micro, _, length, width = normed.shape
+    cols = width // size
+    count, total = micro * size * length, size * length
+    dims = (size, depth, micro, length, width, units, cols)
+    cosine, sine = tables(total)
+    hbm = pl.BlockSpec(memory_space=pl.ANY)
+    vmem = pl.BlockSpec(memory_space=pltpu.VMEM)
+    dma = pltpu.SemaphoreType.DMA
+    sums = dma((2 * depth,))
+    shape = jax.ShapeDtypeStruct
+    tall, deep = (units // depth, width), (size, rows, units)
+    return pl.pallas_call(
+        functools.partial(attn_layer_kernel, dims),
+        in_specs=[pl.BlockSpec(memory_space=pltpu.SMEM)] + [vmem] * 2 + [hbm] * 7 + [vmem],
+        out_specs=[hbm] * 6 + [vmem] * 2,
+        out_shape=[
+            shape((count, 3 * cols), BF),
+            shape((count, cols), BF),
+            shape(attn.shape, BF),
+            shape(deep, BF),
+            shape((2,) + tall, BF),
+            shape((4,) + deep, BF),
+            shape((1, 3 * cols), F32),
+            shape(tall, F32),
+        ],
+        scratch_shapes=[
+            pltpu.VMEM((count, width), BF),
+            pltpu.VMEM((count, width), BF),
+            pltpu.VMEM(attn.shape, BF),
+            pltpu.VMEM((4, micro, cols // LANES, total, LANES), BF),
+            pltpu.VMEM((count, 3 * cols), BF),
+            pltpu.VMEM((count, cols), BF),
+            pltpu.VMEM(attn.shape, BF),
+            pltpu.VMEM((total, LANES), F32),
+            pltpu.VMEM((total, LANES), F32),
+            pltpu.VMEM((256, 512), F32),
+            pltpu.VMEM(tall, BF),
+            pltpu.VMEM(tall, BF),
+            pltpu.VMEM((2,) + tall, BF),
+            pltpu.VMEM(deep, BF),
+            pltpu.VMEM(deep, BF),
+            pltpu.VMEM((4,) + deep, BF),
+            dma((3,)),
+            dma((2,)),
+            dma((4,)),
+        ]
+        + [sums] * 4,
+        compiler_params=pltpu.CompilerParams(
+            collective_id=3, has_side_effects=True, vmem_limit_bytes=60 * 1024 * 1024
+        ),
+        cost_estimate=pl.CostEstimate(
+            flops=40 * 1000**3, bytes_accessed=300 * 1000 * 1000, transcendentals=0
+        ),
+    )(
+        starts,
+        cosine,
+        sine,
+        normed.reshape(count, width),
+        up.reshape(count, width),
+        attn,
+        grad_two,
+        grad_one,
+        old_two,
+        old_one,
+        full,
+    )
+
+
+def close_kernel(
+    dims,
+    tokens_hbm,
+    up_hbm,
+    grads_hbm,
+    attn_hbm,
+    one_hbm,
+    two_hbm,
+    turned_hbm,
+    pre_hbm,
+    mixed_hbm,
+    hidden_hbm,
+    one_sum_hbm,
+    full_ref,
+    bqkv_ref,
+    bone_ref,
+    act_ref,
+    ingrad_ref,
+    qkv_ref,
+    out_ref,
+    vec_ref,
+    one_out_hbm,
+    landing,
+    tokens_v,
+    up_v,
+    attn_v,
+    one_v,
+    two_v,
+    turned_v,
+    pre_v,
+    mixed_v,
+    hidden_v,
+    to_core,
+    sums,
+    coming,
+    line_a,
+    line_b,
+    line_out,
+    total_v,
+    spread_v,
+    one_land,
+    one_wide,
+    vec_in,
+    load_sem,
+    core_send,
+    core_recv,
+    axis_send,
+    axis_recv,
+    line_load,
+    line_send,
+    line_recv,
+    a2a_send,
+    a2a_recv,
+    vec_send,
+    vec_recv,
+    one_send,
+    one_recv,
+    wide_sem,
+):
+    size, depth, micro, length, width, units, cols = dims
+    me, at = lax.axis_index("seq"), lax.axis_index("fsdp")
+    count = size.bit_length() - 1
+    chips = size // 2
+    chip, core = me >> 1, me & 1
+    half = width // 2
+    per = width // size
+
+    loads = [
+        pltpu.make_async_copy(src, dst, load_sem.at[n])
+        for n, (src, dst) in enumerate(
+            (
+                (turned_hbm, turned_v),
+                (attn_hbm, attn_v),
+                (pre_hbm, pre_v),
+                (one_hbm, one_v),
+                (hidden_hbm, hidden_v),
+                (two_hbm, two_v),
+                (mixed_hbm, mixed_v),
+                (tokens_hbm, tokens_v),
+                (up_hbm, up_v),
+            )
+        )
+    ]
+    for load in loads:
+        load.start()
+    greet(size, depth)
+
+    def line_copy(step, way, part, src):
+        number = (step * 2 + (way > 0)) * 2 + part
+        return remote(
+            src,
+            landing.at[number],
+            line_send.at[number],
+            line_recv.at[number],
+            {"fsdp": jnp.clip(at + way, 0, depth - 1)},
+        )
+
+    def place_of(way):
+        return at if way > 0 else depth - 1 - at
+
+    def chunk(origin, part):
+        return grads_hbm.at[pl.ds(part * chips, chips), origin]
+
+    def line_step(step):
+        for part in range(2):
+            for way in (1, -1):
+                place = place_of(way)
+                away = jnp.clip(depth - step + place, 0, depth - 1)
+                origin = away if way > 0 else depth - 1 - away
+                slot = (way > 0) * 2 + part
+
+                @pl.when(place == 0)
+                def _():
+                    line_copy(step, way, part, chunk(origin, part)).start()
+
+                if step > 1:
+
+                    @pl.when((place >= 1) & (place <= step - 1) & (place < depth - 1))
+                    def _():
+                        mine = pltpu.make_async_copy(
+                            chunk(origin, part), line_a.at[0], line_load.at[0]
+                        )
+                        mine.start()
+                        arrived = line_copy(step - 1, way, part, line_out.at[slot])
+                        arrived.wait_recv()
+                        came = pltpu.make_async_copy(
+                            landing.at[((step - 1) * 2 + (way > 0)) * 2 + part],
+                            line_b.at[0],
+                            line_load.at[1],
+                        )
+                        came.start()
+
+                        @pl.when(place <= step - 2)
+                        def _():
+                            arrived.wait_send()
+
+                        mine.wait()
+                        came.wait()
+                        line_out[slot] = (
+                            line_a[0].astype(F32) + line_b[0].astype(F32)
+                        ).astype(BF)
+                        line_copy(step, way, part, line_out.at[slot]).start()
+
+    def line_finish(part):
+        mine = pltpu.make_async_copy(chunk(at, part), line_a.at[0], line_load.at[0])
+        mine.start()
+        for way in (1, -1):
+            place = place_of(way)
+            slot = int(way > 0)
+
+            @pl.when(place >= 1)
+            def _():
+                line_copy(depth - 1, way, part, line_out.at[0]).wait_recv()
+                came = pltpu.make_async_copy(
+                    landing.at[((depth - 1) * 2 + (way > 0)) * 2 + part],
+                    line_b.at[slot],
+                    line_load.at[1],
+                )
+                came.start()
+                came.wait()
+
+            @pl.when(place == 0)
+            def _():
+                line_b[slot] = jnp.zeros_like(line_b[slot])
+
+        mine.wait()
+        summed = line_a[0].astype(F32) + line_b[0].astype(F32) + line_b[1].astype(F32)
+        total_v[pl.ds(part * chips, chips)] = summed.astype(BF)
+        for block in range(chips):
+            out_ref[:, (part * chips + block) * cols : (part * chips + block + 1) * cols] = summed[
+                block, :, 3 * cols :
+            ]
+
+    def line_sent():
+        for part in range(2):
+            for way in (1, -1):
+                place = place_of(way)
+
+                @pl.when(place == 0)
+                def _():
+                    for step in range(1, depth):
+                        line_copy(step, way, part, line_out.at[0]).wait_send()
+
+                @pl.when((place >= 1) & (place < depth - 1))
+                def _():
+                    line_copy(depth - 1, way, part, line_out.at[0]).wait_send()
+
+    def back_copy(step):
+        peer = me ^ step
+        return remote(
+            total_v.at[peer, :, pl.ds(0, 3 * cols)],
+            spread_v.at[me],
+            a2a_send.at[step],
+            a2a_recv.at[step],
+            {"seq": peer},
+        )
+
+    def one_copy(step):
+        peer = me ^ step
+        return remote(
+            one_sum_hbm.at[peer],
+            one_land.at[me],
+            one_send.at[step],
+            one_recv.at[step],
+            {"seq": peer},
+        )
+
+    one_mine = pltpu.make_async_copy(one_sum_hbm.at[me], one_land.at[me], one_recv.at[0])
+
+    def one_widen():
+        one_mine.wait()
+        for step in range(1, size):
+            one_copy(step).wait_recv()
+
+        def copy(block, slot):
+            at = pl.ds(pl.multiple_of(block * units, units), units)
+            return pltpu.make_async_copy(
+                one_wide.at[slot], one_out_hbm.at[:, at], wide_sem.at[slot]
+            )
+
+        for block in range(size):
+            slot = block % 2
+            if block >= 2:
+                copy(block - 2, slot).wait()
+            one_wide[slot] = one_land[block].astype(F32)
+            copy(block, slot).start()
+        for block in range(size - 2, size):
+            copy(block, block % 2).wait()
+
+    def core_copy(array, m):
+        number = array * micro + m
+        return remote(
+            to_core.at[m],
+            sums.at[number],
+            core_send.at[number],
+            core_recv.at[number],
+            {"seq": me ^ 1},
+        )
+
+    orders = (list(range(count - 1)), list(range(count - 1))[::-1])
+
+    def stage_copies(array, m, part, stage):
+        bit = orders[part][stage]
+        done = sum(1 << b for b in orders[part][:stage])
+        first = chips - (chips >> stage)
+        columns = slice(part * half, (part + 1) * half)
+        found = []
+        for mask in range(chips):
+            if mask & (done | (1 << bit)):
+                continue
+            slot = first + len(found)
+            number = ((array * micro + m) * 2 + part) * (chips - 1) + slot
+            copy = remote(
+                sums.at[array * micro + m, chip ^ (mask | (1 << bit)), :, columns],
+                coming.at[array * micro + m, slot, :, columns],
+                axis_send.at[number],
+                axis_recv.at[number],
+                {"seq": me ^ (2 << bit)},
+            )
+            found.append((mask, slot, copy))
+        return found
+
+    def stage_start(array, m, stage):
+        for part in range(2):
+            for _, _, copy in stage_copies(array, m, part, stage):
+                copy.start()
+
+    def stage_add(array, m, stage):
+        number = array * micro + m
+        for part in range(2):
+            columns = slice(part * half, (part + 1) * half)
+            for mask, slot, copy in stage_copies(array, m, part, stage):
+                copy.wait_recv()
+                if stage < count - 2:
+                    block = chip ^ mask
+                    sums[number, block, :, columns] = (
+                        sums[number, block, :, columns].astype(F32)
+                        + coming[number, slot, :, columns].astype(F32)
+                    ).astype(BF)
+
+    def stage_last(array, m):
+        number = array * micro + m
+        return sums[number, chip].astype(F32) + coming[number, chips - 2].astype(F32)
+
+    over_last = (((1,), (1,)), ((), ()))
+
+    def grad_terms(m, parity, write):
+        first = parity * chips
+        turned = turned_v[m, pl.ds(first, chips)].reshape(chips * length, 3 * cols)
+        pre = pre_v[m, pl.ds(first, chips)].reshape(chips * length, units)
+
+        @pl.loop(0, size)
+        def _(s):
+            w = attn_v[s, :, :, : 3 * cols].reshape(per, 3 * cols)
+            y = lax.dot_general(turned, w, over_last, preferred_element_type=F32)
+            w = one_v[s].reshape(per, units)
+            y = y + lax.dot_general(pre, w, over_last, preferred_element_type=F32)
+            write(pl.ds(pl.multiple_of(s * per, per), per), y.reshape(chips, length, per))
+
+    def act_terms(m, parity, write):
+        first = parity * chips
+        mixed = mixed_v[m, pl.ds(first, chips)].reshape(chips * length, cols)
+        hidden = hidden_v[m, pl.ds(first, chips)].reshape(chips * length, units)
+
+        @pl.loop(0, size)
+        def _(s):
+            columns = pl.ds(pl.multiple_of(s * per, per), per)
+            w = attn_v[s, :, :, 3 * cols :].reshape(per, cols)
+            y = jnp.dot(mixed, w, preferred_element_type=F32)
+            w = two_v[:, :, columns].reshape(units, per)
+            y = y + jnp.dot(hidden, w, preferred_element_type=F32)
+            write(columns, y.reshape(chips, length, per))
+
+    def terms_away(array, m, function):
+        if array:
+            core_copy(0, m).wait_send()
+
+        def write(columns, y):
+            to_core[m, :, :, columns] = y.astype(BF)
+
+        function(m, 1 - core, write)
+        core_copy(array, m).start()
+
+    def terms_here(array, m, function):
+        core_copy(array, m).wait_recv()
+        number = array * micro + m
+
+        def write(columns, y):
+            sums[number, :, :, columns] = (y + sums[number, :, :, columns].astype(F32)).astype(BF)
+
+        function(m, core, write)
+        stage_start(array, m, 0)
+
+    gain = full_ref[0:1, :]
+    vec_ref[...] = jnp.zeros_like(vec_ref)
+    for part in range(3):
+        columns = pl.ds(pl.multiple_of(me * cols, cols), cols)
+        vec_ref[2 + part : 3 + part, columns] = bqkv_ref[:, part * cols : (part + 1) * cols]
+    bone_at = pl.multiple_of(lax.rem(me * units, width), units)
+    vec_ref[pl.ds(6 + me * units // width, 1), pl.ds(bone_at, units)] = bone_ref[...]
+
+    def norm_back(m):
+        x = tokens_v[m].astype(F32)
+        dy = stage_last(0, m)
+        center = x - jnp.mean(x, axis=-1, keepdims=True)
+        spread = jnp.mean(center * center, axis=-1, keepdims=True)
+        r = lax.rsqrt(spread + EPSILON)
+        xhat = center * r
+        g = dy * gain
+        inner = g - jnp.mean(g, axis=-1, keepdims=True)
+        inner = inner - xhat * jnp.mean(g * xhat, axis=-1, keepdims=True)
+        upstream = up_v[m].astype(F32)
+        ingrad_ref[m] = upstream + r * inner
+        vec_ref[5:6, :] += jnp.sum(upstream, axis=0, keepdims=True)
+        vec_ref[0:1, :] += jnp.sum(dy * xhat, axis=0, keepdims=True)
+        vec_ref[1:2, :] += jnp.sum(dy, axis=0, keepdims=True)
+
+    def act_out(m):
+        bias = full_ref[5:6, :] + full_ref[6 + size * units // width : 7 + size * units // width, :]
+        total = tokens_v[m].astype(F32) + stage_last(1, m) + bias
+        act_ref[m] = total.astype(BF)
+
+    levels = [("seq", 1 << bit) for bit in range(count)]
+    levels = levels + [("fsdp", 1 << bit) for bit in range(depth.bit_length() - 1)]
+
+    def vec_copy(level):
+        axis, step = levels[level]
+        mine = me if axis == "seq" else at
+        return remote(
+            vec_ref,
+            vec_in.at[level],
+            vec_send.at[level],
+            vec_recv.at[level],
+            {axis: mine ^ step},
+        )
+
+    def vec_level(level):
+        copy = vec_copy(level)
+        copy.wait()
+        vec_ref[...] += vec_in[level]
+        if level + 1 < len(levels):
+            vec_copy(level + 1).start()
+
+    one_mine.start()
+    for step in range(1, size):
+        one_copy(step).start()
+    line_step(1)
+    for load in loads[:4]:
+        load.wait()
+    for m in range(micro):
+        terms_away(0, m, grad_terms)
+    for m in range(micro):
+        terms_here(0, m, grad_terms)
+    line_step(2)
+    for load in loads[4:]:
+        load.wait()
+    stage_add(0, 0, 0)
+    stage_start(0, 0, 1)
+    for m in range(micro):
+        terms_away(1, m, act_terms)
+    stage_add(0, 1, 0)
+    stage_start(0, 1, 1)
+    for m in range(micro):
+        terms_here(1, m, act_terms)
+    one_widen()
+    stage_add(0, 0, 1)
+    norm_back(0)
+    line_step(3)
+    stage_add(0, 1, 1)
+    norm_back(1)
+    vec_copy(0).start()
+    stage_add(1, 0, 0)
+    stage_start(1, 0, 1)
+    vec_level(0)
+    vec_level(1)
+    stage_add(1, 1, 0)
+    stage_start(1, 1, 1)
+    vec_level(2)
+    vec_level(3)
+    stage_add(1, 0, 1)
+    act_out(0)
+    vec_level(4)
+    stage_add(1, 1, 1)
+    act_out(1)
+    for part in range(2):
+        line_finish(part)
+        for step in range(1, size):
+            peer = me ^ step
+
+            @pl.when((peer >= part * chips) & (peer < (part + 1) * chips))
+            def _():
+                back_copy(step).start()
+
+    def put(block, values):
+        for part in range(3):
+            start = pl.multiple_of(part * width + block * cols, cols)
+            qkv_ref[:, pl.ds(start, cols)] = values[:, part * cols : (part + 1) * cols]
+
+    put(me, total_v[me, :, : 3 * cols].astype(F32))
+    for step in range(1, size):
+        back_copy(step).wait_recv()
+        put(me ^ step, spread_v[me ^ step].astype(F32))
+
+    line_sent()
+    for step in range(1, size):
+        back_copy(step).wait_send()
+        one_copy(step).wait_send()
+    for m in range(micro):
+        core_copy(1, m).wait_send()
+        for array in range(2):
+            for part in range(2):
+                for stage in range(count - 1):
+                    for _, _, copy in stage_copies(array, m, part, stage):
+                        copy.wait_send()
+
+
+def close_layer(
+    tokens, upstream, grads, attn, one, two, turned, pre, mixed, hidden, one_sum, full, bqkv, bone
+):
+    size, depth = lax.axis_size("seq"), lax.axis_size("fsdp")
+    micro, length, width = tokens.shape
+    units, cols = one.shape[-1], width // size
+    rows = width // (size * depth)
+    dims = (size, depth, micro, length, width, units, cols)
+    chips, count = size // 2, size.bit_length() - 1
+    hbm = pl.BlockSpec(memory_space=pl.ANY)
+    vmem = pl.BlockSpec(memory_space=pltpu.VMEM)
+    dma = pltpu.SemaphoreType.DMA
+    levels = count + depth.bit_length() - 1
+    piece = (chips, rows, 4 * cols)
+    loaded = (tokens, upstream, attn, one, two, turned, pre, mixed, hidden)
+    return pl.pallas_call(
+        functools.partial(close_kernel, dims),
+        in_specs=[hbm] * 11 + [vmem] * 3,
+        out_specs=[vmem] * 5 + [hbm] * 2,
+        out_shape=[
+            jax.ShapeDtypeStruct(tokens.shape, BF),
+            jax.ShapeDtypeStruct(tokens.shape, F32),
+            jax.ShapeDtypeStruct((rows, 3 * width), F32),
+            jax.ShapeDtypeStruct((rows, width), F32),
+            jax.ShapeDtypeStruct(full.shape, F32),
+            jax.ShapeDtypeStruct((rows, size * units), F32),
+            jax.ShapeDtypeStruct((4 * depth,) + piece, BF),
+        ],
+        scratch_shapes=[pltpu.VMEM(v.shape, BF) for v in loaded]
+        + [
+            pltpu.VMEM((micro, chips, length, width), BF),
+            pltpu.VMEM((2 * micro, chips, length, width), BF),
+            pltpu.VMEM((2 * micro, chips - 1, length, width), BF),
+            pltpu.VMEM((1,) + piece, BF),
+            pltpu.VMEM((2,) + piece, BF),
+            pltpu.VMEM((4,) + piece, BF),
+            pltpu.VMEM((size, rows, 4 * cols), BF),
+            pltpu.VMEM((size, rows, 3 * cols), BF),
+            pltpu.VMEM(one_sum.shape, BF),
+            pltpu.VMEM((2,) + one_sum.shape[1:], F32),
+            pltpu.VMEM((levels,) + full.shape, F32),
+            dma((9,)),
+            dma((2 * micro,)),
+            dma((2 * micro,)),
+            dma((4 * micro * (chips - 1),)),
+            dma((4 * micro * (chips - 1),)),
+            dma((2,)),
+            dma((4 * depth,)),
+            dma((4 * depth,)),
+            dma((size,)),
+            dma((size,)),
+            dma((levels,)),
+            dma((levels,)),
+            dma((size,)),
+            dma((size,)),
+            dma((2,)),
+        ],
+        compiler_params=pltpu.CompilerParams(
+            collective_id=4, has_side_effects=True, vmem_limit_bytes=60 * 1024 * 1024
+        ),
+        cost_estimate=pl.CostEstimate(
+            flops=30 * 1000**3, bytes_accessed=300 * 1000 * 1000, transcendentals=0
+        ),
+    )(
+        tokens,
+        upstream,
+        grads,
+        attn,
+        one,
+        two,
+        turned,
+        pre,
+        mixed,
+        hidden,
+        one_sum,
+        full,
+        bqkv,
+        bone,
+    )[:6]
+
+
 def gelu_tanh(values):
     return jax.nn.gelu(values, approximate=True)
 
@@ -673,31 +1955,17 @@
         return mine + self.right.astype(F32) + self.left.astype(F32)
 
 
-def per_device(
-    tokens,
-    ln_gain,
-    ln_bias,
-    w_qkv,
-    b_qkv,
-    w_out,
-    b_out,
-    w_fc1,
-    b_fc1,
-    w_fc2,
-    b_fc2,
-    piece_starts,
-    cotangent,
+def staged_layer(
+    tokens, upstream, w_fc2, starts, normed, up, my_one, two_near, attn_cols, full, index
 ):
     size, depth = lax.axis_size("seq"), lax.axis_size("fsdp")
     me = lax.axis_index("seq")
-    micro, _, length, width = tokens.shape
+    micro, length, width = tokens.shape
     rows = width // (size * depth)
     hidden_rows = w_fc2.shape[0]
     cols = width // size
     units = hidden_rows * depth
     count = micro * size * length
-    tokens = tokens[:, 0]
-    upstream = cotangent[:, 0]
 
     def contract_last(left, right):
         return lax.dot_general(left, right, (((1,), (1,)), ((), ())), preferred_element_type=F32)
@@ -717,24 +1985,14 @@
             out = lax.dynamic_update_slice_in_dim(out, piece[None], origin, 0)
         return out
 
-    index = me * depth + lax.axis_index("fsdp")
-    packed = []
-    for vector in (ln_gain, ln_bias, b_qkv, b_out, b_fc1, b_fc2):
-        extent = vector.shape[0]
-        flat = jnp.zeros((extent * size * depth,), BF)
-        flat = lax.dynamic_update_slice(flat, vector, (index * extent,))
-        packed.append(flat.reshape(-1, width))
-    packed = jnp.concatenate(packed, axis=0)
-    packed = jnp.pad(packed, ((0, -packed.shape[0] % 16), (0, 0)))
-    normed, up, my_one, two_right, two_left, attn_cols, full = load_all(
-        tokens, upstream, w_fc1, w_fc2, w_qkv, w_out, packed
-    )
     normed = normed.reshape(count, width)
     up = up.reshape(count, width)
     my_one = my_one.reshape(width, units)
     two = Gather(w_fc2)
-    two.right.append(two_right)
-    two.left.append(two_left)
+    at = lax.axis_index("fsdp")
+    for way, found in ((-1, two.right), (1, two.left)):
+        origin = jnp.clip(at + way, 0, depth - 1)
+        found.append(lax.dynamic_index_in_dim(two_near, origin, 0, keepdims=False))
     gain, shift, bias_out = full[0], full[1], full[5]
     bias_qkv = lax.dynamic_slice_in_dim(full[2:5], me * cols, cols, 1).reshape(-1)
     ratio = size * units // width
@@ -772,14 +2030,12 @@
     )
     sum_two.step()
     attn.rest()
-    pieces = attn.pieces()
-    my_qkv = place_columns([(p[..., : 3 * cols], o) for p, o in pieces]).reshape(width, 3 * cols)
-    my_out = place_rows([(p[..., 3 * cols :].transpose(1, 0, 2), o) for p, o in pieces])
-    my_out = my_out.reshape(cols, width)
+    attn_weights = place_columns(attn.pieces())
+    my_qkv = attn_weights[..., : 3 * cols].reshape(width, 3 * cols)
+    my_out = attn_weights[..., 3 * cols :].transpose(1, 2, 0, 3).reshape(cols, width)
     projected = jnp.dot(normed, my_qkv, preferred_element_type=F32) + bias_qkv
     projected = projected.reshape(micro, size, length, 3 * cols)
     mixed_grad = contract_last(up, my_out).astype(BF).reshape(micro, size, length, cols)
-    starts = piece_starts[:, 0]
     parts = [attention(starts[:1], projected[:1], mixed_grad[:1])]
     (sum_one.right, sum_one.left), (projected, mixed_grad), parts = sum_two.fence(
         (sum_one.right, sum_one.left), (projected, mixed_grad), parts
@@ -798,27 +2054,29 @@
     grad_qkv, grad_out, (sum_two.right, sum_two.left) = sum_one.fence(
         grad_qkv, grad_out, (sum_two.right, sum_two.left)
     )
-
-    def attn_chunk(o):
-        return jnp.concatenate(
-            [
-                lax.dynamic_index_in_dim(grad_qkv, o, 1, keepdims=False),
-                lax.dynamic_index_in_dim(grad_out, o, 0, keepdims=False).transpose(1, 0, 2),
-            ],
-            axis=-1,
-        )
-
-    sum_attn = Scatter(attn_chunk)
-    sum_attn.step()
-    sum_one.rest()
-    sum_two.rest()
+    grad_attn = jnp.concatenate([grad_qkv, grad_out.transpose(2, 0, 1, 3)], axis=-1)
 
     def to_rows(mine, parts):
         mine = lax.all_to_all(mine.astype(BF), "seq", 0, 0, tiled=True).astype(F32)
         return mine.reshape(size, rows, parts, -1).transpose(1, 2, 0, 3).reshape(rows, -1)
 
+    sum_one.rest()
+    sum_two.rest()
     out_two = sum_two.total()
     out_one = to_rows(sum_one.total(), 1)
+
+    def put(values, extent, at):
+        return lax.dynamic_update_slice_in_dim(jnp.zeros(extent, F32), values, at, -1)
+
+    bqkv = jnp.sum(projected_grad.astype(F32), axis=0).reshape(3, cols)
+    bqkv = put(bqkv, (3, width), me * cols)
+    bone = put(jnp.sum(pre_grad.astype(F32), axis=0), (size * units,), me * units)
+    btwo = jnp.sum(upstream.astype(F32), axis=(0, 1))[None]
+    early = [jnp.zeros((2, width), F32), bqkv, btwo, bone.reshape(ratio, width)]
+    early = jnp.pad(jnp.concatenate(early), ((0, full.shape[0] - 6 - ratio), (0, 0)))
+
+    sum_attn = Scatter(lambda o: lax.dynamic_index_in_dim(grad_attn, o, 1, keepdims=False))
+    sum_attn.step()
     grad_terms = contract_last(projected_grad, my_qkv) + contract_last(pre_grad, my_one)
     grad_terms = grad_terms.astype(BF).reshape(micro, size, length, width)
     (grad_terms,) = sum_attn.fence(grad_terms)
@@ -836,36 +2094,100 @@
     _, norm_back = jax.vjp(layer_norm, tokens.astype(F32), gain, shift)
     input_grad, gain_grad, shift_grad = norm_back(normed_grad)
     input_grad = input_grad + upstream.astype(F32)
-
-    def put(values, extent, at):
-        return lax.dynamic_update_slice_in_dim(jnp.zeros(extent, F32), values, at, -1)
-
-    bqkv = jnp.sum(projected_grad.astype(F32), axis=0).reshape(3, cols)
-    bqkv = put(bqkv, (3, width), me * cols)
-    bone = put(jnp.sum(pre_grad.astype(F32), axis=0), (size * units,), me * units)
-    btwo = jnp.sum(upstream.astype(F32), axis=(0, 1))
-    packed = [gain_grad, shift_grad, bqkv[:2], bqkv[2], bone, btwo]
-    packed = [v.reshape(size, depth, -1) for v in packed]
-    summed = scatter_small(jnp.concatenate(packed, axis=-1))
-    vectors = []
-    start = 0
-    for v in packed:
-        vectors.append(summed[start : start + v.shape[-1]])
-        start += v.shape[-1]
+    vectors = early.at[:2].add(jnp.stack([gain_grad, shift_grad]))
+    vectors = lax.psum(vectors, ("seq", "fsdp"))
+
+    return activations, input_grad, out_qkv, out_out, vectors, out_one, out_two
+
+
+def per_device(
+    tokens,
+    ln_gain,
+    ln_bias,
+    w_qkv,
+    b_qkv,
+    w_out,
+    b_out,
+    w_fc1,
+    b_fc1,
+    w_fc2,
+    b_fc2,
+    piece_starts,
+    cotangent,
+):
+    size, depth = lax.axis_size("seq"), lax.axis_size("fsdp")
+    me = lax.axis_index("seq")
+    micro, _, length, width = tokens.shape
+    rows = width // (size * depth)
+    hidden_rows = w_fc2.shape[0]
+    cols = width // size
+    units = hidden_rows * depth
+    count = micro * size * length
+    tokens = tokens[:, 0]
+    upstream = cotangent[:, 0]
+
+    index = me * depth + lax.axis_index("fsdp")
+    packed = []
+    for vector in (ln_gain, ln_bias, b_qkv, b_out, b_fc1, b_fc2):
+        extent = vector.shape[0]
+        flat = jnp.zeros((extent * size * depth,), BF)
+        flat = lax.dynamic_update_slice(flat, vector, (index * extent,))
+        packed.append(flat.reshape(-1, width))
+    packed = jnp.concatenate(packed, axis=0)
+    packed = jnp.pad(packed, ((0, -packed.shape[0] % 16), (0, 0)))
+    starts = piece_starts[:, 0]
+    loaded = load_all(tokens, upstream, w_fc1, w_fc2, w_qkv, w_out, packed)
+    if (size, depth, micro) == (8, 4, 2):
+        normed, up, one, two_near, attn_cols, full = loaded
+        hidden, pre, two, attn, grad_two, grad_one, land_two, land_one, bone = feed_forward(
+            normed, up, one, two_near, attn_cols, full
+        )
+        turned, mixed, grads, one_sum, _, _, bqkv, out_two = attention_layer(
+            starts, normed, up, attn, grad_two, grad_one, land_two, land_one, full
+        )
+        wide = (micro, size, length, -1)
+        activations, input_grad, out_qkv, out_out, vectors, out_one = close_layer(
+            tokens,
+            upstream,
+            grads,
+            attn,
+            one,
+            two,
+            turned.reshape(wide),
+            pre.reshape(wide),
+            mixed.reshape(wide),
+            hidden.reshape(wide),
+            one_sum,
+            full,
+            bqkv,
+            bone,
+        )
+    else:
+        activations, input_grad, out_qkv, out_out, vectors, out_one, out_two = staged_layer(
+            tokens, upstream, w_fc2, starts, *loaded, index
+        )
+    ratio = w_fc1.shape[1] // width
+
+    def own(values):
+        values = values.reshape(-1)
+        extent = values.shape[0] // (size * depth)
+        return lax.dynamic_slice_in_dim(values, index * extent, extent, 0)
+
+    grad_b_two = own(vectors[5])
     return (
         activations[:, None],
         input_grad[:, None],
-        vectors[0],
-        vectors[1],
+        own(vectors[0]),
+        own(vectors[1]),
         out_qkv,
-        vectors[2],
-        vectors[3],
+        own(vectors[2:4]),
+        own(vectors[4]),
         out_out,
-        vectors[5],
+        grad_b_two,
         out_one,
-        vectors[4],
+        own(vectors[6 : 6 + ratio]),
         out_two,
-        vectors[5],
+        grad_b_two,
     )
 
 

time: 642 us -> 492 us (0.77)
  Pallas kernels: 162 us -> 449 us
  matrix products: 131 us -> 0 us
  starting transfers between devices: 101 us -> 0 us
  waiting for transfers between devices: 96.5 us -> 0 us
  other arithmetic: 61.2 us -> 0 us
  local copies, waits for them, and re-layouts: 79.2 us -> 32 us
    pallas_call x2 -> x3, Pallas kernels: 45.1 us -> 332 us  [the longest x1 124 us: feed_forward(): pl.pallas_call(functools.partial(ffn_kernel, dims), in_specs=[hbm] * 5 +...]
    dot_general x12 -> x0, matrix products: 131 us -> none  [the longest x4 44.4 us: contract_last(): lax.dot_general(left, right, (((1,), (1,)), ((), ())), preferred_element_...]
    ppermute x46 -> x0, waiting for transfers between devices: 96.5 us -> none  [the longest x14 36 us: line_left(): lax.ppermute(value, 'fsdp', [(last - i, last - i - 1) for i in senders])]
    ppermute x46 -> x0, starting transfers between devices: 79.3 us -> none  [the longest x14 39 us: line_right(): return lax.ppermute(value, 'fsdp', [(i, i + 1) for i in senders])]
    convert_element_type x18 -> x0, other arithmetic: 30.3 us -> none  [the longest x6 16 us: step(): coming = (coming.astype(F32) + self.left.astype(F32)).astype(BF)]
    all_to_all x2 -> x0, starting transfers between devices: 21.3 us -> none  [to_rows(): mine = lax.all_to_all(mine.astype(BF), 'seq', 0, 0, tiled=True).astype(F32)]
    slice x17 -> x1, local copies, waits for them, and re-layouts: 13 us -> 1.02 us  [per_device(): grad_b_two = own(vectors[5])]
    dynamic_slice x19 -> x4, local copies, waits for them, and re-layouts: 10.9 us -> 2.4 us  [own(): return lax.dynamic_slice_in_dim(values, index * extent, extent, 0)]
  transfers between devices with their start and end apart: 48 -> 0, of which waited for: 13 -> 0; matrix products, arithmetic and copies ran while one was open for 34% -> 0% of each run, Pallas kernels for 7% -> 0%
where the time goes in v3:
time: 492 us; the launch traced here: 482 us
  Pallas kernels  449 us (91%)
  local copies, waits for them, and re-layouts  32 us (7%)
    pallas_call x1, Pallas kernels, feed_forward(): pl.pallas_call(functools.partial(ffn_kernel, dims), in_specs=[hbm] * 5 +...  124 us
    pallas_call x1, Pallas kernels, close_layer(): pl.pallas_call(functools.partial(close_kernel, dims), in_specs=[hbm] * 11...  121 us
    pallas_call x1, Pallas kernels, load_all(): pl.pallas_call(functools.partial(load_kernel, dims), in_specs=[hbm] * 6 +...  117 us
    pallas_call x1, Pallas kernels, attention_layer(): pl.pallas_call(functools.partial(attn_layer_kernel, dims), in_specs=[pl.B...  86.8 us
    unnamed x39, local copies, waits for them, and re-layouts  23.1 us

profile of v3, /device:TPU:15, one launch (start us, length us, event | category | flops | bytes accessed | tf_op | source)
XLA Modules:
  0.0 482.0 jit_solution(6592787725770091746)
XLA Ops:
  0.7 0.9 dynamic_update_slice.25
  1.6 0.9 dynamic_update_slice.23
  2.4 0.9 dynamic_update_slice.22
  3.3 0.9 dynamic_update_slice.27
  4.2 0.9 dynamic_update_slice.24
  5.1 0.9 dynamic_update_slice.26
  6.0 0.2 concatenate.3
  6.2 0.0 copy-start
  6.2 1.2 copy-done
  7.4 0.0 copy-start.1
  7.4 1.2 copy-done.1
  8.6 0.0 copy-start.2
  8.6 1.2 copy-done.2
  9.9 0.0 copy-start.3
  9.9 1.2 copy-done.3
  11.1 0.0 copy-start.4
  11.1 1.1 copy-done.4
  12.2 0.0 copy-start.5
  12.2 0.9 copy-done.5
  13.2 117.2 %shard_map.246 = (bf16[2,8,128,2048]{3,2,1,0:T(8,128)(2,1)}, bf16[2,8,128,2048]{3,2,1,0:T(8,128)(2,1)}, bf16[8,4,64,1024]{3,2,1,0:T(8,128)(2,1)S(1)}, bf16[4,256...) custom-call(bf16[2,128,2048]{2,1,0:T(8,128)(2,1)S(1)} %bitcast.34, ...), custom_call_target="tpu_custom_call" | custom-call | flops 1000 | bytes 300000000 | tf_op jit(solution)/shard_map/pallas_call | solution.py:686
  130.4 0.0 copy-start.6
  130.4 1.9 copy-done.6
  132.3 0.0 copy-start.7
  132.3 1.0 copy-done.7
  133.3 0.0 copy-start.8
  133.3 0.7 copy-done.8
  133.9 123.9 %shard_map.247 = (bf16[2048,1024]{1,0:T(8,128)(2,1)}, bf16[2048,1024]{1,0:T(8,128)(2,1)}, bf16[4,256,2048]{2,1,0:T(8,128)(2,1)}, bf16[8,4,64,1024]{3,2,1,0:T(8,1...) custom-call(bf16[2048,2048]{1,0:T(8,128)(2,1)} %bitcast.45, ...), custom_call_target="tpu_custom_call" | custom-call | flops 33999998976 | bytes 300000000 | tf_op jit(solution)/shard_map/pallas_call | solution.py:972
  257.9 86.8 %shard_map.248 = (bf16[2048,768]{1,0:T(8,128)(2,1)}, bf16[2048,256]{1,0:T(8,128)(2,1)}, bf16[8,4,64,1024]{3,2,1,0:T(8,128)(2,1)}, bf16[8,64,1024]{2,1,0:T(8,128)...) custom-call(s32[2,2]{1,0:T(2,128)} %bitcast.49, ...), custom_call_target="tpu_custom_call" | custom-call | flops 40000000000 | bytes 300000000 | tf_op jit(solution)/shard_map/pallas_call | solution.py:1279
  344.7 120.9 %shard_map.249 = (bf16[2,128,2048]{2,1,0:T(8,128)(2,1)}, f32[2,128,2048]{2,1,0:T(8,128)}, f32[64,6144]{1,0:T(8,128)}, f32[64,2048]{1,0:T(8,128)}, f32[16,2048]{1...) custom-call(bf16[2,128,2048]{2,1,0:T(8,128)(2,1)} %bitcast.33, bf16[2,128,2048]{2,1,0:T(8,128)(2,1)} %bitcast.35, ...), custom_call_target="tpu_custom_call" | custom-call | flops 30000001024 | bytes 300000000 | tf_op jit(solution)/shard_map/pallas_call | solution.py:1807
  465.6 0.0 copy-start.11
  465.6 1.0 slice_bitcast_fusion.1
  466.6 0.6 dynamic_slice.30
  467.2 0.9 slice_bitcast_fusion
  468.1 1.0 fusion.4
  469.1 0.6 fusion.2
  469.7 0.0 copy-start.13
  469.7 0.6 fusion
  470.3 0.6 dynamic_slice.35
  470.9 0.5 copy.46
  471.4 2.3 copy.47
  473.7 0.0 copy-start.12
  473.7 0.0 copy-start.10
  473.7 3.3 copy.48
  477.0 0.0 copy-done.11
  477.0 0.0 copy-start.9
  477.0 1.1 copy.49
  478.2 0.0 copy-done.13
  478.2 0.0 copy-done.12
  478.2 0.8 copy.50
  479.0 0.0 copy-done.10
  479.0 1.3 copy.51
  480.3 0.0 copy-done.9
  480.3 1.3 copy.52
  (11 shorter events, 0.1 us)
Async XLA Ops:
  6.2 1.2 copy-start
  7.4 1.2 copy-start.1
  8.6 1.2 copy-start.2
  9.9 1.2 copy-start.3
  11.1 1.1 copy-start.4
  12.2 0.9 copy-start.5
  130.4 1.9 copy-start.6
  132.3 1.0 copy-start.7
  133.3 0.7 copy-start.8
  465.6 11.4 %copy-start.11 = (f32[64,6144]{1,0:T(8,128)S(1)}, f32[64,6144]{1,0:T(8,128)}, u32[]{:S(2)}) copy-start(f32[64,6144]{1,0:T(8,128)} %get-tuple-element.131) | copy-start | bytes 4718596
  469.7 8.5 %copy-start.13 = (f32[64]{0:T(128)}, f32[64]{0:T(128)S(1)}, u32[]{:S(2)}) copy-start(f32[64]{0:T(128)S(1)} %get-tuple-element.135) | copy-start | bytes 772
  473.7 4.4 copy-start.12
  473.7 5.2 %copy-start.10 = (f32[64,8192]{1,0:T(8,128)S(1)}, f32[64,8192]{1,0:T(8,128)}, u32[]{:S(2)}) copy-start(f32[64,8192]{1,0:T(8,128)} %get-tuple-element.136) | copy-start | bytes 6291460
  477.0 3.3 copy-start.9

commit v4 on v3

--- a/solution.py
+++ b/solution.py
@@ -305,35 +305,38 @@
             {"fsdp": jnp.clip(at + way, 0, self.depth - 1)},
         )
 
-    def start(self, step, here=True):
+    def origin(self, step, way):
+        away = jnp.clip(self.depth - step + self.place(way), 0, self.depth - 1)
+        return away if way > 0 else self.depth - 1 - away
+
+    def source(self, step):
+        for way in (1, -1):
+
+            @pl.when(self.place(way) == 0)
+            def _():
+                self.copy(step, way, self.chunk(self.origin(step, way))).start()
+
+    def forward(self, step, here=True):
         for way in (1, -1):
             place = self.place(way)
-            away = jnp.clip(self.depth - step + place, 0, self.depth - 1)
-            origin = away if way > 0 else self.depth - 1 - away
-
-            @pl.when(place == 0)
+
+            @pl.when((place >= 1) & (place <= step - 1) & (place < self.depth - 1))
             def _():
-                self.copy(step, way, self.chunk(origin)).start()
-
-            if step > 1:
-
-                @pl.when((place >= 1) & (place <= step - 1) & (place < self.depth - 1))
-                def _():
-                    mine = pltpu.make_async_copy(self.chunk(origin), self.own, self.load.at[0])
-                    mine.start()
-                    if here:
-                        self.copy(step - 1, way, self.out(step, way)).wait_recv()
-                    came = pltpu.make_async_copy(
-                        self.landing(step - 1, way), self.held, self.load.at[1]
-                    )
-                    came.start()
-                    mine.wait()
-                    came.wait()
-                    target = self.out(step, way)
-                    target[...] = (self.own[...].astype(F32) + self.held[...].astype(F32)).astype(
-                        BF
-                    )
-                    self.copy(step, way, target).start()
+                mine = pltpu.make_async_copy(
+                    self.chunk(self.origin(step, way)), self.own, self.load.at[0]
+                )
+                mine.start()
+                if here:
+                    self.copy(step - 1, way, self.out(step, way)).wait_recv()
+                came = pltpu.make_async_copy(
+                    self.landing(step - 1, way), self.held, self.load.at[1]
+                )
+                came.start()
+                mine.wait()
+                came.wait()
+                target = self.out(step, way)
+                target[...] = (self.own[...].astype(F32) + self.held[...].astype(F32)).astype(BF)
+                self.copy(step, way, target).start()
 
     def arrive(self, step, consumed):
         for way in (1, -1):
@@ -366,13 +369,116 @@
         mine.wait()
         return self.own[...].astype(F32) + right[...].astype(F32) + left[...].astype(F32)
 
-    def sent(self, step):
+    def sent_first(self, step):
+        for way in (1, -1):
+
+            @pl.when(self.place(way) == 0)
+            def _():
+                self.copy(step, way, self.out(step, way)).wait_send()
+
+    def sent_on(self, step):
         for way in (1, -1):
             place = self.place(way)
 
-            @pl.when((place == 0) | ((place <= step - 1) & (place < self.depth - 1)))
+            @pl.when((place >= 1) & (place <= step - 1) & (place < self.depth - 1))
             def _():
                 self.copy(step, way, self.out(step, way)).wait_send()
+
+    def sent(self, step):
+        self.sent_first(step)
+        self.sent_on(step)
+
+
+class SeqSum:
+    def __init__(self, size, width, to_core, sums, coming, core_sems, axis_sems, base):
+        self.size, self.width = size, width
+        self.to_core, self.sums, self.coming = to_core, sums, coming
+        self.core_sems, self.axis_sems, self.base = core_sems, axis_sems, base
+        self.chips = size // 2
+        self.bits = size.bit_length() - 2
+        bits = list(range(self.bits))
+        self.orders = (bits, bits[::-1])
+
+    def core_copy(self):
+        me = lax.axis_index("seq")
+        send, recv = self.core_sems
+        return remote(self.to_core, self.sums, send, recv, {"seq": me ^ 1})
+
+    def away(self, terms):
+        def write(columns, y):
+            self.to_core[:, :, columns] = y.astype(BF)
+
+        terms(1 - (lax.axis_index("seq") & 1), write)
+        self.core_copy().start()
+
+    def here(self, terms):
+        self.core_copy().wait_recv()
+
+        def write(columns, y):
+            self.sums[:, :, columns] = (y + self.sums[:, :, columns].astype(F32)).astype(BF)
+
+        terms(lax.axis_index("seq") & 1, write)
+        self.start(0)
+
+    def copies(self, part, stage):
+        me = lax.axis_index("seq")
+        half = self.width // 2
+        bit = self.orders[part][stage]
+        done = sum(1 << b for b in self.orders[part][:stage])
+        first = self.chips - (self.chips >> stage)
+        columns = slice(part * half, (part + 1) * half)
+        send, recv = self.axis_sems
+        found = []
+        for mask in range(self.chips):
+            if mask & (done | (1 << bit)):
+                continue
+            slot = first + len(found)
+            number = self.base + part * (self.chips - 1) + slot
+            copy = remote(
+                self.sums.at[(me >> 1) ^ (mask | (1 << bit)), :, columns],
+                self.coming.at[slot, :, columns],
+                send.at[number],
+                recv.at[number],
+                {"seq": me ^ (2 << bit)},
+            )
+            found.append((mask, slot, copy))
+        return found
+
+    def start(self, stage):
+        for part in range(2):
+            for _, _, copy in self.copies(part, stage):
+                copy.start()
+
+    def add(self, stage):
+        half = self.width // 2
+        for part in range(2):
+            columns = slice(part * half, (part + 1) * half)
+            for mask, slot, copy in self.copies(part, stage):
+                copy.wait_recv()
+                if stage < self.bits - 1:
+                    block = (lax.axis_index("seq") >> 1) ^ mask
+                    self.sums[block, :, columns] = (
+                        self.sums[block, :, columns].astype(F32)
+                        + self.coming[slot, :, columns].astype(F32)
+                    ).astype(BF)
+
+    def step(self, stage):
+        self.add(stage)
+        if stage + 1 < self.bits:
+            self.start(stage + 1)
+
+    def last(self):
+        chip = lax.axis_index("seq") >> 1
+        return self.sums[chip].astype(F32) + self.coming[self.chips - 2].astype(F32)
+
+    def core_sent(self):
+        self.core_copy().wait_send()
+
+    def sent(self):
+        for part in range(2):
+            for stage in range(self.bits):
+                for _, _, copy in self.copies(part, stage):
+                    copy.wait_send()
 
 
 def load_kernel(
@@ -381,16 +487,14 @@
     up_ref,
     one_ref,
     two_ref,
-    qkv_ref,
-    out_ref,
     vec_ref,
     normed_ref,
     all_up_ref,
     my_one_ref,
     my_two_ref,
-    attn_ref,
     full_ref,
     gathered,
+    normed_v,
     vec_seq,
     vec_sum,
     vec_all,
@@ -419,13 +523,17 @@
 
     def vec_seq_copy(step):
         return remote(
-            vec_ref, vec_seq.at[step], vec_send.at[step], vec_recv.at[step], seq(step)
+            vec_sum.at[step],
+            vec_seq.at[step],
+            vec_send.at[step],
+            vec_recv.at[step],
+            seq(1 << step),
         )
 
     def vec_line_copy(step):
         number = size + step
         return remote(
-            vec_sum, vec_all.at[step], vec_send.at[number], vec_recv.at[number], line(step)
+            vec_sum.at[count], vec_all.at[step], vec_send.at[number], vec_recv.at[number], line(step)
         )
 
     def one_copy(step):
@@ -435,17 +543,6 @@
             my_one_ref.at[me, at],
             a2a_send.at[step],
             a2a_recv.at[step],
-            seq(step),
-        )
-
-    def qkv_copy(step, part):
-        peer = me ^ step
-        number = size * (1 + part) + step
-        return remote(
-            qkv_ref.at[:, pl.ds(pl.multiple_of(part * width + peer * cols, 128), cols)],
-            attn_ref.at[me, :, pl.ds(part * cols, cols)],
-            a2a_send.at[number],
-            a2a_recv.at[number],
             seq(step),
         )
 
@@ -466,23 +563,7 @@
             local_sem.at[2],
         ),
     ]
-    for part in range(3):
-        local.append(
-            pltpu.make_async_copy(
-                qkv_ref.at[:, pl.ds(pl.multiple_of(part * width + me * cols, 128), cols)],
-                attn_ref.at[me, :, pl.ds(part * cols, cols)],
-                local_sem.at[3 + part],
-            )
-        )
-    local.append(pltpu.make_async_copy(two_ref, my_two_ref.at[at], local_sem.at[6]))
-    for peer in range(size):
-        local.append(
-            pltpu.make_async_copy(
-                out_ref.at[:, pl.ds(peer * cols, cols)],
-                attn_ref.at[peer, :, pl.ds(3 * cols, cols)],
-                local_sem.at[7 + peer],
-            )
-        )
+    local.append(pltpu.make_async_copy(two_ref, my_two_ref.at[at], local_sem.at[3]))
 
     def one_line(step, way):
         origin = jnp.clip(at - way * (step - 1), 0, depth - 1)
@@ -584,81 +665,88 @@
         for copy in copies:
             copy.wait_recv()
 
-    issue(vec_seq_copy(step) for step in range(1, size))
+    def vec_stage(step):
+        vec_seq_copy(step).wait_recv()
+        total = vec_sum[step].astype(F32) + vec_seq[step].astype(F32)
+        vec_sum[step + 1] = total.astype(BF)
+
     issue(one_copy(step) for step in range(1, size))
     for way in (1, -1):
         start(two_line(way))
     issue(local)
-    vec_seq[0] = vec_ref[...]
-    arrive(vec_seq_copy(step) for step in range(1, size))
-    summed = vec_seq[0].astype(F32)
-    for step in range(1, size):
-        summed = summed + vec_seq[step].astype(F32)
-    vec_sum[...] = summed.astype(BF)
-    issue(vec_line_copy(step) for step in range(1, depth))
-    for which in range(2):
-        issue(both_parts(row_cores, which, -1))
+    vec_sum[0] = vec_ref[...]
+    vec_seq_copy(0).start()
+    issue(both_parts(row_cores, 0, -1))
+    vec_stage(0)
+    vec_seq_copy(1).start()
     arrive(one_copy(step) for step in range(1, size))
     local[0].wait()
     for way in (1, -1):
         start(one_line(1, way))
-    for which in range(2):
-        issue(both_parts(row_stage, which, 0))
-    arrive(vec_line_copy(step) for step in range(1, depth))
-    for step in range(1, depth):
-        summed = summed + vec_all[step].astype(F32)
-    full_ref[...] = summed
-
+    for step in range(1, count):
+        vec_stage(step)
+        if step + 1 < count:
+            vec_seq_copy(step + 1).start()
+    issue(both_parts(row_stage, 0, 0))
+    issue(vec_line_copy(step) for step in range(1, depth))
+
+    def line_on(step):
+        for way in (1, -1):
+            wait_recv(one_arrives(step, way))
+            start(one_line(step + 1, way))
+
+    events = [(which, stage) for which in range(2) for stage in range(count - 1)]
     line_step = 1
-    for stage in range(count - 1):
-        for which in range(2):
-            arrive(both_parts(row_stage, which, stage))
-            issue(both_parts(row_cores, which, stage))
-            if stage + 1 < count - 1:
-                issue(both_parts(row_stage, which, stage + 1))
+    for number, (which, stage) in enumerate(events):
+        arrive(both_parts(row_stage, which, stage))
+        if number + 1 < len(events):
+            issue(both_parts(row_stage, *events[number + 1]))
+        issue(both_parts(row_cores, which, stage))
+        if number == 0:
+            issue(both_parts(row_cores, 1, -1))
+            arrive(vec_line_copy(step) for step in range(1, depth))
+            summed = vec_sum[count].astype(F32)
+            for step in range(1, depth):
+                summed = summed + vec_all[step].astype(F32)
+            full_ref[...] = summed
         if line_step < depth - 1:
-            for way in (1, -1):
-                wait_recv(one_arrives(line_step, way))
-                start(one_line(line_step + 1, way))
+            line_on(line_step)
             line_step += 1
-    for part in range(3):
-        issue(qkv_copy(step, part) for step in range(1, size))
-    while line_step < depth - 1:
-        for way in (1, -1):
-            wait_recv(one_arrives(line_step, way))
-            start(one_line(line_step + 1, way))
-        line_step += 1
-
-    local[1].wait()
-    for stage in range(-1, count - 1):
-        arrive(both_parts(row_cores, 0, stage))
-    gain = full_ref[0:1, :]
-    shift = full_ref[1:2, :]
-
-    @pl.loop(0, micro * size)
-    def _(index):
-        m, block = index // size, lax.rem(index, size)
-        x = gathered[m, block].astype(F32)
-        center = x - jnp.mean(x, axis=-1, keepdims=True)
-        spread = jnp.mean(center * center, axis=-1, keepdims=True)
-        y = center * lax.rsqrt(spread + EPSILON) * gain + shift
-        normed_ref[m, block] = y.astype(BF)
+        if number == len(events) - 2:
+            while line_step < depth - 1:
+                line_on(line_step)
+                line_step += 1
+            local[1].wait()
+            for step in range(-1, count - 1):
+                arrive(both_parts(row_cores, 0, step))
+            gain = full_ref[0:1, :]
+            shift = full_ref[1:2, :]
+
+            @pl.loop(0, micro * size)
+            def _(index):
+                m, block = index // size, lax.rem(index, size)
+                x = gathered[m, block].astype(F32)
+                center = x - jnp.mean(x, axis=-1, keepdims=True)
+                spread = jnp.mean(center * center, axis=-1, keepdims=True)
+                y = center * lax.rsqrt(spread + EPSILON) * gain + shift
+                normed_v[m, block] = y.astype(BF)
+
+            normed_out = pltpu.make_async_copy(normed_v, normed_ref, local_sem.at[4])
+            normed_out.start()
 
     for copy in local[2:]:
         copy.wait()
+    normed_out.wait()
     for stage in range(-1, count - 1):
         arrive(both_parts(row_cores, 1, stage))
-    for part in range(3):
-        arrive(qkv_copy(step, part) for step in range(1, size))
     for way in (1, -1):
         wait_recv(two_arrives(way))
         wait_recv(one_arrives(depth - 1, way))
 
+    for step in range(count):
+        vec_seq_copy(step).wait_send()
     for step in range(1, size):
-        vec_seq_copy(step).wait_send()
         one_copy(step).wait_send()
-        for part in range(3):
-            qkv_copy(step, part).wait_send()
     for step in range(1, depth):
         vec_line_copy(step).wait_send()
         for way in (1, -1):
@@ -674,7 +762,7 @@
                     copy.wait_send()
 
 
-def load_all(tokens, upstream, w_fc1, w_fc2, w_qkv, w_out, vectors):
+def load_all(tokens, upstream, w_fc1, w_fc2, vectors):
     size, depth = lax.axis_size("seq"), lax.axis_size("fsdp")
     micro, length, width = tokens.shape
     rows, units, cols = w_fc1.shape[0], w_fc1.shape[1] // size, width // size
@@ -685,38 +773,38 @@
     dma = pltpu.SemaphoreType.DMA
     return pl.pallas_call(
         functools.partial(load_kernel, dims),
-        in_specs=[hbm] * 6 + [vmem],
-        out_specs=[vmem] + [hbm] * 4 + [vmem],
+        in_specs=[hbm] * 4 + [vmem],
+        out_specs=[hbm] * 4 + [vmem],
         out_shape=[
             jax.ShapeDtypeStruct(gathered, BF),
             jax.ShapeDtypeStruct(gathered, BF),
             jax.ShapeDtypeStruct((size, depth, rows, units), BF),
             jax.ShapeDtypeStruct((depth,) + w_fc2.shape, BF),
-            jax.ShapeDtypeStruct((size, rows, 4 * cols), BF),
             jax.ShapeDtypeStruct(vectors.shape, F32),
         ],
         scratch_shapes=[
             pltpu.VMEM(gathered, BF),
+            pltpu.VMEM(gathered, BF),
             pltpu.VMEM((size,) + vectors.shape, BF),
-            pltpu.VMEM(vectors.shape, BF),
+            pltpu.VMEM((size,) + vectors.shape, BF),
             pltpu.VMEM((depth,) + vectors.shape, BF),
-            dma((7 + size,)),
+            dma((5,)),
             dma((size + depth,)),
             dma((size + depth,)),
-            dma((4 * size,)),
-            dma((4 * size,)),
+            dma((size,)),
+            dma((size,)),
             dma((2 * depth + 2,)),
             dma((2 * depth + 2,)),
             dma((4 * size,)),
             dma((4 * size,)),
         ],
         compiler_params=pltpu.CompilerParams(
-            collective_id=1, has_side_effects=True, vmem_limit_bytes=40 * 1024 * 1024
+            collective_id=1, has_side_effects=True, vmem_limit_bytes=60 * 1024 * 1024
         ),
         cost_estimate=pl.CostEstimate(
             flops=1000, bytes_accessed=300 * 1000 * 1000, transcendentals=0
         ),
-    )(tokens, upstream, w_fc1, w_fc2, w_qkv, w_out, vectors)
+    )(tokens, upstream, w_fc1, w_fc2, vectors)
 
 
 def ffn_kernel(
@@ -725,11 +813,11 @@
     up_hbm,
     one_hbm,
     two_hbm,
-    cols_hbm,
+    qkv_hbm,
+    out_hbm,
     full_ref,
-    hidden_hbm,
-    pre_hbm,
-    all_two_hbm,
+    part_grad_hbm,
+    part_act_hbm,
     attn_hbm,
     grad_two_hbm,
     grad_one_hbm,
@@ -744,9 +832,9 @@
     pre_v,
     grad_two_v,
     grad_one_v,
-    own_two,
-    held_two,
-    out_two,
+    own_one,
+    held_one,
+    out_one,
     load_sem,
     line_load,
     store_sem,
@@ -758,10 +846,14 @@
     sum_two_recv,
     sum_one_send,
     sum_one_recv,
+    a2a_send,
+    a2a_recv,
+    local_sem,
 ):
     size, depth, micro, length, width, units, cols = dims
     me, at = lax.axis_index("seq"), lax.axis_index("fsdp")
     count = micro * size * length
+    per = width // size
     tile = 512
     group = units // depth
 
@@ -787,8 +879,34 @@
         def _():
             copy.start()
 
-    own_attn = pltpu.make_async_copy(cols_hbm, attn_hbm.at[:, at], store_sem.at[0])
-    own_attn.start()
+    def qkv_part(peer, part):
+        return qkv_hbm.at[:, pl.ds(pl.multiple_of(part * width + peer * cols, 128), cols)]
+
+    def qkv_copy(step, part):
+        number = part * size + step
+        return remote(
+            qkv_part(me ^ step, part),
+            attn_hbm.at[me, at, :, pl.ds(part * cols, cols)],
+            a2a_send.at[number],
+            a2a_recv.at[number],
+            {"seq": me ^ step},
+        )
+
+    local = [
+        pltpu.make_async_copy(
+            qkv_part(me, part), attn_hbm.at[me, at, :, pl.ds(part * cols, cols)], local_sem.at[part]
+        )
+        for part in range(3)
+    ] + [
+        pltpu.make_async_copy(
+            out_hbm.at[:, pl.ds(peer * cols, cols)],
+            attn_hbm.at[peer, at, :, pl.ds(3 * cols, cols)],
+            local_sem.at[3 + peer],
+        )
+        for peer in range(size)
+    ]
+    for copy in local:
+        copy.start()
     greet(size, depth)
 
     two = LineGather(
@@ -800,7 +918,7 @@
     )
     attn = LineGather(
         depth,
-        lambda o, step: cols_hbm if step == 1 else attn_hbm.at[:, o],
+        lambda o, step: attn_hbm.at[:, o],
         lambda o: attn_hbm.at[:, o],
         attn_send,
         attn_recv,
@@ -808,10 +926,10 @@
     sum_two = LineSum(
         depth,
         lambda o: grad_two_v.at[o],
-        lambda step, way: land_two.at[(step - 1) * 2 + (way > 0)],
-        own_two,
-        held_two,
-        lambda step, way: out_two.at[int(way > 0)],
+        lambda step, way: land_two.at[int(way > 0)],
+        own_one,
+        held_one,
+        lambda step, way: grad_two_v.at[0],
         line_load,
         sum_two_send,
         sum_two_recv,
@@ -820,14 +938,17 @@
         depth,
         lambda o: grad_one_v.at[:, o],
         lambda step, way: land_one.at[(step - 1) * 2 + (way > 0)],
-        own_two,
-        held_two,
-        lambda step, way: grad_one_v.at[:, 0],
+        own_one,
+        held_one,
+        lambda step, way: out_one.at[int(way > 0)],
         line_load,
         sum_one_send,
         sum_one_recv,
     )
     two.start(2)
+    for part in range(3):
+        for step in range(1, size):
+            qkv_copy(step, part).start()
 
     for load in loads[:2]:
         load.wait()
@@ -855,8 +976,6 @@
             pre_v[rows, columns] = slope.astype(BF)
 
     loads[2].wait()
-    hidden_out = pltpu.make_async_copy(hidden_v, hidden_hbm, store_sem.at[1])
-    hidden_out.start()
     over_first = (((0,), (0,)), ((), ()))
     over_last = (((1,), (1,)), ((), ()))
 
@@ -868,7 +987,7 @@
 
     two.arrive(2)
     two.start(3)
-    sum_two.start(1)
+    sum_two.source(1)
     grad_two_out = pltpu.make_async_copy(grad_two_v, grad_two_hbm, store_sem.at[2])
     grad_two_out.start()
     bone_ref[...] = jnp.zeros_like(bone_ref)
@@ -885,7 +1004,6 @@
             bone_ref[:, columns] += jnp.sum(y.astype(F32), axis=0, keepdims=True)
 
         wide = 1024
-        per = width // size
 
         @pl.loop(0, width // wide)
         def _(d):
@@ -913,6 +1031,11 @@
         def _():
             piece(jnp.clip(origin, 0, depth - 1))
 
+    for copy in local:
+        copy.wait()
+    for part in range(3):
+        for step in range(1, size):
+            qkv_copy(step, part).wait_recv()
     two.arrive(3)
     attn.start(1)
 
@@ -925,38 +1048,59 @@
         def _():
             piece(jnp.clip(origin, 0, depth - 1))
 
-    stores = [
-        pltpu.make_async_copy(pre_v, pre_hbm, store_sem.at[3]),
-        pltpu.make_async_copy(two_v, all_two_hbm, store_sem.at[4]),
-        pltpu.make_async_copy(grad_one_v, grad_one_hbm, store_sem.at[5]),
-    ]
-    for store in stores:
-        store.start()
+    sum_one.source(1)
+    sum_one.source(2)
+    grad_one_out = pltpu.make_async_copy(grad_one_v, grad_one_hbm, store_sem.at[5])
+    grad_one_out.start()
+
+    @pl.loop(0, count // tile)
+    def _(r):
+        rows = pl.ds(pl.multiple_of(r * tile, tile), tile)
+        a = pre_v[rows, :]
+        for s in range(size):
+            w = one_v[s].reshape(per, units)
+            y = lax.dot_general(a, w, over_last, preferred_element_type=F32)
+            normed_v[rows, s * per : (s + 1) * per] = y.astype(BF)
+
+    part_grad = pltpu.make_async_copy(normed_v, part_grad_hbm, store_sem.at[3])
+    part_grad.start()
     attn.arrive(1)
     attn.start(2)
-    sum_one.start(1)
+
+    @pl.loop(0, count // tile)
+    def _(r):
+        rows = pl.ds(pl.multiple_of(r * tile, tile), tile)
+        a = hidden_v[rows, :]
+        for s in range(size):
+            columns = slice(s * per, (s + 1) * per)
+            w = two_v[:, :, columns].reshape(units, per)
+            up_v[rows, columns] = jnp.dot(a, w, preferred_element_type=F32).astype(BF)
+
+    part_act = pltpu.make_async_copy(up_v, part_act_hbm, store_sem.at[4])
+    part_act.start()
     attn.arrive(2)
     attn.start(3)
-    sum_two.start(2)
-    own_attn.wait()
-    hidden_out.wait()
+    sum_one.forward(2)
     grad_two_out.wait()
-    for store in stores:
+    for store in (grad_one_out, part_grad, part_act):
         store.wait()
     attn.arrive(3)
-    sum_two.arrive(1, True)
-    sum_two.arrive(2, False)
-    sum_one.arrive(1, False)
+    sum_two.arrive(1, False)
+    sum_one.arrive(1, True)
+    sum_one.arrive(2, False)
     for step in (2, 3):
         two.sent(step)
     for step in (1, 2, 3):
         attn.sent(step)
     sum_two.sent(1)
-    sum_two.sent(2)
     sum_one.sent(1)
-
-
-def feed_forward(normed, up, one, two, columns, full):
+    sum_one.sent(2)
+    for part in range(3):
+        for step in range(1, size):
+            qkv_copy(step, part).wait_send()
+
+
+def feed_forward(normed, up, one, two, w_qkv, w_out, full):
     size, depth = lax.axis_size("seq"), lax.axis_size("fsdp")
     micro, _, length, width = normed.shape
     units, cols = one.shape[-1], width // size
@@ -971,17 +1115,16 @@
     tall, deep = (depth, units // depth, width), (size, depth, rows, units)
     return pl.pallas_call(
         functools.partial(ffn_kernel, dims),
-        in_specs=[hbm] * 5 + [vmem],
-        out_specs=[hbm] * 8 + [vmem],
+        in_specs=[hbm] * 6 + [vmem],
+        out_specs=[hbm] * 7 + [vmem],
         out_shape=[
-            shape((count, units), BF),
-            shape((count, units), BF),
-            shape(tall, BF),
+            shape((count, width), BF),
+            shape((count, width), BF),
             shape((size, depth, rows, 4 * cols), BF),
             shape(tall, BF),
             shape(deep, BF),
-            shape((4,) + tall[1:], BF),
-            shape((2, size, rows, units), BF),
+            shape((2,) + tall[1:], BF),
+            shape((4, size, rows, units), BF),
             shape((1, units), F32),
         ],
         scratch_shapes=[
@@ -993,21 +1136,30 @@
             pltpu.VMEM((count, units), BF),
             pltpu.VMEM(tall, BF),
             pltpu.VMEM(deep, BF),
-            pltpu.VMEM(tall[1:], BF),
-            pltpu.VMEM(tall[1:], BF),
-            pltpu.VMEM((2,) + tall[1:], BF),
+            pltpu.VMEM((size, rows, units), BF),
+            pltpu.VMEM((size, rows, units), BF),
+            pltpu.VMEM((2, size, rows, units), BF),
             dma((6,)),
             dma((2,)),
             dma((6,)),
         ]
-        + [sums] * 8,
+        + [sums] * 8
+        + [dma((3 * size,)), dma((3 * size,)), dma((3 + size,))],
         compiler_params=pltpu.CompilerParams(
             collective_id=2, has_side_effects=True, vmem_limit_bytes=60 * 1024 * 1024
         ),
         cost_estimate=pl.CostEstimate(
             flops=34 * 1000**3, bytes_accessed=300 * 1000 * 1000, transcendentals=0
         ),
-    )(normed.reshape(count, width), up.reshape(count, width), one, two, columns, full)
+    )(
+        normed.reshape(count, width),
+        up.reshape(count, width),
+        one,
+        two,
+        w_qkv,
+        w_out,
+        full,
+    )
 
 
 def attn_layer_kernel(
@@ -1022,15 +1174,18 @@
     grad_one_hbm,
     old_two,
     old_one,
+    part_act_hbm,
+    tokens_hbm,
     full_ref,
     turned_hbm,
     mixed_hbm,
     grads_hbm,
-    one_hbm,
+    spread_hbm,
     land_two,
     land_one,
     bqkv_ref,
     two_ref,
+    act_ref,
     normed_v,
     up_v,
     attn_v,
@@ -1044,9 +1199,13 @@
     own_two,
     held_two,
     out_two,
-    own_one,
+    one_total,
     held_one,
-    out_one,
+    part_act_v,
+    tokens_v,
+    to_core,
+    act_sums,
+    act_coming,
     load_sem,
     line_load,
     store_sem,
@@ -1054,6 +1213,11 @@
     sum_two_recv,
     sum_one_send,
     sum_one_recv,
+    a2a_send,
+    a2a_recv,
+    core_sem,
+    axis_send,
+    axis_recv,
 ):
     size, depth, micro, length, width, units, cols = dims
     me = lax.axis_index("seq")
@@ -1075,7 +1239,7 @@
         depth,
         lambda o: grad_two_hbm.at[o],
         lambda step, way: (
-            old_two.at[(step - 1) * 2 + (way > 0)] if step < 3 else land_two.at[int(way > 0)]
+            old_two.at[int(way > 0)] if step < 2 else land_two.at[(step - 2) * 2 + (way > 0)]
         ),
         own_two,
         held_two,
@@ -1088,17 +1252,62 @@
         depth,
         lambda o: grad_one_hbm.at[:, o],
         lambda step, way: (
-            old_one.at[int(way > 0)] if step < 2 else land_one.at[(step - 2) * 2 + (way > 0)]
+            old_one.at[(step - 1) * 2 + (way > 0)] if step < 3 else land_one.at[int(way > 0)]
         ),
-        own_one,
-        held_one,
-        lambda step, way: out_one.at[(step - 2) * 2 + (way > 0)],
+        one_total,
+        held_one.at[0],
+        lambda step, way: held_one.at[1 + (way > 0)],
         line_load,
         sum_one_send,
         sum_one_recv,
     )
-    sum_two.start(3, here=False)
-    sum_one.start(2, here=False)
+    sum_one.source(3)
+    sum_two.source(2)
+    sum_two.source(3)
+    sum_one.forward(3, here=False)
+    sum_two.forward(2, here=False)
+    tokens_load = pltpu.make_async_copy(tokens_hbm.at[0], tokens_v, load_sem.at[4])
+    tokens_load.start()
+
+    def part_act_half(parity):
+        blocks = pl.ds(parity * chips, chips)
+        return pltpu.make_async_copy(part_act_hbm.at[0, blocks], part_act_v, load_sem.at[3])
+
+    part_act_half(1 - (me & 1)).start()
+
+    def spread_copy(step):
+        peer = me ^ step
+        return remote(
+            one_total.at[peer],
+            spread_hbm.at[me],
+            a2a_send.at[step],
+            a2a_recv.at[step],
+            {"seq": peer},
+        )
+
+    spread_mine = pltpu.make_async_copy(one_total.at[me], spread_hbm.at[me], store_sem.at[3])
+    act = SeqSum(
+        size,
+        width,
+        to_core,
+        act_sums,
+        act_coming,
+        (core_sem.at[0], core_sem.at[1]),
+        (axis_send, axis_recv),
+        0,
+    )
+
+    def act_terms(parity, write):
+        first = pl.multiple_of(parity * chips * length, chips * length)
+        mine = mixed_v[pl.ds(first, chips * length), :]
+
+        @pl.loop(0, size)
+        def _(s):
+            columns = pl.ds(pl.multiple_of(s * per, per), per)
+            w = attn_v[s, :, :, 3 * cols :].reshape(cols, cols)
+            y = jnp.dot(mine, w, preferred_element_type=F32).reshape(chips, length, per)
+            write(columns, y + part_act_v[:, :, columns].astype(F32))
+
     for load in loads:
         load.wait()
 
@@ -1156,9 +1365,28 @@
     def _(index):
         m, g = index // groups, lax.rem(index, groups)
 
+        @pl.when(index == 2)
+        def _():
+            sum_one.sent(3)
+            total = sum_one.total(3, held_one.at[0], held_one.at[1])
+            one_total[...] = total.astype(BF)
+            for step in range(1, size):
+                spread_copy(step).start()
+            spread_mine.start()
+            tokens_load.wait()
+
+        @pl.when(index == groups)
+        def _():
+            part_act_half(1 - (me & 1)).wait()
+            act.away(act_terms)
+            part_act_half(me & 1).start()
+
         @pl.when(index == micro * groups - 1)
         def _():
-            sum_one.start(3)
+            part_act_half(me & 1).wait()
+            act.here(act_terms)
+            sum_two.sent_on(2)
+            sum_two.forward(3)
 
         def label(positions):
             found = jnp.full(positions.shape, -1, jnp.int32)
@@ -1190,32 +1418,27 @@
             rows = slice(first, first + tile)
             keys = natural_v[1, m, g, :last, :]
             values = natural_v[2, m, g, :last, :]
-            mixed = jnp.zeros((tile, LANES), F32)
-            dq = jnp.zeros((tile, LANES), F32)
-            for head in range(LANES // HEAD_DIM):
-                mine = (lane // HEAD_DIM) == head
-                q = jnp.where(mine, natural_v[0, m, g, rows, :], 0)
-                do = jnp.where(mine, natural_v[3, m, g, rows, :], 0)
-                s = lax.dot_general(q, keys, over_last, preferred_element_type=F32)
-                if first:
-                    s = jnp.concatenate(
-                        [s[:, :first], s[:, first:] + bias_s[:, : last - first]], axis=1
-                    )
-                else:
-                    s = s + bias_s[:, : last - first]
-                p = jnp.exp(s - jnp.max(s, axis=1, keepdims=True))
-                p = p * (1.0 / jnp.sum(p, axis=1, keepdims=True))
-                probs = p.astype(BF)
-                att = jnp.dot(probs, values, preferred_element_type=F32)
-                mixed = jnp.where(mine, att, mixed)
-                dp = lax.dot_general(do, values, over_last, preferred_element_type=F32)
-                delta = jnp.sum(p * dp, axis=1, keepdims=True)
-                ds = (p * (dp - delta)).astype(BF)
-                dq = jnp.where(mine, jnp.dot(ds, keys, preferred_element_type=F32), dq)
-                dk_s[:last, :] += lax.dot_general(ds, q, over_first, preferred_element_type=F32)
-                dv_s[:last, :] += lax.dot_general(
-                    probs, do, over_first, preferred_element_type=F32
-                )
+            heads = [(lane // HEAD_DIM) == head for head in range(LANES // HEAD_DIM)]
+            q = jnp.concatenate([jnp.where(h, natural_v[0, m, g, rows, :], 0) for h in heads])
+            do = jnp.concatenate([jnp.where(h, natural_v[3, m, g, rows, :], 0) for h in heads])
+            s = lax.dot_general(q, keys, over_last, preferred_element_type=F32)
+            bias = jnp.concatenate([bias_s[:, : last - first]] * len(heads))
+            if first:
+                s = jnp.concatenate([s[:, :first], s[:, first:] + bias], axis=1)
+            else:
+                s = s + bias
+            p = jnp.exp(s - jnp.max(s, axis=1, keepdims=True))
+            p = p * (1.0 / jnp.sum(p, axis=1, keepdims=True))
+            probs = p.astype(BF)
+            dp = lax.dot_general(do, values, over_last, preferred_element_type=F32)
+            att = jnp.dot(probs, values, preferred_element_type=F32)
+            delta = jnp.sum(p * dp, axis=1, keepdims=True)
+            ds = (p * (dp - delta)).astype(BF)
+            mixed = jnp.where(heads[0], att[:tile], att[tile:])
+            dq = jnp.dot(ds, keys, preferred_element_type=F32)
+            dq = jnp.where(heads[0], dq[:tile], dq[tile:])
+            dk_s[:last, :] += lax.dot_general(ds, q, over_first, preferred_element_type=F32)
+            dv_s[:last, :] += lax.dot_general(probs, do, over_first, preferred_element_type=F32)
             put(mixed_v, first, pl.ds(pl.multiple_of(g * LANES, LANES), LANES), mixed)
             dq = turn(dq * SCALE, cos_ref[rows, :], -sin_ref[rows, :])
             put(turned_v, first, columns_of(0), dq)
@@ -1228,6 +1451,9 @@
     ]
     for store in stores:
         store.start()
+    bits = size.bit_length() - 2
+    for stage in range(bits - 1):
+        act.step(stage)
 
     wide = 512
 
@@ -1249,27 +1475,33 @@
     grads_out = pltpu.make_async_copy(grads_v, grads_hbm, store_sem.at[2])
     grads_out.start()
     bqkv_ref[...] = jnp.sum(turned_v[...].astype(F32), axis=0, keepdims=True)
+    act.add(bits - 1)
+    bias = full_ref[5:6, :] + full_ref[6 + size * units // width : 7 + size * units // width, :]
+    act_ref[...] = (tokens_v[...].astype(F32) + act.last() + bias).astype(BF)
+    sum_two.sent_first(2)
     sum_two.sent(3)
     two_ref[...] = sum_two.total(3, held_two, out_two.at[0])
-    sum_one.sent(2)
-    one_sum = sum_one.total(3, held_one, out_one.at[0])
-    out_one[1] = one_sum.astype(BF)
-    one_out = pltpu.make_async_copy(out_one.at[1], one_hbm, store_sem.at[3])
-    one_out.start()
     for store in stores:
         store.wait()
     grads_out.wait()
-    one_out.wait()
-    sum_one.sent(3)
-
-
-def attention_layer(starts, normed, up, attn, grad_two, grad_one, old_two, old_one, full):
+    spread_mine.wait()
+    for step in range(1, size):
+        spread_copy(step).wait_recv()
+        spread_copy(step).wait_send()
+    act.core_sent()
+    act.sent()
+
+
+def attention_layer(
+    starts, normed, up, attn, grad_two, grad_one, old_two, old_one, part_act, tokens, full
+):
     size, depth, rows, units = grad_one.shape
     micro, _, length, width = normed.shape
     cols = width // size
     count, total = micro * size * length, size * length
     dims = (size, depth, micro, length, width, units, cols)
     cosine, sine = tables(total)
+    chips = size // 2
     hbm = pl.BlockSpec(memory_space=pl.ANY)
     vmem = pl.BlockSpec(memory_space=pltpu.VMEM)
     dma = pltpu.SemaphoreType.DMA
@@ -1278,17 +1510,18 @@
     tall, deep = (units // depth, width), (size, rows, units)
     return pl.pallas_call(
         functools.partial(attn_layer_kernel, dims),
-        in_specs=[pl.BlockSpec(memory_space=pltpu.SMEM)] + [vmem] * 2 + [hbm] * 7 + [vmem],
-        out_specs=[hbm] * 6 + [vmem] * 2,
+        in_specs=[pl.BlockSpec(memory_space=pltpu.SMEM)] + [vmem] * 2 + [hbm] * 9 + [vmem],
+        out_specs=[hbm] * 6 + [vmem] * 3,
         out_shape=[
             shape((count, 3 * cols), BF),
             shape((count, cols), BF),
             shape(attn.shape, BF),
             shape(deep, BF),
-            shape((2,) + tall, BF),
-            shape((4,) + deep, BF),
+            shape((4,) + tall, BF),
+            shape((2,) + deep, BF),
             shape((1, 3 * cols), F32),
             shape(tall, F32),
+            shape((length, width), BF),
         ],
         scratch_shapes=[
             pltpu.VMEM((count, width), BF),
@@ -1305,15 +1538,21 @@
             pltpu.VMEM(tall, BF),
             pltpu.VMEM((2,) + tall, BF),
             pltpu.VMEM(deep, BF),
-            pltpu.VMEM(deep, BF),
-            pltpu.VMEM((4,) + deep, BF),
-            dma((3,)),
+            pltpu.VMEM((3,) + deep, BF),
+            pltpu.VMEM((chips, length, width), BF),
+            pltpu.VMEM((length, width), BF),
+            pltpu.VMEM((chips, length, width), BF),
+            pltpu.VMEM((chips, length, width), BF),
+            pltpu.VMEM((chips - 1, length, width), BF),
+            dma((5,)),
             dma((2,)),
             dma((4,)),
         ]
-        + [sums] * 4,
+        + [sums] * 4
+        + [dma((size,)), dma((size,)), dma((2,))]
+        + [dma((2 * (chips - 1),))] * 2,
         compiler_params=pltpu.CompilerParams(
-            collective_id=3, has_side_effects=True, vmem_limit_bytes=60 * 1024 * 1024
+            collective_id=3, has_side_effects=True, vmem_limit_bytes=62 * 1024 * 1024
         ),
         cost_estimate=pl.CostEstimate(
             flops=40 * 1000**3, bytes_accessed=300 * 1000 * 1000, transcendentals=0
@@ -1329,6 +1568,8 @@
         grad_one,
         old_two,
         old_one,
+        part_act,
+        tokens,
         full,
     )
 
@@ -1339,58 +1580,45 @@
     up_hbm,
     grads_hbm,
     attn_hbm,
-    one_hbm,
-    two_hbm,
     turned_hbm,
-    pre_hbm,
     mixed_hbm,
-    hidden_hbm,
-    one_sum_hbm,
+    part_grad_hbm,
+    part_act_hbm,
     full_ref,
     bqkv_ref,
     bone_ref,
+    first_act_ref,
     act_ref,
     ingrad_ref,
-    qkv_ref,
     out_ref,
     vec_ref,
-    one_out_hbm,
-    landing,
+    spread_hbm,
     tokens_v,
     up_v,
     attn_v,
-    one_v,
-    two_v,
     turned_v,
-    pre_v,
     mixed_v,
-    hidden_v,
+    part_grad_v,
+    part_act_v,
     to_core,
     sums,
     coming,
-    line_a,
-    line_b,
+    grads_v,
+    landing,
     line_out,
     total_v,
-    spread_v,
-    one_land,
-    one_wide,
     vec_in,
     load_sem,
     core_send,
     core_recv,
     axis_send,
     axis_recv,
-    line_load,
     line_send,
     line_recv,
     a2a_send,
     a2a_recv,
     vec_send,
     vec_recv,
-    one_send,
-    one_recv,
-    wide_sem,
 ):
     size, depth, micro, length, width, units, cols = dims
     me, at = lax.axis_index("seq"), lax.axis_index("fsdp")
@@ -1406,17 +1634,16 @@
             (
                 (turned_hbm, turned_v),
                 (attn_hbm, attn_v),
-                (pre_hbm, pre_v),
-                (one_hbm, one_v),
-                (hidden_hbm, hidden_v),
-                (two_hbm, two_v),
+                (part_grad_hbm, part_grad_v),
+                (part_act_hbm.at[pl.ds(1, micro - 1)], part_act_v),
                 (mixed_hbm, mixed_v),
                 (tokens_hbm, tokens_v),
                 (up_hbm, up_v),
+                (grads_hbm, grads_v),
             )
         )
     ]
-    for load in loads:
+    for load in loads[7:] + loads[:7]:
         load.start()
     greet(size, depth)
 
@@ -1434,72 +1661,56 @@
         return at if way > 0 else depth - 1 - at
 
     def chunk(origin, part):
-        return grads_hbm.at[pl.ds(part * chips, chips), origin]
-
-    def line_step(step):
-        for part in range(2):
-            for way in (1, -1):
-                place = place_of(way)
-                away = jnp.clip(depth - step + place, 0, depth - 1)
-                origin = away if way > 0 else depth - 1 - away
-                slot = (way > 0) * 2 + part
-
-                @pl.when(place == 0)
-                def _():
-                    line_copy(step, way, part, chunk(origin, part)).start()
-
-                if step > 1:
-
-                    @pl.when((place >= 1) & (place <= step - 1) & (place < depth - 1))
+        return grads_v.at[pl.ds(part * chips, chips), origin]
+
+    def origin_of(step, way):
+        away = jnp.clip(depth - step + place_of(way), 0, depth - 1)
+        return away if way > 0 else depth - 1 - away
+
+    def line_source():
+        for step in range(1, depth):
+            for part in range(2):
+                for way in (1, -1):
+
+                    @pl.when(place_of(way) == 0)
                     def _():
-                        mine = pltpu.make_async_copy(
-                            chunk(origin, part), line_a.at[0], line_load.at[0]
-                        )
-                        mine.start()
-                        arrived = line_copy(step - 1, way, part, line_out.at[slot])
-                        arrived.wait_recv()
-                        came = pltpu.make_async_copy(
-                            landing.at[((step - 1) * 2 + (way > 0)) * 2 + part],
-                            line_b.at[0],
-                            line_load.at[1],
-                        )
-                        came.start()
-
-                        @pl.when(place <= step - 2)
-                        def _():
-                            arrived.wait_send()
-
-                        mine.wait()
-                        came.wait()
-                        line_out[slot] = (
-                            line_a[0].astype(F32) + line_b[0].astype(F32)
-                        ).astype(BF)
-                        line_copy(step, way, part, line_out.at[slot]).start()
-
-    def line_finish(part):
-        mine = pltpu.make_async_copy(chunk(at, part), line_a.at[0], line_load.at[0])
-        mine.start()
+                        line_copy(step, way, part, chunk(origin_of(step, way), part)).start()
+
+    def line_forward(step, part):
         for way in (1, -1):
             place = place_of(way)
-            slot = int(way > 0)
+            slot = (way > 0) * 2 + part
+
+            @pl.when((place >= 1) & (place <= step - 1) & (place < depth - 1))
+            def _():
+                arrived = line_copy(step - 1, way, part, line_out.at[slot])
+                arrived.wait_recv()
+
+                @pl.when(place <= step - 2)
+                def _():
+                    arrived.wait_send()
+
+                came = landing[((step - 1) * 2 + (way > 0)) * 2 + part]
+                mine = chunk(origin_of(step, way), part)[...]
+                line_out[slot] = (mine.astype(F32) + came.astype(F32)).astype(BF)
+                line_copy(step, way, part, line_out.at[slot]).start()
+
+    def line_finish(part):
+        for way in (1, -1):
+            place = place_of(way)
+            number = ((depth - 1) * 2 + (way > 0)) * 2 + part
 
             @pl.when(place >= 1)
             def _():
                 line_copy(depth - 1, way, part, line_out.at[0]).wait_recv()
-                came = pltpu.make_async_copy(
-                    landing.at[((depth - 1) * 2 + (way > 0)) * 2 + part],
-                    line_b.at[slot],
-                    line_load.at[1],
-                )
-                came.start()
-                came.wait()
 
             @pl.when(place == 0)
             def _():
-                line_b[slot] = jnp.zeros_like(line_b[slot])
-
-        mine.wait()
-        summed = line_a[0].astype(F32) + line_b[0].astype(F32) + line_b[1].astype(F32)
+                landing[number] = jnp.zeros_like(landing[number])
+
+        first = (depth - 1) * 4 + part
+        summed = chunk(at, part)[...].astype(F32)
+        summed = summed + landing[first].astype(F32) + landing[first + 2].astype(F32)
         total_v[pl.ds(part * chips, chips)] = summed.astype(BF)
         for block in range(chips):
             out_ref[:, (part * chips + block) * cols : (part * chips + block + 1) * cols] = summed[
@@ -1524,147 +1735,56 @@
         peer = me ^ step
         return remote(
             total_v.at[peer, :, pl.ds(0, 3 * cols)],
-            spread_v.at[me],
+            spread_hbm.at[me],
             a2a_send.at[step],
             a2a_recv.at[step],
             {"seq": peer},
         )
 
-    def one_copy(step):
-        peer = me ^ step
-        return remote(
-            one_sum_hbm.at[peer],
-            one_land.at[me],
-            one_send.at[step],
-            one_recv.at[step],
-            {"seq": peer},
-        )
-
-    one_mine = pltpu.make_async_copy(one_sum_hbm.at[me], one_land.at[me], one_recv.at[0])
-
-    def one_widen():
-        one_mine.wait()
-        for step in range(1, size):
-            one_copy(step).wait_recv()
-
-        def copy(block, slot):
-            at = pl.ds(pl.multiple_of(block * units, units), units)
-            return pltpu.make_async_copy(
-                one_wide.at[slot], one_out_hbm.at[:, at], wide_sem.at[slot]
-            )
-
-        for block in range(size):
-            slot = block % 2
-            if block >= 2:
-                copy(block - 2, slot).wait()
-            one_wide[slot] = one_land[block].astype(F32)
-            copy(block, slot).start()
-        for block in range(size - 2, size):
-            copy(block, block % 2).wait()
-
-    def core_copy(array, m):
-        number = array * micro + m
-        return remote(
-            to_core.at[m],
+    orders = [(0, m) for m in range(micro)] + [(1, m) for m in range(1, micro)]
+    found = {}
+    for number, (array, m) in enumerate(orders):
+        found[array, m] = SeqSum(
+            size,
+            width,
+            to_core.at[number],
             sums.at[number],
-            core_send.at[number],
-            core_recv.at[number],
-            {"seq": me ^ 1},
-        )
-
-    orders = (list(range(count - 1)), list(range(count - 1))[::-1])
-
-    def stage_copies(array, m, part, stage):
-        bit = orders[part][stage]
-        done = sum(1 << b for b in orders[part][:stage])
-        first = chips - (chips >> stage)
-        columns = slice(part * half, (part + 1) * half)
-        found = []
-        for mask in range(chips):
-            if mask & (done | (1 << bit)):
-                continue
-            slot = first + len(found)
-            number = ((array * micro + m) * 2 + part) * (chips - 1) + slot
-            copy = remote(
-                sums.at[array * micro + m, chip ^ (mask | (1 << bit)), :, columns],
-                coming.at[array * micro + m, slot, :, columns],
-                axis_send.at[number],
-                axis_recv.at[number],
-                {"seq": me ^ (2 << bit)},
-            )
-            found.append((mask, slot, copy))
-        return found
-
-    def stage_start(array, m, stage):
-        for part in range(2):
-            for _, _, copy in stage_copies(array, m, part, stage):
-                copy.start()
-
-    def stage_add(array, m, stage):
-        number = array * micro + m
-        for part in range(2):
-            columns = slice(part * half, (part + 1) * half)
-            for mask, slot, copy in stage_copies(array, m, part, stage):
-                copy.wait_recv()
-                if stage < count - 2:
-                    block = chip ^ mask
-                    sums[number, block, :, columns] = (
-                        sums[number, block, :, columns].astype(F32)
-                        + coming[number, slot, :, columns].astype(F32)
-                    ).astype(BF)
-
-    def stage_last(array, m):
-        number = array * micro + m
-        return sums[number, chip].astype(F32) + coming[number, chips - 2].astype(F32)
+            coming.at[number],
+            (core_send.at[number], core_recv.at[number]),
+            (axis_send, axis_recv),
+            number * 2 * (chips - 1),
+        )
 
     over_last = (((1,), (1,)), ((), ()))
 
-    def grad_terms(m, parity, write):
-        first = parity * chips
-        turned = turned_v[m, pl.ds(first, chips)].reshape(chips * length, 3 * cols)
-        pre = pre_v[m, pl.ds(first, chips)].reshape(chips * length, units)
-
-        @pl.loop(0, size)
-        def _(s):
-            w = attn_v[s, :, :, : 3 * cols].reshape(per, 3 * cols)
-            y = lax.dot_general(turned, w, over_last, preferred_element_type=F32)
-            w = one_v[s].reshape(per, units)
-            y = y + lax.dot_general(pre, w, over_last, preferred_element_type=F32)
-            write(pl.ds(pl.multiple_of(s * per, per), per), y.reshape(chips, length, per))
-
-    def act_terms(m, parity, write):
-        first = parity * chips
-        mixed = mixed_v[m, pl.ds(first, chips)].reshape(chips * length, cols)
-        hidden = hidden_v[m, pl.ds(first, chips)].reshape(chips * length, units)
-
-        @pl.loop(0, size)
-        def _(s):
-            columns = pl.ds(pl.multiple_of(s * per, per), per)
-            w = attn_v[s, :, :, 3 * cols :].reshape(per, cols)
-            y = jnp.dot(mixed, w, preferred_element_type=F32)
-            w = two_v[:, :, columns].reshape(units, per)
-            y = y + jnp.dot(hidden, w, preferred_element_type=F32)
-            write(columns, y.reshape(chips, length, per))
-
-    def terms_away(array, m, function):
-        if array:
-            core_copy(0, m).wait_send()
-
-        def write(columns, y):
-            to_core[m, :, :, columns] = y.astype(BF)
-
-        function(m, 1 - core, write)
-        core_copy(array, m).start()
-
-    def terms_here(array, m, function):
-        core_copy(array, m).wait_recv()
-        number = array * micro + m
-
-        def write(columns, y):
-            sums[number, :, :, columns] = (y + sums[number, :, :, columns].astype(F32)).astype(BF)
-
-        function(m, core, write)
-        stage_start(array, m, 0)
+    def grad_terms(m):
+        def terms(parity, write):
+            blocks = pl.ds(parity * chips, chips)
+            turned = turned_v[m, blocks].reshape(chips * length, 3 * cols)
+
+            @pl.loop(0, size)
+            def _(s):
+                columns = pl.ds(pl.multiple_of(s * per, per), per)
+                w = attn_v[s, :, :, : 3 * cols].reshape(per, 3 * cols)
+                y = lax.dot_general(turned, w, over_last, preferred_element_type=F32)
+                y = y.reshape(chips, length, per)
+                write(columns, y + part_grad_v[m, blocks, :, columns].astype(F32))
+
+        return terms
+
+    def act_terms(m):
+        def terms(parity, write):
+            blocks = pl.ds(parity * chips, chips)
+            mixed = mixed_v[m, blocks].reshape(chips * length, cols)
+
+            @pl.loop(0, size)
+            def _(s):
+                columns = pl.ds(pl.multiple_of(s * per, per), per)
+                w = attn_v[s, :, :, 3 * cols :].reshape(per, cols)
+                y = jnp.dot(mixed, w, preferred_element_type=F32).reshape(chips, length, per)
+                write(columns, y + part_act_v[m - 1, blocks, :, columns].astype(F32))
+
+        return terms
 
     gain = full_ref[0:1, :]
     vec_ref[...] = jnp.zeros_like(vec_ref)
@@ -1676,7 +1796,7 @@
 
     def norm_back(m):
         x = tokens_v[m].astype(F32)
-        dy = stage_last(0, m)
+        dy = found[0, m].last()
         center = x - jnp.mean(x, axis=-1, keepdims=True)
         spread = jnp.mean(center * center, axis=-1, keepdims=True)
         r = lax.rsqrt(spread + EPSILON)
@@ -1692,7 +1812,7 @@
 
     def act_out(m):
         bias = full_ref[5:6, :] + full_ref[6 + size * units // width : 7 + size * units // width, :]
-        total = tokens_v[m].astype(F32) + stage_last(1, m) + bias
+        total = tokens_v[m].astype(F32) + found[1, m].last() + bias
         act_ref[m] = total.astype(BF)
 
     levels = [("seq", 1 << bit) for bit in range(count)]
@@ -1716,48 +1836,33 @@
         if level + 1 < len(levels):
             vec_copy(level + 1).start()
 
-    one_mine.start()
-    for step in range(1, size):
-        one_copy(step).start()
-    line_step(1)
-    for load in loads[:4]:
+    loads[7].wait()
+    line_source()
+    for load in loads[:3]:
         load.wait()
     for m in range(micro):
-        terms_away(0, m, grad_terms)
+        found[0, m].away(grad_terms(m))
+    line_forward(2, 0)
     for m in range(micro):
-        terms_here(0, m, grad_terms)
-    line_step(2)
-    for load in loads[4:]:
+        found[0, m].here(grad_terms(m))
+    for load in loads[3:7]:
         load.wait()
-    stage_add(0, 0, 0)
-    stage_start(0, 0, 1)
-    for m in range(micro):
-        terms_away(1, m, act_terms)
-    stage_add(0, 1, 0)
-    stage_start(0, 1, 1)
-    for m in range(micro):
-        terms_here(1, m, act_terms)
-    one_widen()
-    stage_add(0, 0, 1)
+    act_ref[0] = first_act_ref[...]
+    found[1, 1].away(act_terms(1))
+    line_forward(2, 1)
+    found[1, 1].here(act_terms(1))
+    found[0, 0].step(0)
+    line_forward(3, 0)
+    found[0, 1].step(0)
+    found[0, 0].add(1)
+    line_forward(3, 1)
     norm_back(0)
-    line_step(3)
-    stage_add(0, 1, 1)
+    found[1, 1].step(0)
+    found[0, 1].add(1)
     norm_back(1)
     vec_copy(0).start()
-    stage_add(1, 0, 0)
-    stage_start(1, 0, 1)
-    vec_level(0)
-    vec_level(1)
-    stage_add(1, 1, 0)
-    stage_start(1, 1, 1)
-    vec_level(2)
-    vec_level(3)
-    stage_add(1, 0, 1)
-    act_out(0)
-    vec_level(4)
-    stage_add(1, 1, 1)
-    act_out(1)
-    for part in range(2):
+
+    def finish(part):
         line_finish(part)
         for step in range(1, size):
             peer = me ^ step
@@ -1766,35 +1871,37 @@
             def _():
                 back_copy(step).start()
 
-    def put(block, values):
-        for part in range(3):
-            start = pl.multiple_of(part * width + block * cols, cols)
-            qkv_ref[:, pl.ds(start, cols)] = values[:, part * cols : (part + 1) * cols]
-
-    put(me, total_v[me, :, : 3 * cols].astype(F32))
+    found[1, 1].add(1)
+    act_out(1)
+    vec_level(0)
+    vec_level(1)
+    finish(0)
+    for level in range(2, len(levels)):
+        vec_level(level)
+    finish(1)
+
+    back_mine = pltpu.make_async_copy(
+        total_v.at[me, :, pl.ds(0, 3 * cols)], spread_hbm.at[me], a2a_recv.at[0]
+    )
+    back_mine.start()
+    back_mine.wait()
     for step in range(1, size):
         back_copy(step).wait_recv()
-        put(me ^ step, spread_v[me ^ step].astype(F32))
 
     line_sent()
     for step in range(1, size):
         back_copy(step).wait_send()
-        one_copy(step).wait_send()
-    for m in range(micro):
-        core_copy(1, m).wait_send()
-        for array in range(2):
-            for part in range(2):
-                for stage in range(count - 1):
-                    for _, _, copy in stage_copies(array, m, part, stage):
-                        copy.wait_send()
+    for terms in found.values():
+        terms.core_sent()
+        terms.sent()
 
 
 def close_layer(
-    tokens, upstream, grads, attn, one, two, turned, pre, mixed, hidden, one_sum, full, bqkv, bone
+    tokens, upstream, grads, attn, turned, mixed, part_grad, part_act, full, bqkv, bone, first_act
 ):
     size, depth = lax.axis_size("seq"), lax.axis_size("fsdp")
     micro, length, width = tokens.shape
-    units, cols = one.shape[-1], width // size
+    units, cols = bone.shape[-1], width // size
     rows = width // (size * depth)
     dims = (size, depth, micro, length, width, units, cols)
     chips, count = size // 2, size.bit_length() - 1
@@ -1803,51 +1910,45 @@
     dma = pltpu.SemaphoreType.DMA
     levels = count + depth.bit_length() - 1
     piece = (chips, rows, 4 * cols)
-    loaded = (tokens, upstream, attn, one, two, turned, pre, mixed, hidden)
+    arrays = 2 * micro - 1
+    shape = jax.ShapeDtypeStruct
+    loaded = [v.shape for v in (tokens, upstream, attn, turned, mixed, part_grad)]
+    loaded = loaded + [(micro - 1,) + part_act.shape[1:]]
     return pl.pallas_call(
         functools.partial(close_kernel, dims),
-        in_specs=[hbm] * 11 + [vmem] * 3,
-        out_specs=[vmem] * 5 + [hbm] * 2,
+        in_specs=[hbm] * 8 + [vmem] * 4,
+        out_specs=[vmem] * 4 + [hbm],
         out_shape=[
-            jax.ShapeDtypeStruct(tokens.shape, BF),
-            jax.ShapeDtypeStruct(tokens.shape, F32),
-            jax.ShapeDtypeStruct((rows, 3 * width), F32),
-            jax.ShapeDtypeStruct((rows, width), F32),
-            jax.ShapeDtypeStruct(full.shape, F32),
-            jax.ShapeDtypeStruct((rows, size * units), F32),
-            jax.ShapeDtypeStruct((4 * depth,) + piece, BF),
+            shape(tokens.shape, BF),
+            shape(tokens.shape, F32),
+            shape((rows, width), F32),
+            shape(full.shape, F32),
+            shape((size, rows, 3 * cols), BF),
         ],
-        scratch_shapes=[pltpu.VMEM(v.shape, BF) for v in loaded]
+        scratch_shapes=[pltpu.VMEM(s, BF) for s in loaded]
         + [
-            pltpu.VMEM((micro, chips, length, width), BF),
-            pltpu.VMEM((2 * micro, chips, length, width), BF),
-            pltpu.VMEM((2 * micro, chips - 1, length, width), BF),
-            pltpu.VMEM((1,) + piece, BF),
-            pltpu.VMEM((2,) + piece, BF),
+            pltpu.VMEM((arrays, chips, length, width), BF),
+            pltpu.VMEM((arrays, chips, length, width), BF),
+            pltpu.VMEM((arrays, chips - 1, length, width), BF),
+            pltpu.VMEM(grads.shape, BF),
+            pltpu.VMEM((4 * depth,) + piece, BF),
             pltpu.VMEM((4,) + piece, BF),
             pltpu.VMEM((size, rows, 4 * cols), BF),
-            pltpu.VMEM((size, rows, 3 * cols), BF),
-            pltpu.VMEM(one_sum.shape, BF),
-            pltpu.VMEM((2,) + one_sum.shape[1:], F32),
             pltpu.VMEM((levels,) + full.shape, F32),
             dma((9,)),
-            dma((2 * micro,)),
-            dma((2 * micro,)),
-            dma((4 * micro * (chips - 1),)),
-            dma((4 * micro * (chips - 1),)),
-            dma((2,)),
+            dma((arrays,)),
+            dma((arrays,)),
+            dma((2 * arrays * (chips - 1),)),
+            dma((2 * arrays * (chips - 1),)),
             dma((4 * depth,)),
             dma((4 * depth,)),
             dma((size,)),
             dma((size,)),
             dma((levels,)),
             dma((levels,)),
-            dma((size,)),
-            dma((size,)),
-            dma((2,)),
         ],
         compiler_params=pltpu.CompilerParams(
-            collective_id=4, has_side_effects=True, vmem_limit_bytes=60 * 1024 * 1024
+            collective_id=4, has_side_effects=True, vmem_limit_bytes=62 * 1024 * 1024
         ),
         cost_estimate=pl.CostEstimate(
             flops=30 * 1000**3, bytes_accessed=300 * 1000 * 1000, transcendentals=0
@@ -1857,17 +1958,112 @@
         upstream,
         grads,
         attn,
-        one,
-        two,
         turned,
-        pre,
         mixed,
-        hidden,
-        one_sum,
+        part_grad,
+        part_act,
         full,
         bqkv,
         bone,
-    )[:6]
+        first_act,
+    )
+
+
+def result_kernel(
+    dims,
+    place_ref,
+    act_ref,
+    ingrad_ref,
+    out_ref,
+    two_ref,
+    one_ref,
+    qkv_ref,
+    vec_ref,
+    act_to,
+    ingrad_to,
+    gain_ref,
+    shift_ref,
+    wqkv_ref,
+    bqk_ref,
+    bv_ref,
+    out_to,
+    bout_ref,
+    one_to,
+    bone_ref,
+    two_to,
+    btwo_ref,
+):
+    size, depth, width, cols, units = dims
+    for source, target in (
+        (ingrad_ref, ingrad_to),
+        (two_ref, two_to),
+        (act_ref, act_to),
+        (out_ref, out_to),
+    ):
+        target[...] = source[...]
+    for s in range(size):
+        one_to[:, s * units : (s + 1) * units] = one_ref[s].astype(F32)
+        for part in range(3):
+            start = part * width + s * cols
+            wqkv_ref[:, start : start + cols] = qkv_ref[s, :, part * cols : (part + 1) * cols].astype(
+                F32
+            )
+    index = place_ref[0]
+
+    def own(row, total, target):
+        extent = total // (size * depth)
+        flat = index * extent
+        at = lax.rem(flat, width)
+        values = vec_ref[pl.ds(row + flat // width, 1), :]
+        values = pltpu.roll(values, lax.rem(width - at, width), 1)
+        target[...] = values[:, :extent]
+
+    own(0, width, gain_ref)
+    own(1, width, shift_ref)
+    own(2, 2 * width, bqk_ref)
+    own(4, width, bv_ref)
+    own(5, width, bout_ref)
+    own(5, width, btwo_ref)
+    own(6, size * units, bone_ref)
+
+
+def results(activations, input_grad, grad_out, grad_two, spread_one, spread_qkv, vectors, index):
+    size, rows, units = spread_one.shape
+    width = vectors.shape[-1]
+    depth = width // (size * rows)
+    cols = width // size
+    dims = (size, depth, width, cols, units)
+    vmem = pl.BlockSpec(memory_space=pltpu.VMEM)
+
+    def row(extent):
+        return jax.ShapeDtypeStruct((1, extent // (size * depth)), F32)
+
+    def like(value):
+        return jax.ShapeDtypeStruct(value.shape, value.dtype)
+
+    wide = jax.ShapeDtypeStruct((rows, size * units), F32)
+    shapes = [
+        like(activations),
+        like(input_grad),
+        row(width),
+        row(width),
+        jax.ShapeDtypeStruct((rows, 3 * width), F32),
+        row(2 * width),
+        row(width),
+        like(grad_out),
+        row(width),
+        wide,
+        row(size * units),
+        like(grad_two),
+        row(width),
+    ]
+    return pl.pallas_call(
+        functools.partial(result_kernel, dims),
+        in_specs=[pl.BlockSpec(memory_space=pltpu.SMEM)] + [vmem] * 7,
+        out_specs=[vmem] * len(shapes),
+        out_shape=shapes,
+        compiler_params=pltpu.CompilerParams(vmem_limit_bytes=60 * 1024 * 1024),
+    )(index[None], activations, input_grad, grad_out, grad_two, spread_one, spread_qkv, vectors)
 
 
 def gelu_tanh(values):
@@ -1956,7 +2152,7 @@
 
 
 def staged_layer(
-    tokens, upstream, w_fc2, starts, normed, up, my_one, two_near, attn_cols, full, index
+    tokens, upstream, w_fc2, w_qkv, w_out, starts, normed, up, my_one, two_near, full, index
 ):
     size, depth = lax.axis_size("seq"), lax.axis_size("fsdp")
     me = lax.axis_index("seq")
@@ -1999,6 +2195,10 @@
     bias_one = lax.dynamic_slice_in_dim(full[6 : 6 + ratio].reshape(-1), me * units, units, 0)
     bias_two = full[6 + ratio]
     two.step()
+    split = w_qkv.reshape(rows, 3, size, cols).transpose(2, 0, 1, 3).reshape(size, rows, 3 * cols)
+    attn_cols = lax.all_to_all(split, "seq", 0, 0, tiled=True)
+    out_cols = w_out.reshape(rows, size, cols).transpose(1, 0, 2)
+    attn_cols = jnp.concatenate([attn_cols, out_cols], axis=-1)
     pre = jnp.dot(normed, my_one, preferred_element_type=F32) + bias_one
     hidden, back = jax.vjp(gelu_tanh, pre)
     hidden = hidden.astype(BF)
@@ -2129,43 +2329,56 @@
     index = me * depth + lax.axis_index("fsdp")
     packed = []
     for vector in (ln_gain, ln_bias, b_qkv, b_out, b_fc1, b_fc2):
-        extent = vector.shape[0]
-        flat = jnp.zeros((extent * size * depth,), BF)
-        flat = lax.dynamic_update_slice(flat, vector, (index * extent,))
-        packed.append(flat.reshape(-1, width))
+        mine = jnp.arange(size * depth, dtype=jnp.int32)[:, None] == index
+        packed.append(jnp.where(mine, vector[None, :], 0).astype(BF).reshape(-1, width))
     packed = jnp.concatenate(packed, axis=0)
     packed = jnp.pad(packed, ((0, -packed.shape[0] % 16), (0, 0)))
     starts = piece_starts[:, 0]
-    loaded = load_all(tokens, upstream, w_fc1, w_fc2, w_qkv, w_out, packed)
+    loaded = load_all(tokens, upstream, w_fc1, w_fc2, packed)
     if (size, depth, micro) == (8, 4, 2):
-        normed, up, one, two_near, attn_cols, full = loaded
-        hidden, pre, two, attn, grad_two, grad_one, land_two, land_one, bone = feed_forward(
-            normed, up, one, two_near, attn_cols, full
-        )
-        turned, mixed, grads, one_sum, _, _, bqkv, out_two = attention_layer(
-            starts, normed, up, attn, grad_two, grad_one, land_two, land_one, full
+        normed, up, one, two_near, full = loaded
+        part_grad, part_act, attn, grad_two, grad_one, land_two, land_one, bone = feed_forward(
+            normed, up, one, two_near, w_qkv, w_out, full
         )
         wide = (micro, size, length, -1)
-        activations, input_grad, out_qkv, out_out, vectors, out_one = close_layer(
+        part_act = part_act.reshape(wide)
+        turned, mixed, grads, spread_one, _, _, bqkv, out_two, first_act = attention_layer(
+            starts,
+            normed,
+            up,
+            attn,
+            grad_two,
+            grad_one,
+            land_two,
+            land_one,
+            part_act,
+            tokens,
+            full,
+        )
+        activations, input_grad, out_out, vectors, spread_qkv = close_layer(
             tokens,
             upstream,
             grads,
             attn,
-            one,
-            two,
             turned.reshape(wide),
-            pre.reshape(wide),
             mixed.reshape(wide),
-            hidden.reshape(wide),
-            one_sum,
+            part_grad.reshape(wide),
+            part_act,
             full,
             bqkv,
             bone,
-        )
-    else:
-        activations, input_grad, out_qkv, out_out, vectors, out_one, out_two = staged_layer(
-            tokens, upstream, w_fc2, starts, *loaded, index
-        )
+            first_act,
+        )
+
+        found = results(
+            activations, input_grad, out_out, out_two, spread_one, spread_qkv, vectors, index
+        )
+        found = [v.reshape(-1) if n in (2, 3, 5, 6, 8, 10, 12) else v for n, v in enumerate(found)]
+        return (found[0][:, None], found[1][:, None]) + tuple(found[2:])
+
+    activations, input_grad, out_qkv, out_out, vectors, out_one, out_two = staged_layer(
+        tokens, upstream, w_fc2, w_qkv, w_out, starts, *loaded, index
+    )
     ratio = w_fc1.shape[1] // width
 
     def own(values):

time: 492 us -> 448 us (0.911)
  local copies, waits for them, and re-layouts: 32 us -> 2.04 us
  Pallas kernels: 449 us -> 436 us
    unnamed x39 -> x8, local copies, waits for them, and re-layouts: 23.1 us -> 0.73 us
    pallas_call x3 -> x4, Pallas kernels: 362 us -> 348 us  [the longest x1 126 us: feed_forward(): pl.pallas_call(functools.partial(ffn_kernel, dims), in_specs=[hbm] * 6 +...]
    dynamic_update_slice x6 -> x0, local copies, waits for them, and re-layouts: 5.2 us -> none  [per_device(): flat = lax.dynamic_update_slice(flat, vector, (index * extent,))]
where the time goes in v4:
time: 448 us; the launch traced here: 440 us
  Pallas kernels  436 us (97%)
    pallas_call x1, Pallas kernels, feed_forward(): pl.pallas_call(functools.partial(ffn_kernel, dims), in_specs=[hbm] * 6 +...  126 us
    pallas_call x1, Pallas kernels, load_all(): pl.pallas_call(functools.partial(load_kernel, dims), in_specs=[hbm] * 4 +...  109 us
    pallas_call x1, Pallas kernels, close_layer(): pl.pallas_call(functools.partial(close_kernel, dims), in_specs=[hbm] * 8...  106 us
    pallas_call x1, Pallas kernels, attention_layer(): pl.pallas_call(functools.partial(attn_layer_kernel, dims), in_specs=[pl.B...  88.1 us

profile of v4, /device:TPU:15, one launch (start us, length us, event | category | flops | bytes accessed | tf_op | source)
XLA Modules:
  0.0 440.4 jit_solution(14394592479425102239)
XLA Ops:
  0.6 0.0 copy-start
  0.7 0.6 copy-done
  1.3 0.1 broadcast_bitcast_fusion
  1.4 0.7 broadcast_select_fusion
  2.2 0.1 select_n.71
  2.3 0.8 broadcast_select_fusion.2
  3.1 0.1 select_n.76
  3.1 0.1 select_n.69
  3.2 0.1 select_n.73
  3.3 0.1 select_n.67
  3.4 0.2 concatenate.3
  3.6 0.6 pad.4.vec_ref
  4.3 109.0 %shard_map.246 = (bf16[2,8,128,2048]{3,2,1,0:T(8,128)(2,1)}, bf16[2,8,128,2048]{3,2,1,0:T(8,128)(2,1)}, bf16[8,4,64,1024]{3,2,1,0:T(8,128)(2,1)}, bf16[4,256,2048]{2,1,0:T(8,128)(2,1)}, f32[16,2048]{1,0:T(8,128)}) custom-call(bf16[2,128,2048]{2,1,0:T(8,128)(2,1)} %bitcast.29, bf16[2,128,2048]{2,1,0:T(8,128)(2,1)} %bitcast.32, bf16[64,8192]{1,0:T(8,128)(2,1)} %one_ref.1, ...), custom_call_target="tpu_custom_call" | custom-call | flops 1000 | bytes 300000000 | tf_op jit(solution)/shard_map/pallas_call | solution.py:774
  113.3 125.5 %shard_map.247 = (bf16[2048,2048]{1,0:T(8,128)(2,1)}, bf16[2048,2048]{1,0:T(8,128)(2,1)}, bf16[8,4,64,1024]{3,2,1,0:T(8,128)(2,1)}, bf16[4,256,2048]{2,1,0:T(8,1...) custom-call(bf16[2048,2048]{1,0:T(8,128)(2,1)} %bitcast.36, ...), custom_call_target="tpu_custom_call" | custom-call | flops 33999998976 | bytes 300000000 | tf_op jit(solution)/shard_map/pallas_call | solution.py:1116
  238.8 88.1 %shard_map.248 = (bf16[2048,768]{1,0:T(8,128)(2,1)}, bf16[2048,256]{1,0:T(8,128)(2,1)}, bf16[8,4,64,1024]{3,2,1,0:T(8,128)(2,1)}, bf16[8,64,1024]{2,1,0:T(8,128)...) custom-call(s32[2,2]{1,0:T(2,128)} %bitcast.42, ...), custom_call_target="tpu_custom_call" | custom-call | flops 40000000000 | bytes 300000000 | tf_op jit(solution)/shard_map/pallas_call | solution.py:1511
  326.9 0.0 copy-start.1
  326.9 106.2 %shard_map.249 = (bf16[2,128,2048]{2,1,0:T(8,128)(2,1)}, f32[2,128,2048]{2,1,0:T(8,128)}, f32[64,2048]{1,0:T(8,128)}, f32[16,2048]{1,0:T(8,128)}, bf16[8,64,768]{2,1,0:T(8,128)(2,1)}) custom-call(bf16[2,128,2048]{2,1,0:T(8,128)(2,1)} %bitcast.31, bf16[2,128,2048]{2,1,0:T(8,128)(2,1)} %bitcast.33, bf16[8,4,64,1024]{3,2,1,0:T(8,128)(2,1)} %get-tuple-element.62.grads_hbm, ...), custom_call_target="tpu_custom_call" | custom-call | flops 30000001024 | bytes 300000000 | tf_op jit(solution)/shard_map/pallas_call | solution.py:1917
  433.1 7.1 %shard_map.250 = (bf16[2,128,2048]{2,1,0:T(8,128)(2,1)}, f32[2,128,2048]{2,1,0:T(8,128)}, f32[1,64]{1,0:T(1,128)}, f32[1,64]{1,0:T(1,128)}, f32[64,6144]{1,0:T(8...) custom-call(s32[1]{0:T(128)} %bitcast.place_ref, ...), custom_call_target="tpu_custom_call" | custom-call | tf_op jit(solution)/shard_map/pallas_call | solution.py:2060
  440.2 0.0 copy-done.1
  (6 shorter events, 0.1 us)
Async XLA Ops:
  0.6 0.7 copy-start
  326.9 113.3 %copy-start.1 = (bf16[256]{0:T(256)(128)(2,1)S(1)}, bf16[256]{0:T(256)(128)(2,1)}, u32[]{:S(2)}) copy-start(bf16[256]{0:T(256)(128)(2,1)} %param.23) | copy-start | bytes 1540

commit v5 on v4

--- a/solution.py
+++ b/solution.py
@@ -683,11 +683,12 @@
     local[0].wait()
     for way in (1, -1):
         start(one_line(1, way))
+    for which in range(2):
+        issue(both_parts(row_stage, which, 0))
     for step in range(1, count):
         vec_stage(step)
         if step + 1 < count:
             vec_seq_copy(step + 1).start()
-    issue(both_parts(row_stage, 0, 0))
     issue(vec_line_copy(step) for step in range(1, depth))
 
     def line_on(step):
@@ -695,44 +696,45 @@
             wait_recv(one_arrives(step, way))
             start(one_line(step + 1, way))
 
-    events = [(which, stage) for which in range(2) for stage in range(count - 1)]
     line_step = 1
-    for number, (which, stage) in enumerate(events):
-        arrive(both_parts(row_stage, which, stage))
-        if number + 1 < len(events):
-            issue(both_parts(row_stage, *events[number + 1]))
-        issue(both_parts(row_cores, which, stage))
-        if number == 0:
-            issue(both_parts(row_cores, 1, -1))
-            arrive(vec_line_copy(step) for step in range(1, depth))
-            summed = vec_sum[count].astype(F32)
-            for step in range(1, depth):
-                summed = summed + vec_all[step].astype(F32)
-            full_ref[...] = summed
-        if line_step < depth - 1:
-            line_on(line_step)
-            line_step += 1
-        if number == len(events) - 2:
-            while line_step < depth - 1:
-                line_on(line_step)
-                line_step += 1
-            local[1].wait()
-            for step in range(-1, count - 1):
-                arrive(both_parts(row_cores, 0, step))
-            gain = full_ref[0:1, :]
-            shift = full_ref[1:2, :]
-
-            @pl.loop(0, micro * size)
-            def _(index):
-                m, block = index // size, lax.rem(index, size)
-                x = gathered[m, block].astype(F32)
-                center = x - jnp.mean(x, axis=-1, keepdims=True)
-                spread = jnp.mean(center * center, axis=-1, keepdims=True)
-                y = center * lax.rsqrt(spread + EPSILON) * gain + shift
-                normed_v[m, block] = y.astype(BF)
-
-            normed_out = pltpu.make_async_copy(normed_v, normed_ref, local_sem.at[4])
-            normed_out.start()
+    for stage in range(count - 1):
+        for which in range(2):
+            arrive(both_parts(row_stage, which, stage))
+            if stage + 1 < count - 1:
+                issue(both_parts(row_stage, which, stage + 1))
+            issue(both_parts(row_cores, which, stage))
+            if stage == 0 and which == 0:
+                issue(both_parts(row_cores, 1, -1))
+                arrive(vec_line_copy(step) for step in range(1, depth))
+                summed = vec_sum[count].astype(F32)
+                for step in range(1, depth):
+                    summed = summed + vec_all[step].astype(F32)
+                full_ref[...] = summed
+            elif which == 0 or stage == 0:
+                if line_step < depth - 1:
+                    line_on(line_step)
+                    line_step += 1
+            if stage == count - 2 and which == 0:
+                while line_step < depth - 1:
+                    line_on(line_step)
+                    line_step += 1
+                local[1].wait()
+                for step in range(-1, count - 1):
+                    arrive(both_parts(row_cores, 0, step))
+                gain = full_ref[0:1, :]
+                shift = full_ref[1:2, :]
+
+                @pl.loop(0, micro * size)
+                def _(index):
+                    m, block = index // size, lax.rem(index, size)
+                    x = gathered[m, block].astype(F32)
+                    center = x - jnp.mean(x, axis=-1, keepdims=True)
+                    spread = jnp.mean(center * center, axis=-1, keepdims=True)
+                    y = center * lax.rsqrt(spread + EPSILON) * gain + shift
+                    normed_v[m, block] = y.astype(BF)
+
+                normed_out = pltpu.make_async_copy(normed_v, normed_ref, local_sem.at[4])
+                normed_out.start()
 
     for copy in local[2:]:
         copy.wait()
@@ -824,6 +826,7 @@
     land_two,
     land_one,
     bone_ref,
+    btwo_ref,
     normed_v,
     up_v,
     one_v,
@@ -1053,6 +1056,12 @@
     grad_one_out = pltpu.make_async_copy(grad_one_v, grad_one_hbm, store_sem.at[5])
     grad_one_out.start()
 
+    btwo_ref[...] = jnp.zeros_like(btwo_ref)
+    for m in range(micro):
+        mine = pl.multiple_of((m * size + store_index(me)) * length, length)
+        rows = up_v[pl.ds(mine, length), :].astype(F32)
+        btwo_ref[...] += jnp.sum(rows, axis=0, keepdims=True)
+
     @pl.loop(0, count // tile)
     def _(r):
         rows = pl.ds(pl.multiple_of(r * tile, tile), tile)
@@ -1116,7 +1125,7 @@
     return pl.pallas_call(
         functools.partial(ffn_kernel, dims),
         in_specs=[hbm] * 6 + [vmem],
-        out_specs=[hbm] * 7 + [vmem],
+        out_specs=[hbm] * 7 + [vmem] * 2,
         out_shape=[
             shape((count, width), BF),
             shape((count, width), BF),
@@ -1126,6 +1135,7 @@
             shape((2,) + tall[1:], BF),
             shape((4, size, rows, units), BF),
             shape((1, units), F32),
+            shape((1, width), F32),
         ],
         scratch_shapes=[
             pltpu.VMEM((count, width), BF),
@@ -1587,11 +1597,13 @@
     full_ref,
     bqkv_ref,
     bone_ref,
+    btwo_ref,
     first_act_ref,
     act_ref,
     ingrad_ref,
     out_ref,
     vec_ref,
+    norm_ref,
     spread_hbm,
     tokens_v,
     up_v,
@@ -1607,6 +1619,9 @@
     landing,
     line_out,
     total_v,
+    norm_v,
+    norm_seq,
+    norm_line,
     vec_in,
     load_sem,
     core_send,
@@ -1619,6 +1634,8 @@
     a2a_recv,
     vec_send,
     vec_recv,
+    norm_send,
+    norm_recv,
 ):
     size, depth, micro, length, width, units, cols = dims
     me, at = lax.axis_index("seq"), lax.axis_index("fsdp")
@@ -1643,7 +1660,7 @@
             )
         )
     ]
-    for load in loads[7:] + loads[:7]:
+    for load in loads[7:] + loads[:3]:
         load.start()
     greet(size, depth)
 
@@ -1791,6 +1808,8 @@
     for part in range(3):
         columns = pl.ds(pl.multiple_of(me * cols, cols), cols)
         vec_ref[2 + part : 3 + part, columns] = bqkv_ref[:, part * cols : (part + 1) * cols]
+    vec_ref[5:6, :] = btwo_ref[...]
+    norm_v[...] = jnp.zeros_like(norm_v)
     bone_at = pl.multiple_of(lax.rem(me * units, width), units)
     vec_ref[pl.ds(6 + me * units // width, 1), pl.ds(bone_at, units)] = bone_ref[...]
 
@@ -1804,19 +1823,53 @@
         g = dy * gain
         inner = g - jnp.mean(g, axis=-1, keepdims=True)
         inner = inner - xhat * jnp.mean(g * xhat, axis=-1, keepdims=True)
-        upstream = up_v[m].astype(F32)
-        ingrad_ref[m] = upstream + r * inner
-        vec_ref[5:6, :] += jnp.sum(upstream, axis=0, keepdims=True)
-        vec_ref[0:1, :] += jnp.sum(dy * xhat, axis=0, keepdims=True)
-        vec_ref[1:2, :] += jnp.sum(dy, axis=0, keepdims=True)
+        ingrad_ref[m] = up_v[m].astype(F32) + r * inner
+        norm_v[0:1, :] += jnp.sum(dy * xhat, axis=0, keepdims=True)
+        norm_v[1:2, :] += jnp.sum(dy, axis=0, keepdims=True)
 
     def act_out(m):
         bias = full_ref[5:6, :] + full_ref[6 + size * units // width : 7 + size * units // width, :]
         total = tokens_v[m].astype(F32) + found[1, m].last() + bias
         act_ref[m] = total.astype(BF)
 
-    levels = [("seq", 1 << bit) for bit in range(count)]
-    levels = levels + [("fsdp", 1 << bit) for bit in range(depth.bit_length() - 1)]
+    def norm_seq_copy(step):
+        peer = me ^ step
+        return remote(
+            norm_v.at[:, pl.ds(pl.multiple_of(peer * per, per), per)],
+            norm_seq.at[step],
+            norm_send.at[step],
+            norm_recv.at[step],
+            {"seq": peer},
+        )
+
+    def norm_line_copy(step):
+        number = size + step
+        return remote(
+            norm_seq.at[0],
+            norm_line.at[step],
+            norm_send.at[number],
+            norm_recv.at[number],
+            {"fsdp": lax.rem(at + step, depth)},
+        )
+
+    def norm_line_start():
+        total = norm_v[:, pl.ds(pl.multiple_of(me * per, per), per)]
+        for step in range(1, size):
+            norm_seq_copy(step).wait_recv()
+            total = total + norm_seq[step]
+        norm_seq[0] = total
+        for step in range(1, depth):
+            norm_line_copy(step).start()
+
+    def norm_finish():
+        total = norm_seq[0]
+        for step in range(1, depth):
+            norm_line_copy(step).wait_recv()
+            total = total + norm_line[step]
+        norm_ref[...] = total
+
+    levels = [("fsdp", 1 << bit) for bit in range(depth.bit_length() - 1)]
+    levels = levels + [("seq", 1 << bit) for bit in range(count)]
 
     def vec_copy(level):
         axis, step = levels[level]
@@ -1836,15 +1889,23 @@
         if level + 1 < len(levels):
             vec_copy(level + 1).start()
 
+    vec_copy(0).start()
     loads[7].wait()
+    vec_level(0)
     line_source()
     for load in loads[:3]:
         load.wait()
-    for m in range(micro):
-        found[0, m].away(grad_terms(m))
+    for load in loads[3:7]:
+        load.start()
+    found[0, 0].away(grad_terms(0))
+    vec_level(1)
+    found[0, 1].away(grad_terms(1))
+    vec_level(2)
     line_forward(2, 0)
-    for m in range(micro):
-        found[0, m].here(grad_terms(m))
+    vec_level(3)
+    found[0, 0].here(grad_terms(0))
+    vec_level(4)
+    found[0, 1].here(grad_terms(1))
     for load in loads[3:7]:
         load.wait()
     act_ref[0] = first_act_ref[...]
@@ -1855,12 +1916,14 @@
     line_forward(3, 0)
     found[0, 1].step(0)
     found[0, 0].add(1)
+    norm_back(0)
     line_forward(3, 1)
-    norm_back(0)
-    found[1, 1].step(0)
     found[0, 1].add(1)
     norm_back(1)
-    vec_copy(0).start()
+    for step in range(1, size):
+        norm_seq_copy(step).start()
+    found[1, 1].step(0)
+    norm_line_start()
 
     def finish(part):
         line_finish(part)
@@ -1871,14 +1934,11 @@
             def _():
                 back_copy(step).start()
 
+    finish(0)
     found[1, 1].add(1)
     act_out(1)
-    vec_level(0)
-    vec_level(1)
-    finish(0)
-    for level in range(2, len(levels)):
-        vec_level(level)
     finish(1)
+    norm_finish()
 
     back_mine = pltpu.make_async_copy(
         total_v.at[me, :, pl.ds(0, 3 * cols)], spread_hbm.at[me], a2a_recv.at[0]
@@ -1890,6 +1950,10 @@
 
     line_sent()
     for step in range(1, size):
+        norm_seq_copy(step).wait_send()
+    for step in range(1, depth):
+        norm_line_copy(step).wait_send()
+    for step in range(1, size):
         back_copy(step).wait_send()
     for terms in found.values():
         terms.core_sent()
@@ -1897,7 +1961,19 @@
 
 
 def close_layer(
-    tokens, upstream, grads, attn, turned, mixed, part_grad, part_act, full, bqkv, bone, first_act
+    tokens,
+    upstream,
+    grads,
+    attn,
+    turned,
+    mixed,
+    part_grad,
+    part_act,
+    full,
+    bqkv,
+    bone,
+    btwo,
+    first_act,
 ):
     size, depth = lax.axis_size("seq"), lax.axis_size("fsdp")
     micro, length, width = tokens.shape
@@ -1916,13 +1992,14 @@
     loaded = loaded + [(micro - 1,) + part_act.shape[1:]]
     return pl.pallas_call(
         functools.partial(close_kernel, dims),
-        in_specs=[hbm] * 8 + [vmem] * 4,
-        out_specs=[vmem] * 4 + [hbm],
+        in_specs=[hbm] * 8 + [vmem] * 5,
+        out_specs=[vmem] * 5 + [hbm],
         out_shape=[
             shape(tokens.shape, BF),
             shape(tokens.shape, F32),
             shape((rows, width), F32),
             shape(full.shape, F32),
+            shape((8, width // size), F32),
             shape((size, rows, 3 * cols), BF),
         ],
         scratch_shapes=[pltpu.VMEM(s, BF) for s in loaded]
@@ -1934,6 +2011,9 @@
             pltpu.VMEM((4 * depth,) + piece, BF),
             pltpu.VMEM((4,) + piece, BF),
             pltpu.VMEM((size, rows, 4 * cols), BF),
+            pltpu.VMEM((8, width), F32),
+            pltpu.VMEM((size, 8, width // size), F32),
+            pltpu.VMEM((depth, 8, width // size), F32),
             pltpu.VMEM((levels,) + full.shape, F32),
             dma((9,)),
             dma((arrays,)),
@@ -1946,6 +2026,8 @@
             dma((size,)),
             dma((levels,)),
             dma((levels,)),
+            dma((size + depth,)),
+            dma((size + depth,)),
         ],
         compiler_params=pltpu.CompilerParams(
             collective_id=4, has_side_effects=True, vmem_limit_bytes=62 * 1024 * 1024
@@ -1965,6 +2047,7 @@
         full,
         bqkv,
         bone,
+        btwo,
         first_act,
     )
 
@@ -1979,6 +2062,7 @@
     one_ref,
     qkv_ref,
     vec_ref,
+    norm_ref,
     act_to,
     ingrad_to,
     gain_ref,
@@ -2018,8 +2102,11 @@
         values = pltpu.roll(values, lax.rem(width - at, width), 1)
         target[...] = values[:, :extent]
 
-    own(0, width, gain_ref)
-    own(1, width, shift_ref)
+    per = width // size
+    extent = per // depth
+    norms = pltpu.roll(norm_ref[...], lax.rem(per - lax.rem(index, depth) * extent, per), 1)
+    gain_ref[...] = norms[0:1, :extent]
+    shift_ref[...] = norms[1:2, :extent]
     own(2, 2 * width, bqk_ref)
     own(4, width, bv_ref)
     own(5, width, bout_ref)
@@ -2027,7 +2114,9 @@
     own(6, size * units, bone_ref)
 
 
-def results(activations, input_grad, grad_out, grad_two, spread_one, spread_qkv, vectors, index):
+def results(
+    activations, input_grad, grad_out, grad_two, spread_one, spread_qkv, vectors, norms, index
+):
     size, rows, units = spread_one.shape
     width = vectors.shape[-1]
     depth = width // (size * rows)
@@ -2059,11 +2148,21 @@
     ]
     return pl.pallas_call(
         functools.partial(result_kernel, dims),
-        in_specs=[pl.BlockSpec(memory_space=pltpu.SMEM)] + [vmem] * 7,
+        in_specs=[pl.BlockSpec(memory_space=pltpu.SMEM)] + [vmem] * 8,
         out_specs=[vmem] * len(shapes),
         out_shape=shapes,
         compiler_params=pltpu.CompilerParams(vmem_limit_bytes=60 * 1024 * 1024),
-    )(index[None], activations, input_grad, grad_out, grad_two, spread_one, spread_qkv, vectors)
+    )(
+        index[None],
+        activations,
+        input_grad,
+        grad_out,
+        grad_two,
+        spread_one,
+        spread_qkv,
+        vectors,
+        norms,
+    )
 
 
 def gelu_tanh(values):
@@ -2337,7 +2436,7 @@
     loaded = load_all(tokens, upstream, w_fc1, w_fc2, packed)
     if (size, depth, micro) == (8, 4, 2):
         normed, up, one, two_near, full = loaded
-        part_grad, part_act, attn, grad_two, grad_one, land_two, land_one, bone = feed_forward(
+        part_grad, part_act, attn, grad_two, grad_one, land_two, land_one, *sums = feed_forward(
             normed, up, one, two_near, w_qkv, w_out, full
         )
         wide = (micro, size, length, -1)
@@ -2355,7 +2454,7 @@
             tokens,
             full,
         )
-        activations, input_grad, out_out, vectors, spread_qkv = close_layer(
+        activations, input_grad, out_out, vectors, norms, spread_qkv = close_layer(
             tokens,
             upstream,
             grads,
@@ -2366,12 +2465,12 @@
             part_act,
             full,
             bqkv,
-            bone,
+            *sums,
             first_act,
         )
 
         found = results(
-            activations, input_grad, out_out, out_two, spread_one, spread_qkv, vectors, index
+            activations, input_grad, out_out, out_two, spread_one, spread_qkv, vectors, norms, index
         )
         found = [v.reshape(-1) if n in (2, 3, 5, 6, 8, 10, 12) else v for n, v in enumerate(found)]
         return (found[0][:, None], found[1][:, None]) + tuple(found[2:])

time: 448 us -> 430 us (0.960)
  Pallas kernels: 436 us -> 417 us
    pallas_call x1, Pallas kernels: 109 us -> 99.7 us  [load_all(): pl.pallas_call(functools.partial(load_kernel, dims), in_specs=[hbm] * 4 +...]
    pallas_call x1, Pallas kernels: 106 us -> 98.5 us  [close_layer(): pl.pallas_call(functools.partial(close_kernel, dims), in_specs=[hbm] * 8...]
where the time goes in v5:
time: 430 us; the launch traced here: 422 us
  Pallas kernels  417 us (97%)
    pallas_call x1, Pallas kernels, feed_forward(): pl.pallas_call(functools.partial(ffn_kernel, dims), in_specs=[hbm] * 6 +...  125 us
    pallas_call x1, Pallas kernels, load_all(): pl.pallas_call(functools.partial(load_kernel, dims), in_specs=[hbm] * 4 +...  99.7 us
    pallas_call x1, Pallas kernels, close_layer(): pl.pallas_call(functools.partial(close_kernel, dims), in_specs=[hbm] * 8...  98.5 us
    pallas_call x1, Pallas kernels, attention_layer(): pl.pallas_call(functools.partial(attn_layer_kernel, dims), in_specs=[pl.B...  87.3 us

profile of v5, /device:TPU:15, one launch (start us, length us, event | category | flops | bytes accessed | tf_op | source)
XLA Modules:
  0.0 422.0 jit_solution(11817269411842239096)
XLA Ops:
  0.6 0.0 copy-start
  0.7 0.6 copy-done
  1.3 0.1 broadcast_bitcast_fusion
  1.4 0.7 broadcast_select_fusion
  2.2 0.1 select_n.71
  2.3 0.8 broadcast_select_fusion.2
  3.1 0.1 select_n.76
  3.1 0.1 select_n.69
  3.2 0.1 select_n.73
  3.3 0.1 select_n.67
  3.4 0.2 concatenate.3
  3.6 0.6 pad.4.vec_ref
  4.3 99.7 %shard_map.246 = (bf16[2,8,128,2048]{3,2,1,0:T(8,128)(2,1)}, bf16[2,8,128,2048]{3,2,1,0:T(8,128)(2,1)}, bf16[8,4,64,1024]{3,2,1,0:T(8,128)(2,1)}, bf16[4,256,2048]{2,1,0:T(8,128)(2,1)}, f32[16,2048]{1,0:T(8,128)}) custom-call(bf16[2,128,2048]{2,1,0:T(8,128)(2,1)} %bitcast.29, bf16[2,128,2048]{2,1,0:T(8,128)(2,1)} %bitcast.32, bf16[64,8192]{1,0:T(8,128)(2,1)} %one_ref.1, ...), custom_call_target="tpu_custom_call" | custom-call | flops 1000 | bytes 300000000 | tf_op jit(solution)/shard_map/pallas_call | solution.py:776
  104.0 124.8 %shard_map.247 = (bf16[2048,2048]{1,0:T(8,128)(2,1)}, bf16[2048,2048]{1,0:T(8,128)(2,1)}, bf16[8,4,64,1024]{3,2,1,0:T(8,128)(2,1)}, bf16[4,256,2048]{2,1,0:T(8,1...) custom-call(bf16[2048,2048]{1,0:T(8,128)(2,1)} %bitcast.36, ...), custom_call_target="tpu_custom_call" | custom-call | flops 33999998976 | bytes 300000000 | tf_op jit(solution)/shard_map/pallas_call | solution.py:1125
  228.8 87.3 %shard_map.248 = (bf16[2048,768]{1,0:T(8,128)(2,1)}, bf16[2048,256]{1,0:T(8,128)(2,1)}, bf16[8,4,64,1024]{3,2,1,0:T(8,128)(2,1)}, bf16[8,64,1024]{2,1,0:T(8,128)...) custom-call(s32[2,2]{1,0:T(2,128)} %bitcast.42, ...), custom_call_target="tpu_custom_call" | custom-call | flops 40000000000 | bytes 300000000 | tf_op jit(solution)/shard_map/pallas_call | solution.py:1521
  316.2 0.0 copy-start.1
  316.2 98.5 %shard_map.249 = (bf16[2,128,2048]{2,1,0:T(8,128)(2,1)}, f32[2,128,2048]{2,1,0:T(8,128)}, f32[64,2048]{1,0:T(8,128)}, f32[16,2048]{1,0:T(8,128)}, f32[8,256]{1,0:T(8,128)}, /*index=5*/bf16[8,64,768]{2,1,0:T(8,128)(2,1)}) custom-call(bf16[2,128,2048]{2,1,0:T(8,128)(2,1)} %bitcast.31, bf16[2,128,2048]{2,1,0:T(8,128)(2,1)} %bitcast.33, ...), custom_call_target="tpu_custom_call" | custom-call | flops 30000001024 | bytes 300000000 | tf_op jit(solution)/shard_map/pallas_call | solution.py:1993
  414.6 7.1 %shard_map.250 = (bf16[2,128,2048]{2,1,0:T(8,128)(2,1)}, f32[2,128,2048]{2,1,0:T(8,128)}, f32[1,64]{1,0:T(1,128)}, f32[1,64]{1,0:T(1,128)}, f32[64,6144]{1,0:T(8...) custom-call(s32[1]{0:T(128)} %bitcast.place_ref, ...), custom_call_target="tpu_custom_call" | custom-call | tf_op jit(solution)/shard_map/pallas_call | solution.py:2149
  421.8 0.0 copy-done.1
  (6 shorter events, 0.1 us)
Async XLA Ops:
  0.6 0.7 copy-start
  316.2 105.6 %copy-start.1 = (bf16[256]{0:T(256)(128)(2,1)S(1)}, bf16[256]{0:T(256)(128)(2,1)}, u32[]{:S(2)}) copy-start(bf16[256]{0:T(256)(128)(2,1)} %param.23) | copy-start | bytes 1540

commit v6 on v5

--- a/solution.py
+++ b/solution.py
@@ -1868,8 +1868,29 @@
             total = total + norm_line[step]
         norm_ref[...] = total
 
-    levels = [("fsdp", 1 << bit) for bit in range(depth.bit_length() - 1)]
-    levels = levels + [("seq", 1 << bit) for bit in range(count)]
+    levels = [("seq", 1 << bit) for bit in range(count)]
+
+    def vec_line_copy(step):
+        number = count + step
+        return remote(
+            vec_in.at[count],
+            vec_in.at[number],
+            vec_send.at[number],
+            vec_recv.at[number],
+            {"fsdp": lax.rem(at + step, depth)},
+        )
+
+    def vec_line_start():
+        vec_in[count] = vec_ref[...]
+        for step in range(1, depth):
+            vec_line_copy(step).start()
+
+    def vec_finish():
+        for step in range(1, depth):
+            copy = vec_line_copy(step)
+            copy.wait()
+            vec_ref[...] += vec_in[count + step]
+
 
     def vec_copy(level):
         axis, step = levels[level]
@@ -1891,8 +1912,8 @@
 
     vec_copy(0).start()
     loads[7].wait()
+    line_source()
     vec_level(0)
-    line_source()
     for load in loads[:3]:
         load.wait()
     for load in loads[3:7]:
@@ -1902,9 +1923,8 @@
     found[0, 1].away(grad_terms(1))
     vec_level(2)
     line_forward(2, 0)
-    vec_level(3)
+    vec_line_start()
     found[0, 0].here(grad_terms(0))
-    vec_level(4)
     found[0, 1].here(grad_terms(1))
     for load in loads[3:7]:
         load.wait()
@@ -1939,6 +1959,7 @@
     act_out(1)
     finish(1)
     norm_finish()
+    vec_finish()
 
     back_mine = pltpu.make_async_copy(
         total_v.at[me, :, pl.ds(0, 3 * cols)], spread_hbm.at[me], a2a_recv.at[0]
@@ -1984,7 +2005,7 @@
     hbm = pl.BlockSpec(memory_space=pl.ANY)
     vmem = pl.BlockSpec(memory_space=pltpu.VMEM)
     dma = pltpu.SemaphoreType.DMA
-    levels = count + depth.bit_length() - 1
+    levels = count + depth
     piece = (chips, rows, 4 * cols)
     arrays = 2 * micro - 1
     shape = jax.ShapeDtypeStruct
@@ -2030,7 +2051,7 @@
             dma((size + depth,)),
         ],
         compiler_params=pltpu.CompilerParams(
-            collective_id=4, has_side_effects=True, vmem_limit_bytes=62 * 1024 * 1024
+            collective_id=4, has_side_effects=True, vmem_limit_bytes=63 * 1024 * 1024
         ),
         cost_estimate=pl.CostEstimate(
             flops=30 * 1000**3, bytes_accessed=300 * 1000 * 1000, transcendentals=0

time: 430 us -> 423 us (0.984)
  no operation moved by 1% of the time
where the time goes in v6:
time: 423 us; the launch traced here: 418 us
  Pallas kernels  413 us (98%)
    pallas_call x1, Pallas kernels, feed_forward(): pl.pallas_call(functools.partial(ffn_kernel, dims), in_specs=[hbm] * 6 +...  125 us
    pallas_call x1, Pallas kernels, load_all(): pl.pallas_call(functools.partial(load_kernel, dims), in_specs=[hbm] * 4 +...  99.7 us
    pallas_call x1, Pallas kernels, close_layer(): pl.pallas_call(functools.partial(close_kernel, dims), in_specs=[hbm] * 8...  94.4 us
    pallas_call x1, Pallas kernels, attention_layer(): pl.pallas_call(functools.partial(attn_layer_kernel, dims), in_specs=[pl.B...  87.4 us

profile of v6, /device:TPU:15, one launch (start us, length us, event | category | flops | bytes accessed | tf_op | source)
XLA Modules:
  0.0 417.9 jit_solution(5208882465596401239)
XLA Ops:
  0.6 0.0 copy-start
  0.7 0.6 copy-done
  1.3 0.1 broadcast_bitcast_fusion
  1.4 0.7 broadcast_select_fusion
  2.2 0.1 select_n.71
  2.3 0.8 broadcast_select_fusion.2
  3.1 0.1 select_n.76
  3.1 0.1 select_n.69
  3.2 0.1 select_n.73
  3.3 0.1 select_n.67
  3.4 0.2 concatenate.3
  3.6 0.6 pad.4.vec_ref
  4.3 99.7 %shard_map.246 = (bf16[2,8,128,2048]{3,2,1,0:T(8,128)(2,1)}, bf16[2,8,128,2048]{3,2,1,0:T(8,128)(2,1)}, bf16[8,4,64,1024]{3,2,1,0:T(8,128)(2,1)}, bf16[4,256,2048]{2,1,0:T(8,128)(2,1)}, f32[16,2048]{1,0:T(8,128)}) custom-call(bf16[2,128,2048]{2,1,0:T(8,128)(2,1)} %bitcast.29, bf16[2,128,2048]{2,1,0:T(8,128)(2,1)} %bitcast.32, bf16[64,8192]{1,0:T(8,128)(2,1)} %one_ref.1, ...), custom_call_target="tpu_custom_call" | custom-call | flops 1000 | bytes 300000000 | tf_op jit(solution)/shard_map/pallas_call | solution.py:776
  104.0 124.8 %shard_map.247 = (bf16[2048,2048]{1,0:T(8,128)(2,1)}, bf16[2048,2048]{1,0:T(8,128)(2,1)}, bf16[8,4,64,1024]{3,2,1,0:T(8,128)(2,1)}, bf16[4,256,2048]{2,1,0:T(8,1...) custom-call(bf16[2048,2048]{1,0:T(8,128)(2,1)} %bitcast.36, ...), custom_call_target="tpu_custom_call" | custom-call | flops 33999998976 | bytes 300000000 | tf_op jit(solution)/shard_map/pallas_call | solution.py:1125
  228.8 87.4 %shard_map.248 = (bf16[2048,768]{1,0:T(8,128)(2,1)}, bf16[2048,256]{1,0:T(8,128)(2,1)}, bf16[8,4,64,1024]{3,2,1,0:T(8,128)(2,1)}, bf16[8,64,1024]{2,1,0:T(8,128)...) custom-call(s32[2,2]{1,0:T(2,128)} %bitcast.42, ...), custom_call_target="tpu_custom_call" | custom-call | flops 40000000000 | bytes 300000000 | tf_op jit(solution)/shard_map/pallas_call | solution.py:1521
  316.2 0.0 copy-start.1
  316.2 94.4 %shard_map.249 = (bf16[2,128,2048]{2,1,0:T(8,128)(2,1)}, f32[2,128,2048]{2,1,0:T(8,128)}, f32[64,2048]{1,0:T(8,128)}, f32[16,2048]{1,0:T(8,128)}, f32[8,256]{1,0:T(8,128)}, /*index=5*/bf16[8,64,768]{2,1,0:T(8,128)(2,1)}) custom-call(bf16[2,128,2048]{2,1,0:T(8,128)(2,1)} %bitcast.31, bf16[2,128,2048]{2,1,0:T(8,128)(2,1)} %bitcast.33, ...), custom_call_target="tpu_custom_call" | custom-call | flops 30000001024 | bytes 300000000 | tf_op jit(solution)/shard_map/pallas_call | solution.py:2014
  410.6 7.1 %shard_map.250 = (bf16[2,128,2048]{2,1,0:T(8,128)(2,1)}, f32[2,128,2048]{2,1,0:T(8,128)}, f32[1,64]{1,0:T(1,128)}, f32[1,64]{1,0:T(1,128)}, f32[64,6144]{1,0:T(8...) custom-call(s32[1]{0:T(128)} %bitcast.place_ref, ...), custom_call_target="tpu_custom_call" | custom-call | tf_op jit(solution)/shard_map/pallas_call | solution.py:2170
  417.7 0.0 copy-done.1
  (6 shorter events, 0.1 us)
Async XLA Ops:
  0.6 0.7 copy-start
  316.2 101.5 %copy-start.1 = (bf16[256]{0:T(256)(128)(2,1)S(1)}, bf16[256]{0:T(256)(128)(2,1)}, u32[]{:S(2)}) copy-start(bf16[256]{0:T(256)(128)(2,1)} %param.23) | copy-start | bytes 1540
